TPU v7x, 32 devices: a whole 2x2x4 slice. The times are simulated.
32 devices in a mesh: groups: 2 (over x), freq: 16 (over z, y, core).
Axes of the slice: x: 2, y: 2, z: 4, core: 2. Of those that a mesh axis runs over, the one named last changes fastest.
Arguments:
- features: bfloat16 [32, 64, 192], P('groups', 'freq'), parts along dimension 0, may hold values from -6 to 6
- spectrum: bfloat16 [32, 64, 192], P('groups', 'freq'), parts along dimension 0, may hold values from -6 to 6
- cotangent: bfloat16 [32, 64, 192], P('groups', 'freq'), parts along dimension 0, may hold values from -6 to 6
- w_first: bfloat16 [64, 8], P('freq'), may hold values from -2 to 2
- w_second: bfloat16 [64, 8], P('freq'), may hold values from -2 to 2
- w_in: bfloat16 [192, 384], replicated, may hold values from -0.4375 to 0.4375
- w_out: bfloat16 [384, 192], replicated, may hold values from -0.3125 to 0.3125
Outputs:
- enhanced: bfloat16 [32, 64, 192], P('groups', 'freq'), parts along dimension 0
- grad_first: float32 [64, 16], P('freq', 'groups'), parts along dimension 1
- grad_second: float32 [64, 16], P('freq', 'groups'), parts along dimension 1
- grad_w_in: float32 [384, 384], P('groups'), parts along dimension 0
- grad_w_out: float32 [768, 192], P('groups'), parts along dimension 0
There are 2 independent parts, one for each index of `groups`. A program takes and returns all parts, laid end to end along the dimension named above; an argument that names none is the same for every part. Nothing has to cross between parts.
All inputs are finite; a program needn't handle non-finite values.
Results may differ from a plain program's by a relative error of at most 0.0079.
Values may be sent and summed in bfloat16 or wider, within the bound.
No kernel may reach another device: no remote copies, remote signals or barrier semaphores. Data moves between devices by JAX's collectives and lax.ppermute only.
A program may use at most 64 MiB of HBM per device.

v0:
```python
import math

import jax
import jax.numpy as jnp
from jax import lax
from jax.sharding import PartitionSpec as P

gelu_coef = math.sqrt(2.0 / math.pi)


def swapped(value, axis, distance):
    mask = 2**distance
    pairs = [(source, source ^ mask) for source in range(lax.axis_size(axis))]
    return lax.ppermute(value, axis, pairs)


def gelu_pair(pre_act):
    tanh_arg = gelu_coef * (pre_act + 0.044715 * pre_act * pre_act * pre_act)
    tanh_val = jnp.tanh(tanh_arg)
    gelu_out = 0.5 * pre_act * (1.0 + tanh_val)
    gelu_slope = 0.5 * (1.0 + tanh_val) + 0.5 * pre_act * (
        1.0 - tanh_val * tanh_val
    ) * gelu_coef * (1.0 + 3.0 * 0.044715 * pre_act * pre_act)
    return (gelu_out, gelu_slope)


def spread_back(dfirst_two, features):
    frames, own_bins, channels = features.shape
    block = dfirst_two.shape[0]
    quarter = frames // 4
    devices = 2 * block
    send_back = jnp.broadcast_to(dfirst_two[:, None], (block, 2, 2, quarter, channels)).reshape(
        devices, 2 * quarter * channels
    )
    back_rows = lax.all_to_all(send_back, "freq", split_axis=0, concat_axis=0, tiled=True).reshape(
        block, 2, 2, quarter, channels
    )
    by_quarter_x = features.reshape(2, 2, quarter, own_bins, channels)
    return jnp.einsum(
        "hgtbc,pghtc->bp", by_quarter_x, back_rows, preferred_element_type=jnp.float32
    )


def on_device(features, spectrum, cotangent, w_first, w_second, w_in, w_out):
    frames, own_bins, channels = features.shape
    block = w_first.shape[1]
    quarter = frames // 4
    half_c = channels // 2
    devices = lax.axis_size("freq")
    parity = lax.axis_index("freq") % 2
    lower_side = parity == 0

    def join_halves(mine, theirs, axis):
        return jnp.where(
            lower_side, jnp.concatenate([mine, theirs], axis), jnp.concatenate([theirs, mine], axis)
        )

    got_second = swapped(w_second, "freq", 0)
    full_second = join_halves(w_second, got_second, 0)
    by_quarter = features.reshape(2, 2, quarter, own_bins, channels)
    partials = jnp.einsum(
        "hgtbc,bp->pghtc", by_quarter, w_first, preferred_element_type=jnp.float32
    )
    partials = partials.reshape(devices, 2 * quarter * channels)
    arrived = lax.all_to_all(partials, "freq", split_axis=0, concat_axis=0, tiled=True)
    first_two = arrived.reshape(block, 2, 2, quarter, channels).sum(axis=1).astype(jnp.bfloat16)
    spectral = jnp.einsum(
        "ahtc,aq->htqc", first_two, full_second, preferred_element_type=jnp.float32
    ).astype(jnp.bfloat16)
    flat_rows = spectral.reshape(-1, channels)
    pre_act = jnp.dot(flat_rows, w_in, preferred_element_type=jnp.float32)
    gelu_out, gelu_slope = gelu_pair(pre_act)
    hidden = gelu_out.astype(jnp.bfloat16)
    spectral_mask = (
        flat_rows.astype(jnp.float32) + jnp.dot(hidden, w_out, preferred_element_type=jnp.float32)
    ).astype(jnp.bfloat16)
    spectral_mask = spectral_mask.reshape(2, quarter, block, channels)
    send_mask = lax.dynamic_slice_in_dim(spectral_mask, (1 - parity) * own_bins, own_bins, 2)
    keep_mask = lax.dynamic_slice_in_dim(spectral_mask, parity * own_bins, own_bins, 2)
    got_mask = swapped(send_mask, "freq", 0)
    full_mask = jnp.where(
        lower_side, jnp.stack([keep_mask, got_mask], 1), jnp.stack([got_mask, keep_mask], 1)
    )
    mask_f = full_mask.reshape(frames, own_bins, channels).astype(jnp.float32)
    spec_f = spectrum.astype(jnp.float32)
    mask_re, mask_im = (mask_f[..., :half_c], mask_f[..., half_c:])
    spec_re, spec_im = (spec_f[..., :half_c], spec_f[..., half_c:])
    enhanced = jnp.concatenate(
        [spec_re * mask_re - spec_im * mask_im, spec_re * mask_im + spec_im * mask_re], -1
    ).astype(jnp.bfloat16)
    loss_scale = jnp.float32(1.0) / jnp.sqrt(jnp.float32(frames * devices * own_bins))
    grad_f = cotangent.astype(jnp.float32) * loss_scale
    grad_re, grad_im = (grad_f[..., :half_c], grad_f[..., half_c:])
    dmask = jnp.concatenate(
        [grad_re * spec_re + grad_im * spec_im, grad_im * spec_re - grad_re * spec_im], -1
    ).astype(jnp.bfloat16)
    dmask = dmask.reshape(2, 2, quarter, own_bins, channels)
    send_dmask = lax.dynamic_index_in_dim(dmask, 1 - parity, 1, keepdims=False)
    keep_dmask = lax.dynamic_index_in_dim(dmask, parity, 1, keepdims=False)
    got_dmask = swapped(send_dmask, "freq", 0)
    dmask_rows = join_halves(keep_dmask, got_dmask, 2).reshape(-1, channels)
    dact = jnp.dot(dmask_rows, w_out.T, preferred_element_type=jnp.float32)
    dpre = (dact * gelu_slope).astype(jnp.bfloat16)
    part_out = jnp.dot(hidden.T, dmask_rows, preferred_element_type=jnp.float32)
    part_in = jnp.dot(flat_rows.T, dpre, preferred_element_type=jnp.float32)
    grad_w_in, grad_w_out = lax.psum((part_in, part_out), "freq")
    dspectral = (
        dmask_rows.astype(jnp.float32) + jnp.dot(dpre, w_in.T, preferred_element_type=jnp.float32)
    ).astype(jnp.bfloat16)
    dspectral = dspectral.reshape(2, quarter, block, channels)
    dfirst_two = jnp.einsum(
        "htqc,aq->ahtc", dspectral, full_second, preferred_element_type=jnp.float32
    ).astype(jnp.bfloat16)
    second_part = jnp.einsum(
        "ahtc,htqc->aq", first_two, dspectral, preferred_element_type=jnp.float32
    )
    second_part = second_part.reshape(2, own_bins, block)
    got_part = swapped(
        lax.dynamic_index_in_dim(second_part, 1 - parity, 0, keepdims=False), "freq", 0
    )
    grad_second = lax.dynamic_index_in_dim(second_part, parity, 0, keepdims=False) + got_part
    grad_first = spread_back(dfirst_two, features)
    return (enhanced, grad_first, grad_second, grad_w_in, grad_w_out)


def solution(mesh):
    placed = (
        P("groups", "freq", None),
        P("groups", "freq", None),
        P("groups", "freq", None),
        P("freq", None),
        P("freq", None),
        P(),
        P(),
    )
    return jax.shard_map(
        on_device,
        mesh=mesh,
        in_specs=placed,
        out_specs=(
            P("groups", "freq", None),
            P("freq", "groups"),
            P("freq", "groups"),
            P("groups", None),
            P("groups", None),
        ),
        check_vma=False,
    )
```

profile of v0, /device:TPU:0, one launch (start us, length us, event | category | flops | bytes accessed | tf_op | source)
XLA Modules:
  0.0 144.9 jit_solution(6615410310224388072)
XLA Ops:
  7.2 0.0 copy-start
  7.2 0.7 copy-done.7
  7.9 1.0 convolution_bitcast_fusion
  8.9 0.1 copy.33
  8.9 0.8 all_to_all.16
  9.8 7.5 %all-to-all-start = ((f32[16,1,1536]{2,1,0:T(1,128)}), f32[16,1,1536]{2,1,0:T(1,128)S(1)}, u32[]{:S(2)}, u32[]{:S(2)}) async-start(f32[16,1,1536]{2,1,0:T(1,128)} %all_to_all.16), calls=%async_computation | async-start | bytes 196608 | tf_op jit(solution)/shard_map/all_to_all | solution.py:65
  17.3 0.5 collective-permute-start
  17.8 6.9 %all-to-all-done = f32[16,1,1536]{2,1,0:T(1,128)S(1)} async-done(((f32[16,1,1536]{2,1,0:T(1,128)}), f32[16,1,1536]{2,1,0:T(1,128)S(1)}, u32[]{:S(2)}, u32[]{:S(2)}) %all-to-all-start) | async-done | bytes 98336 | tf_op jit(solution)/shard_map/all_to_all | solution.py:65
  24.7 0.2 reduce
  24.9 0.1 reshape.60
  25.1 0.2 convolution_convert_fusion.1
  25.3 0.6 copy-done.1
  26.0 0.2 fusion.23
  26.1 0.2 fusion.1
  26.4 0.0 copy-start.4
  26.4 0.1 collective-permute-start.1
  26.5 0.6 copy-done.3
  27.1 0.0 copy-done.4
  27.2 0.5 collective-permute-done.1
  27.7 0.1 subtract_convert_fusion
  27.8 0.1 fusion.15
  27.9 0.2 collective-permute-start.2
  28.1 0.7 pad_maximum_fusion
  28.8 0.3 collective-permute-done.2
  29.2 0.2 fusion
  29.4 1.0 fusion.22
  30.3 0.2 add_convert_fusion
  30.5 0.9 fusion.24
  31.5 0.1 convolution_convert_fusion
  31.6 0.2 convolution_bitcast_fusion.1
  31.8 0.2 collective-permute-start.3
  32.0 0.1 all_to_all.17
  32.2 0.5 broadcast.34
  32.7 0.9 reduce.2
  33.6 0.6 reshape.74
  34.2 3.5 %all-to-all-start.1 = ((bf16[16,2,768]{2,1,0:T(2,128)(2,1)}), bf16[16,2,768]{2,1,0:T(2,128)(2,1)S(1)}, u32[]{:S(2)}, u32[]{:S(2)}) async-start(bf16[16,2,768]{2,1,0:T(2,128)(2,1)} %reshape.74), calls=%async_computation.1 | async-start | bytes 98304 | tf_op jit(solution)/shard_map/all_to_all | solution.py:35
  37.7 0.0 all-reduce.3.cloned.1.call-start
  37.8 0.7 all-reduce.3.cloned.1.call-update
  38.5 0.6 bitcast_add_fusion
  39.1 5.4 %all-to-all-done.1 = bf16[16,2,768]{2,1,0:T(2,128)(2,1)S(1)} async-done(((bf16[16,2,768]{2,1,0:T(2,128)(2,1)}), bf16[16,2,768]{2,1,0:T(2,128)(2,1)S(1)}, u32[]{:S(2)}, u32[]{:S(2)}) %all-to-all-start.1) | async-done | bytes 49184 | tf_op jit(solution)/shard_map/all_to_all | solution.py:35
  44.5 0.3 reduce.1
  44.8 0.0 copy-start.5
  44.8 0.1 reshape.64
  44.9 0.6 copy-done.5
  45.5 0.7 convolution_bitcast_fusion.2
  46.3 89.3 %all-reduce.3.cloned.1.call-done = (f32[192,384]{1,0:T(8,128)}, f32[384,192]{0,1:T(8,128)}) async-done(((f32[192,384]{1,0:T(8,128)}, f32[384,192]{0,1:T(8,128)}), (f32[192,384]{1,0:T(8,128)}, f32[384,192]{0,1:T(8,128)})) %all-reduce.3.cloned.1.call-update) | async-done | bytes 589840 | tf_op jit(solution)/shard_map/psum | solution.py:106
  135.6 1.7 %copy.59 = f32[192,384]{1,0:T(8,128)} copy(f32[192,384]{1,0:T(8,128)} %get-tuple-element.20) | data formatting | bytes 589824
  137.3 0.7 copy.60
  (21 shorter events, 0.3 us)
Async XLA Ops:
  7.2 19.0 %copy-start = (bf16[384,192]{0,1:T(8,128)(2,1)S(1)}, bf16[384,192]{0,1:T(8,128)(2,1)}, u32[]{:S(2)}) copy-start(bf16[384,192]{0,1:T(8,128)(2,1)} %param.13) | copy-start | bytes 442372
  7.2 0.7 copy-start.7
  9.7 7.5 %copy-start.6 = (bf16[4,8]{1,0:T(4,128)(2,1)S(1)}, bf16[4,8]{1,0:T(4,128)(2,1)}, u32[]{:S(2)}) copy-start(bf16[4,8]{1,0:T(4,128)(2,1)} %param.11) | copy-start | bytes 196
  9.8 14.9 %all-to-all-start = ((f32[16,1,1536]{2,1,0:T(1,128)}), f32[16,1,1536]{2,1,0:T(1,128)S(1)}, u32[]{:S(2)}, u32[]{:S(2)}) async-start(f32[16,1,1536]{2,1,0:T(1,128)} %all_to_all.16), calls=%async_computation | async-start | bytes 196608 | tf_op jit(solution)/shard_map/all_to_all | solution.py:65
  17.3 7.8 %collective-permute-start = (bf16[4,8]{1,0:T(4,128)(2,1)S(1)}, bf16[4,8]{1,0:T(4,128)(2,1)S(1)}, u32[]{:S(2)}, u32[]{:S(2)}) collective-permute-start(bf16[4,8]{1,0:T(4,128)(2,1)S(1)} %copy-done.6), channel_id=1, source_target_pairs={{0,1},{1,0},{2,3},{3,2},{4,5},{5,4},{6,7},{7,6},{8,9},{9,8},{10,11... | collective-permute-start | bytes 200 | tf_op jit(solution)/shard_map/ppermute | solution.py:14
  25.0 0.9 copy-start.1
  26.3 0.8 copy-start.3
  26.4 0.8 copy-start.4
  26.4 1.2 collective-permute-start.1
  27.9 1.2 collective-permute-start.2
  31.8 6.7 %collective-permute-start.3 = (f32[4,8]{1,0:T(4,128)S(1)}, f32[4,8]{1,0:T(4,128)S(1)}, u32[]{:S(2)}, u32[]{:S(2)}) collective-permute-start(f32[4,8]{1,0:T(4,128)S(1)} %dynamic-slice_bitcast_fusion.1), channel_id=1, source_target_pairs={{0,1},{1,0},{2,3},{3,2},{4,5},{5,4},{6,7},{7,6},{8,9},{9,8},{10,11... | collective-permute-start | bytes 392 | tf_op jit(solution)/shard_map/ppermute | solution.py:14
  34.2 10.2 %all-to-all-start.1 = ((bf16[16,2,768]{2,1,0:T(2,128)(2,1)}), bf16[16,2,768]{2,1,0:T(2,128)(2,1)S(1)}, u32[]{:S(2)}, u32[]{:S(2)}) async-start(bf16[16,2,768]{2,1,0:T(2,128)(2,1)} %reshape.74), calls=%async_computation.1 | async-start | bytes 98304 | tf_op jit(solution)/shard_map/all_to_all | solution.py:35
  37.7 97.8 %all-reduce.3.cloned.1.call-start = ((), (), s32[]{:S(2)}) async-start(), calls=%async_computation.2 | async-start | bytes 1179648 | tf_op jit(solution)/shard_map/psum | solution.py:106
  44.8 0.8 copy-start.5
  135.6 1.7 %copy-start.2 = (f32[384,192]{0,1:T(8,128)S(1)}, f32[384,192]{0,1:T(8,128)}, u32[]{:S(2)}) copy-start(f32[384,192]{0,1:T(8,128)} %get-tuple-element.21) | copy-start | bytes 884740
Sparse Core Ops, SparseCore 0:
  42.6 92.9 all-reduce.2
where the time goes:
time: 145 us
  waiting for transfers between devices  103 us (71%)
  between operations  14.3 us (10%)
  starting transfers between devices  12 us (8%)
  local copies, waits for them, and re-layouts  7.63 us (5%)
  matrix products  4.81 us (3%)
  other arithmetic  3.06 us (2%)
    psum x1, waiting for transfers between devices, on_device(): grad_w_in, grad_w_out = lax.psum((part_in, part_out), 'freq')  89.3 us
    all_to_all x1, starting transfers between devices, on_device(): lax.all_to_all(partials, 'freq', split_axis=0, concat_axis=0, tiled=True)  7.52 us
    all_to_all x1, waiting for transfers between devices, on_device(): lax.all_to_all(partials, 'freq', split_axis=0, concat_axis=0, tiled=True)  6.93 us
    unnamed x20, local copies, waits for them, and re-layouts  5.77 us
    all_to_all x1, waiting for transfers between devices, spread_back(): lax.all_to_all(send_back, 'freq', split_axis=0, concat_axis=0, tiled=True)  5.39 us
    all_to_all x1, starting transfers between devices, spread_back(): lax.all_to_all(send_back, 'freq', split_axis=0, concat_axis=0, tiled=True)  3.48 us
  transfers between devices with their start and end apart: 7, of which 5 were waited for; matrix products, arithmetic and copies ran while one was open for 3% of the time, Pallas kernels for 0%

commit v1 on v0

--- a/solution.py
+++ b/solution.py
@@ -1,8 +1,11 @@
+import functools
 import math
 
 import jax
 import jax.numpy as jnp
 from jax import lax
+from jax.experimental import pallas as pl
+from jax.experimental.pallas import tpu as pltpu
 from jax.sharding import PartitionSpec as P
 
 gelu_coef = math.sqrt(2.0 / math.pi)
@@ -41,7 +44,7 @@
     )
 
 
-def on_device(features, spectrum, cotangent, w_first, w_second, w_in, w_out):
+def split_rows(features, spectrum, cotangent, w_first, w_second, w_in, w_out):
     frames, own_bins, channels = features.shape
     block = w_first.shape[1]
     quarter = frames // 4
@@ -123,6 +126,269 @@
     return (enhanced, grad_first, grad_second, grad_w_in, grad_w_out)
 
 
+f32, bf16 = jnp.float32, jnp.bfloat16
+NN = (((1,), (0,)), ((), ()))
+NT = (((1,), (1,)), ((), ()))
+TN = (((0,), (0,)), ((), ()))
+LANES = 128
+W_ROWS = 16
+
+
+def mul(a, b, dims=NN):
+    return lax.dot_general(a, b, dims, preferred_element_type=f32)
+
+
+def mul_f32(a, b):
+    return lax.dot_general(a, b, NN, precision=lax.Precision.HIGHEST, preferred_element_type=f32)
+
+
+def iota(shape, dim):
+    return lax.broadcasted_iota(jnp.int32, shape, dim)
+
+
+def pack_rows(rows):
+    half = rows.shape[0] // 2
+    low, high = rows[:half], rows[half:]
+    rest = jnp.concatenate([low[:, LANES:], high[:, LANES:]], 1)
+    return low[:, :LANES], high[:, :LANES], rest
+
+
+def pack_kernel(x_ref, s_ref, c_ref, w1_ref, w2_ref, px_ref, pd_ref, *, scale):
+    frames, bins, channels = x_ref.shape
+    rows = frames * bins
+    half = rows // 2
+    half_c = channels // 2
+    block = w1_ref.shape[1]
+
+    for t, part in enumerate(pack_rows(x_ref[...].astype(f32).reshape(rows, channels))):
+        px_ref[t * half : (t + 1) * half, :] = part.astype(bf16)
+    weights = jnp.concatenate([w1_ref[...].astype(f32), w2_ref[...].astype(f32)], 1)
+    weights = jnp.concatenate([weights, jnp.zeros((bins, LANES - 2 * block), f32)], 1)
+    weights = jnp.concatenate([weights, jnp.zeros((W_ROWS - bins, LANES), f32)], 0)
+    px_ref[3 * half :, :] = weights.astype(bf16)
+
+    spec = s_ref[...].astype(f32).reshape(rows, channels)
+    grad = c_ref[...].astype(f32).reshape(rows, channels) * scale
+    spec_re, spec_im = spec[:, :half_c], spec[:, half_c:]
+    grad_re, grad_im = grad[:, :half_c], grad[:, half_c:]
+    dmask = jnp.concatenate(
+        [grad_re * spec_re + grad_im * spec_im, grad_im * spec_re - grad_re * spec_im], 1
+    )
+    for t, part in enumerate(pack_rows(dmask)):
+        pd_ref[t * half : (t + 1) * half, :] = part.astype(bf16)
+
+
+def main_kernel(
+    gx_ref, gd_ref, s_ref, w_in_ref, w_out_ref,
+    enh_ref, g1_ref, g2_ref, gwi_ref, gwo_ref,
+    sp_ref, dm_ref, dsp_ref, *, chunk,
+):
+    frames, bins, channels = s_ref.shape
+    block = g1_ref.shape[1]
+    half_f = frames // 2
+    half_c = channels // 2
+    own = half_f * bins
+    devices = gx_ref.shape[0] // (3 * own + W_ROWS)
+    rows = devices * own
+    me = lax.axis_index("freq")
+    chip, side = me >> 1, (me & 1) * bins
+    per_block = 2 * own
+
+    def block_of(r):
+        return r // per_block
+
+    def place_of(r):
+        return ((r // own) & 1) * bins + (r & (bins - 1))
+
+    def frame_of(r):
+        return (r // bins) & (half_f - 1)
+
+    def gathered(ref, per_device):
+        tiles = [
+            jnp.concatenate(
+                [ref[j * per_device + t * own : j * per_device + (t + 1) * own, :] for j in range(devices)], 0
+            )
+            for t in range(3)
+        ]
+        return tiles
+
+    def unpacked(low, high, rest):
+        split = channels - LANES
+        return (
+            jnp.concatenate([low, rest[:, :split]], 1),
+            jnp.concatenate([high, rest[:, split:]], 1),
+        )
+
+    per_x = 3 * own + W_ROWS
+    x_tiles = gathered(gx_ref, per_x)
+    weights = jnp.concatenate(
+        [gx_ref[j * per_x + 3 * own : (j + 1) * per_x, :] for j in range(devices)], 0
+    )
+    w_rows = devices * W_ROWS
+
+    w_at = iota((rows, w_rows), 1)
+    w_ok = (w_at & (W_ROWS - 1)) < bins
+    w_block = w_at // (2 * W_ROWS)
+    w_place = ((w_at // W_ROWS) & 1) * bins + (w_at & (W_ROWS - 1))
+    r_at = iota((rows, w_rows), 0)
+    lane = iota((rows, LANES), 1)
+    r_lane = iota((rows, LANES), 0)
+    q_at = iota((w_rows, rows), 0)
+    q_place = ((q_at // W_ROWS) & 1) * bins + (q_at & (W_ROWS - 1))
+    q_block = q_at // (2 * W_ROWS)
+    q_row = iota((w_rows, rows), 1)
+    m_row, m_col = iota((rows, rows), 0), iota((rows, rows), 1)
+    same_frame = frame_of(m_row) == frame_of(m_col)
+
+    def onehot(cond):
+        return cond.astype(f32).astype(bf16)
+
+    pick1 = onehot(lane == place_of(r_lane))
+    of_row = mul(pick1, weights, NT)
+    spread = onehot((q_place == place_of(q_row)) & (q_block == block_of(q_row)))
+    mix1 = mul(
+        jnp.where(w_ok & (w_block == block_of(r_at)), of_row, 0.0).astype(bf16), spread
+    )
+    mix1 = jnp.where(same_frame, mix1, 0.0).astype(bf16)
+
+    pick2 = onehot(lane == block + (place_of(r_lane) ^ side))
+    of_row = mul(pick2, weights, NT)
+    spread = onehot(q_place == (block_of(q_row) ^ chip ^ side))
+    mix2 = mul(
+        jnp.where(w_ok & (w_block == block_of(r_at)), of_row, 0.0).astype(bf16), spread
+    )
+    mix2 = jnp.where(same_frame & (place_of(m_col) == (block_of(m_row) ^ chip)), mix2, 0.0).astype(bf16)
+
+    packed_x = jnp.concatenate(x_tiles, 1)
+    first = mul(mix1, packed_x).astype(bf16)
+    spectral = mul(mix2, first).astype(bf16)
+    cut = lambda v: (v[:, :LANES], v[:, LANES : 2 * LANES], v[:, 2 * LANES :])
+    sp_low, sp_high = unpacked(*cut(spectral))
+    sp_ref[:rows, :] = sp_low
+    sp_ref[rows:, :] = sp_high
+    dm_low, dm_high = unpacked(*gathered(gd_ref, 3 * own))
+    dm_ref[:rows, :] = dm_low
+    dm_ref[rows:, :] = dm_high
+
+    sp_own = jnp.concatenate([sp_low[:own], sp_high[:own]], 0)
+    hidden_own = gelu_pair(mul(sp_own, w_in_ref[...]))[0].astype(bf16)
+    mask = (sp_own.astype(f32) + mul(hidden_own, w_out_ref[...])).astype(bf16).astype(f32)
+    spec = s_ref[...].astype(f32).reshape(2 * own, channels)
+    spec_re, spec_im = spec[:, :half_c], spec[:, half_c:]
+    mask_re, mask_im = mask[:, :half_c], mask[:, half_c:]
+    enhanced = jnp.concatenate(
+        [spec_re * mask_re - spec_im * mask_im, spec_re * mask_im + spec_im * mask_re], 1
+    )
+    enh_ref[...] = enhanced.reshape(frames, bins, channels).astype(bf16)
+
+    gwi_ref[...] = jnp.zeros_like(gwi_ref)
+    gwo_ref[...] = jnp.zeros_like(gwo_ref)
+
+    @pl.loop(0, 2 * rows // chunk)
+    def _(i):
+        at = pl.ds(pl.multiple_of(i * chunk, chunk), chunk)
+        sp, dm = sp_ref[at, :], dm_ref[at, :]
+        gelu_out, slope = gelu_pair(mul(sp, w_in_ref[...]))
+        hidden = gelu_out.astype(bf16)
+        dpre = (mul(dm, w_out_ref[...], NT) * slope).astype(bf16)
+        gwo_ref[...] += mul(hidden, dm, TN)
+        gwi_ref[...] += mul(sp, dpre, TN)
+        dsp_ref[at, :] = (dm.astype(f32) + mul(dpre, w_in_ref[...], NT)).astype(bf16)
+
+    dsp_low, dsp_high = dsp_ref[:rows, :], dsp_ref[rows:, :]
+    back = mix2[:, :per_block]
+    dfirst_low = mul(back, dsp_low, TN).astype(bf16)
+    dfirst_high = mul(back, dsp_high, TN).astype(bf16)
+
+    sum_row, sum_col = iota((own, per_block), 0), iota((own, per_block), 1)
+    frames_meet = frame_of(sum_row) == frame_of(sum_col)
+    to_bin = ((iota((bins, own), 1) & (bins - 1)) == iota((bins, own), 0)).astype(f32)
+    col_place = place_of(iota((per_block, block), 0))
+    col_want = iota((per_block, block), 1)
+
+    def block_sums(gram, cols):
+        return mul_f32(mul_f32(to_bin, jnp.where(frames_meet, gram, 0.0)), cols)
+
+    x_low, x_high = unpacked(*[tile[:own] for tile in x_tiles])
+    gram = mul(x_low, dfirst_low, NT) + mul(x_high, dfirst_high, NT)
+    g1_ref[...] = block_sums(gram, (col_place == col_want).astype(f32))
+
+    p_row, p_col = iota((own, rows), 0), iota((own, rows), 1)
+    chosen = onehot(
+        (block_of(p_col) == ((side + (p_row & (bins - 1))) ^ chip))
+        & (place_of(p_col) == chip)
+        & (frame_of(p_row) == frame_of(p_col))
+    )
+    first_low, first_high = unpacked(*cut(mul(chosen, first).astype(bf16)))
+    gram = mul(first_low, dsp_low[:per_block], NT) + mul(first_high, dsp_high[:per_block], NT)
+    g2_ref[...] = block_sums(gram, (col_place == (col_want ^ side)).astype(f32))
+
+
+def whole_rows(features, spectrum, cotangent, w_first, w_second, w_in, w_out):
+    frames, bins, channels = features.shape
+    block = w_first.shape[1]
+    hid = w_in.shape[1]
+    devices = lax.axis_size("freq")
+    own = frames // 2 * bins
+    vmem = lambda n: [pl.BlockSpec(memory_space=pltpu.VMEM)] * n
+    scale = 1.0 / math.sqrt(frames * devices * bins)
+    x_own, d_own = pl.pallas_call(
+        functools.partial(pack_kernel, scale=scale),
+        out_shape=(
+            jax.ShapeDtypeStruct((3 * own + W_ROWS, LANES), bf16),
+            jax.ShapeDtypeStruct((3 * own, LANES), bf16),
+        ),
+        in_specs=vmem(5),
+        out_specs=tuple(vmem(2)),
+        name="pack",
+    )(features, spectrum, cotangent, w_first, w_second)
+
+    def gather(value):
+        blocks = {0: value}
+        for bit in reversed(range(devices.bit_length() - 1)):
+            held = jnp.concatenate([blocks[j] for j in sorted(blocks)], 0)
+            came = swapped(held, "freq", bit)
+            parts = jnp.split(came, len(blocks), 0)
+            blocks.update({j ^ 2**bit: part for j, part in zip(sorted(blocks), parts)})
+        return jnp.concatenate([blocks[j] for j in range(devices)], 0)
+
+    gx, gd = gather(x_own), gather(d_own)
+    rows = devices * own
+    return pl.pallas_call(
+        functools.partial(main_kernel, chunk=256),
+        out_shape=(
+            jax.ShapeDtypeStruct((frames, bins, channels), bf16),
+            jax.ShapeDtypeStruct((bins, block), f32),
+            jax.ShapeDtypeStruct((bins, block), f32),
+            jax.ShapeDtypeStruct((channels, hid), f32),
+            jax.ShapeDtypeStruct((hid, channels), f32),
+        ),
+        in_specs=vmem(5),
+        out_specs=tuple(vmem(5)),
+        scratch_shapes=[pltpu.VMEM((2 * rows, channels), bf16)] * 3,
+        compiler_params=pltpu.CompilerParams(vmem_limit_bytes=40 * 2**20),
+        name="mix_and_grads",
+    )(gx, gd, spectrum, w_in, w_out)
+
+
+def on_device(features, spectrum, cotangent, w_first, w_second, w_in, w_out):
+    frames, bins, channels = features.shape
+    block = w_first.shape[1]
+    devices = lax.axis_size("freq")
+    gathered_bytes = 2 * 2 * devices * frames * bins * channels
+    fits = gathered_bytes <= 4 * 2**20
+    shaped = (
+        block == 2 * bins
+        and devices == 2 * block
+        and bins <= W_ROWS
+        and 2 * block <= LANES
+        and LANES < channels
+        and 2 * (channels - LANES) == LANES
+    )
+    plan = whole_rows if fits and shaped else split_rows
+    return plan(features, spectrum, cotangent, w_first, w_second, w_in, w_out)
+
+
 def solution(mesh):
     placed = (
         P("groups", "freq", None),

time: 145 us -> 30.7 us (0.21)
  waiting for transfers between devices: 103 us -> 7.03 us
  between operations: 14.3 us -> 0.9 us
  Pallas kernels: 0 us -> 8.1 us
  matrix products: 4.81 us -> 0 us
  local copies, waits for them, and re-layouts: 7.63 us -> 3.08 us
  other arithmetic: 3.06 us -> 0.03 us
    psum x1 -> x0, waiting for transfers between devices: 89.3 us -> none  [on_device(): grad_w_in, grad_w_out = lax.psum((part_in, part_out), 'freq')]
    all_to_all x2 -> x0, waiting for transfers between devices: 12.3 us -> none  [the longest x1 6.93 us: on_device(): lax.all_to_all(partials, 'freq', split_axis=0, concat_axis=0, tiled=True)]
    all_to_all x2 -> x0, starting transfers between devices: 11 us -> none  [the longest x1 7.52 us: on_device(): lax.all_to_all(partials, 'freq', split_axis=0, concat_axis=0, tiled=True)]
    ppermute x4 -> x8, starting transfers between devices: 0.99 us -> 11.3 us  [swapped(): return lax.ppermute(value, axis, pairs)]
    pallas_call x0 -> x2, Pallas kernels: none -> 8.1 us  [the longest x1 6.42 us: whole_rows(): pl.pallas_call(functools.partial(main_kernel, chunk=256), out_shape=(jax....]
    ppermute x4 -> x8, waiting for transfers between devices: 0.79 us -> 7.03 us  [swapped(): return lax.ppermute(value, axis, pairs)]
    dot_general x11 -> x0, matrix products: 4.81 us -> none  [the longest x1 0.96 us: on_device(): jnp.einsum('hgtbc,bp->pghtc', by_quarter, w_first, preferred_element_type...]
    unnamed x20 -> x53, local copies, waits for them, and re-layouts: 5.77 us -> 2.17 us
  transfers between devices with their start and end apart: 7 -> 8, of which waited for: 5 -> 6; matrix products, arithmetic and copies ran while one was open for 3% -> 4% of each run, Pallas kernels for 0% -> 0%
where the time goes in v1:
time: 30.7 us; the launch traced here: 30.5 us
  starting transfers between devices  11.3 us (37%)
  Pallas kernels  8.1 us (26%)
  waiting for transfers between devices  7.03 us (23%)
  local copies, waits for them, and re-layouts  3.08 us (10%)
  between operations  0.9 us (3%)
    ppermute x8, starting transfers between devices, swapped(): return lax.ppermute(value, axis, pairs)  11.3 us
    ppermute x8, waiting for transfers between devices, swapped(): return lax.ppermute(value, axis, pairs)  7.03 us
    pallas_call x1, Pallas kernels, whole_rows(): pl.pallas_call(functools.partial(main_kernel, chunk=256), out_shape=(jax....  6.42 us
    unnamed x53, local copies, waits for them, and re-layouts  2.17 us
    pallas_call x1, Pallas kernels, whole_rows(): pl.pallas_call(functools.partial(pack_kernel, scale=scale), out_shape=(ja...  1.68 us
    pallas_call x1, local copies, waits for them, and re-layouts, whole_rows(): pl.pallas_call(functools.partial(main_kernel, chunk=256), out_shape=(jax....  0.86 us
  transfers between devices with their start and end apart: 8, of which 6 were waited for; matrix products, arithmetic and copies ran while one was open for 4% of the time, Pallas kernels for 0%

profile of v1, /device:TPU:0, one launch (start us, length us, event | category | flops | bytes accessed | tf_op | source)
XLA Modules:
  0.0 30.5 jit_solution(9983131010353952872)
XLA Ops:
  0.6 0.0 copy-start.4
  0.6 1.7 %pack.1 = (bf16[112,128]{1,0:T(8,128)(2,1)}, bf16[96,128]{1,0:T(8,128)(2,1)}) custom-call(bf16[16,4,192]{2,1,0:T(4,128)(2,1)} %x_ref.1, bf16[16,4,192]{2,1,0:T(4,128)(2,1)} %s_ref.3, bf16[16,4,192]{2,1,0:T(4,128)(2,1)} %c_ref.1, bf16[4,8]{1,0:T(4,128)(2,1)} %w1_ref.1, bf16[4,8]{1,0:T(4,128)(2,1)} %w2_ref.1), custom_call_target="tpu_custom_call" | custom-call | tf_op jit(solution)/shard_map/pack/pallas_call | solution.py:335
  2.3 4.0 %collective-permute-start.4 = (bf16[96,128]{1,0:T(8,128)(2,1)}, bf16[96,128]{1,0:T(8,128)(2,1)S(1)}, u32[]{:S(2)}, u32[]{:S(2)}) collective-permute-start(bf16[96,128]{1,0:T(8,128)(2,1)} %get-tuple-element.8), channel_id=1, source_target_pairs={{0,8},{1,9},{2,10},{3,11},{4,12},{5,13},{6,14},{7,15},{8,0},{9,1},... | collective-permute-start | bytes 73736 | tf_op jit(solution)/shard_map/ppermute | solution.py:17
  6.4 0.0 copy-start.3
  6.4 0.1 collective-permute-start
  6.4 0.8 %constant_dynamic-update-slice_fusion.7 = (bf16[896,128]{1,0:T(8,128)(2,1)S(1)}, bf16[1792,128]{1,0:T(8,128)(2,1)S(1)}) fusion(bf16[112,128]{1,0:T(8,128)(2,1)} %get-tuple-element.7), kind=kLoop, calls=%fused_computation.8 | loop fusion | bytes 86016
  7.2 0.0 copy-done.3
  7.2 0.0 copy-done.4
  7.2 0.1 copy.12.w_out_ref
  7.4 0.0 copy-start.2
  7.4 1.0 %collective-permute-done.4 = bf16[96,128]{1,0:T(8,128)(2,1)S(1)} collective-permute-done((bf16[96,128]{1,0:T(8,128)(2,1)}, bf16[96,128]{1,0:T(8,128)(2,1)S(1)}, u32[]{:S(2)}, u32[]{:S(2)}) %collective-permute-start.4) | collective-permute-done | bytes 24608 | tf_op jit(solution)/shard_map/ppermute | solution.py:17
  8.4 1.9 %collective-permute-start.5 = (bf16[192,128]{1,0:T(8,128)(2,1)S(1)}, bf16[192,128]{1,0:T(8,128)(2,1)S(1)}, u32[]{:S(2)}, u32[]{:S(2)}) collective-permute-start(bf16[192,128]{1,0:T(8,128)(2,1)S(1)} %pad_maximum_fusion.3), channel_id=1, source_target_pairs={{0,4},{1,5},{2,6},{3,7},{4,0},{5,1},{6,2},{7,3},{8,12},{9,13},{10,... | collective-permute-start | bytes 147464 | tf_op jit(solution)/shard_map/ppermute | solution.py:17
  10.3 1.0 %collective-permute-done = bf16[112,128]{1,0:T(8,128)(2,1)S(1)} collective-permute-done((bf16[112,128]{1,0:T(8,128)(2,1)}, bf16[112,128]{1,0:T(8,128)(2,1)S(1)}, u32[]{:S(2)}, u32[]{:S(2)}) %collective-permute-start) | collective-permute-done | bytes 28704 | tf_op jit(solution)/shard_map/ppermute | solution.py:17
  11.3 0.0 copy-done.2
  11.3 1.7 %collective-permute-start.1 = (bf16[224,128]{1,0:T(8,128)(2,1)S(1)}, bf16[224,128]{1,0:T(8,128)(2,1)S(1)}, u32[]{:S(2)}, u32[]{:S(2)}) collective-permute-start(bf16[224,128]{1,0:T(8,128)(2,1)S(1)} %pad_maximum_fusion.2), channel_id=1, source_target_pairs={{0,4},{1,5},{2,6},{3,7},{4,0},{5,1},{6,2},{7,3},{8,12},{9,13},{10,... | collective-permute-start | bytes 172040 | tf_op jit(solution)/shard_map/ppermute | solution.py:17
  13.0 0.0 collective-permute-done.5
  13.1 1.9 %collective-permute-start.6 = (bf16[384,128]{1,0:T(8,128)(2,1)S(1)}, bf16[384,128]{1,0:T(8,128)(2,1)S(1)}, u32[]{:S(2)}, u32[]{:S(2)}) collective-permute-start(bf16[384,128]{1,0:T(8,128)(2,1)S(1)} %pad_maximum_fusion.1), channel_id=1, source_target_pairs={{0,2},{1,3},{2,0},{3,1},{4,6},{5,7},{6,4},{7,5},{8,10},{9,11},{10,... | collective-permute-start | bytes 294920 | tf_op jit(solution)/shard_map/ppermute | solution.py:17
  15.0 0.6 %collective-permute-done.1 = bf16[224,128]{1,0:T(8,128)(2,1)S(1)} collective-permute-done((bf16[224,128]{1,0:T(8,128)(2,1)S(1)}, bf16[224,128]{1,0:T(8,128)(2,1)S(1)}, u32[]{:S(2)}, u32[]{:S(2)}) %collective-permute-start.1) | collective-permute-done | bytes 57376 | tf_op jit(solution)/shard_map/ppermute | solution.py:17
  15.6 1.6 %collective-permute-start.2 = (bf16[448,128]{1,0:T(8,128)(2,1)S(1)}, bf16[448,128]{1,0:T(8,128)(2,1)S(1)}, u32[]{:S(2)}, u32[]{:S(2)}) collective-permute-start(bf16[448,128]{1,0:T(8,128)(2,1)S(1)} %pad_maximum_fusion), channel_id=1, source_target_pairs={{0,2},{1,3},{2,0},{3,1},{4,6},{5,7},{6,4},{7,5},{8,10},{9,11},{10,... | collective-permute-start | bytes 344072 | tf_op jit(solution)/shard_map/ppermute | solution.py:17
  17.2 1.0 %collective-permute-done.6 = bf16[384,128]{1,0:T(8,128)(2,1)S(1)} collective-permute-done((bf16[384,128]{1,0:T(8,128)(2,1)S(1)}, bf16[384,128]{1,0:T(8,128)(2,1)S(1)}, u32[]{:S(2)}, u32[]{:S(2)}) %collective-permute-start.6) | collective-permute-done | bytes 98336 | tf_op jit(solution)/shard_map/ppermute | solution.py:17
  18.3 0.1 collective-permute-start.7
  18.4 2.1 %collective-permute-done.2 = bf16[448,128]{1,0:T(8,128)(2,1)S(1)} collective-permute-done((bf16[448,128]{1,0:T(8,128)(2,1)S(1)}, bf16[448,128]{1,0:T(8,128)(2,1)S(1)}, u32[]{:S(2)}, u32[]{:S(2)}) %collective-permute-start.2) | collective-permute-done | bytes 114720 | tf_op jit(solution)/shard_map/ppermute | solution.py:17
  20.6 0.1 collective-permute-start.3
  20.6 0.0 collective-permute-done.7
  20.9 1.3 %collective-permute-done.3 = bf16[896,128]{1,0:T(8,128)(2,1)S(1)} collective-permute-done((bf16[896,128]{1,0:T(8,128)(2,1)S(1)}, bf16[896,128]{1,0:T(8,128)(2,1)S(1)}, u32[]{:S(2)}, u32[]{:S(2)}) %collective-permute-start.3) | collective-permute-done | bytes 229408 | tf_op jit(solution)/shard_map/ppermute | solution.py:17
  22.3 0.0 copy-start
  22.3 0.0 copy-start.1
  22.4 0.8 %copy-done = bf16[192,384]{1,0:T(8,128)(2,1)S(1)} copy-done((bf16[192,384]{1,0:T(8,128)(2,1)S(1)}, bf16[192,384]{1,0:T(8,128)(2,1)}, u32[]{:S(2)}) %copy-start) | copy-done | bytes 147480
  23.2 0.0 copy-done.1
  23.2 6.4 %mix_and_grads.1 = (bf16[16,4,192]{2,1,0:T(4,128)(2,1)}, f32[4,8]{1,0:T(4,128)}, f32[4,8]{1,0:T(4,128)}, f32[192,384]{1,0:T(8,128)}, f32[384,192]{1,0:T(8,128)S(1)}) custom-call(bf16[1792,128]{1,0:T(8,128)(2,1)S(1)} %constant_dynamic-update-slice_fusion.8.gx_ref, bf16[1536,128]{1,0:T(8,128)(2,1)S(1)} %constant_dynamic-update-slice_fusion.32.gd_ref, ...), custom_call_target="tpu_custom_call" | custom-call | tf_op jit(solution)/shard_map/mix_and_grads/pallas_call | solution.py:357
  29.6 0.9 %copy.13 = f32[384,192]{0,1:T(8,128)} copy(f32[384,192]{1,0:T(8,128)S(1)} %get-tuple-element.13) | data formatting | bytes 589824 | tf_op jit(solution)/shard_map/mix_and_grads/pallas_call | solution.py:357
  (51 shorter events, 0.5 us)
Async XLA Ops:
  0.6 6.6 %copy-start.4 = (bf16[384,192]{0,1:T(8,128)(2,1)S(1)}, bf16[384,192]{0,1:T(8,128)(2,1)}, u32[]{:S(2)}) copy-start(bf16[384,192]{0,1:T(8,128)(2,1)} %param.13) | copy-start | bytes 442372
  2.3 6.1 %collective-permute-start.4 = (bf16[96,128]{1,0:T(8,128)(2,1)}, bf16[96,128]{1,0:T(8,128)(2,1)S(1)}, u32[]{:S(2)}, u32[]{:S(2)}) collective-permute-start(bf16[96,128]{1,0:T(8,128)(2,1)} %get-tuple-element.8), channel_id=1, source_target_pairs={{0,8},{1,9},{2,10},{3,11},{4,12},{5,13},{6,14},{7,15},{8,0},{9,1},... | collective-permute-start | bytes 73736 | tf_op jit(solution)/shard_map/ppermute | solution.py:17
  6.4 0.8 %copy-start.3 = (bf16[96,128]{1,0:T(8,128)(2,1)S(1)}, bf16[96,128]{1,0:T(8,128)(2,1)}, u32[]{:S(2)}) copy-start(bf16[96,128]{1,0:T(8,128)(2,1)} %get-tuple-element.8) | copy-start | bytes 73732
  6.4 5.0 %collective-permute-start = (bf16[112,128]{1,0:T(8,128)(2,1)}, bf16[112,128]{1,0:T(8,128)(2,1)S(1)}, u32[]{:S(2)}, u32[]{:S(2)}) collective-permute-start(bf16[112,128]{1,0:T(8,128)(2,1)} %get-tuple-element.7), channel_id=1, source_target_pairs={{0,8},{1,9},{2,10},{3,11},{4,12},{5,13},{6,14},{7,15},{8,0},{9,1},... | collective-permute-start | bytes 86024 | tf_op jit(solution)/shard_map/ppermute | solution.py:17
  7.4 4.0 %copy-start.2 = (bf16[112,128]{1,0:T(8,128)(2,1)S(1)}, bf16[112,128]{1,0:T(8,128)(2,1)}, u32[]{:S(2)}) copy-start(bf16[112,128]{1,0:T(8,128)(2,1)} %get-tuple-element.7) | copy-start | bytes 86020
  8.4 4.7 %collective-permute-start.5 = (bf16[192,128]{1,0:T(8,128)(2,1)S(1)}, bf16[192,128]{1,0:T(8,128)(2,1)S(1)}, u32[]{:S(2)}, u32[]{:S(2)}) collective-permute-start(bf16[192,128]{1,0:T(8,128)(2,1)S(1)} %pad_maximum_fusion.3), channel_id=1, source_target_pairs={{0,4},{1,5},{2,6},{3,7},{4,0},{5,1},{6,2},{7,3},{8,12},{9,13},{10,... | collective-permute-start | bytes 147464 | tf_op jit(solution)/shard_map/ppermute | solution.py:17
  11.3 4.2 %collective-permute-start.1 = (bf16[224,128]{1,0:T(8,128)(2,1)S(1)}, bf16[224,128]{1,0:T(8,128)(2,1)S(1)}, u32[]{:S(2)}, u32[]{:S(2)}) collective-permute-start(bf16[224,128]{1,0:T(8,128)(2,1)S(1)} %pad_maximum_fusion.2), channel_id=1, source_target_pairs={{0,4},{1,5},{2,6},{3,7},{4,0},{5,1},{6,2},{7,3},{8,12},{9,13},{10,... | collective-permute-start | bytes 172040 | tf_op jit(solution)/shard_map/ppermute | solution.py:17
  13.1 5.2 %collective-permute-start.6 = (bf16[384,128]{1,0:T(8,128)(2,1)S(1)}, bf16[384,128]{1,0:T(8,128)(2,1)S(1)}, u32[]{:S(2)}, u32[]{:S(2)}) collective-permute-start(bf16[384,128]{1,0:T(8,128)(2,1)S(1)} %pad_maximum_fusion.1), channel_id=1, source_target_pairs={{0,2},{1,3},{2,0},{3,1},{4,6},{5,7},{6,4},{7,5},{8,10},{9,11},{10,... | collective-permute-start | bytes 294920 | tf_op jit(solution)/shard_map/ppermute | solution.py:17
  15.6 4.9 %collective-permute-start.2 = (bf16[448,128]{1,0:T(8,128)(2,1)S(1)}, bf16[448,128]{1,0:T(8,128)(2,1)S(1)}, u32[]{:S(2)}, u32[]{:S(2)}) collective-permute-start(bf16[448,128]{1,0:T(8,128)(2,1)S(1)} %pad_maximum_fusion), channel_id=1, source_target_pairs={{0,2},{1,3},{2,0},{3,1},{4,6},{5,7},{6,4},{7,5},{8,10},{9,11},{10,... | collective-permute-start | bytes 344072 | tf_op jit(solution)/shard_map/ppermute | solution.py:17
  18.3 2.3 %collective-permute-start.7 = (bf16[768,128]{1,0:T(8,128)(2,1)S(1)}, bf16[768,128]{1,0:T(8,128)(2,1)S(1)}, u32[]{:S(2)}, u32[]{:S(2)}) collective-permute-start(bf16[768,128]{1,0:T(8,128)(2,1)S(1)} %constant_dynamic-update-slice_fusion.24), channel_id=1, source_target_pairs={{0,1},{1,0},{2,3},{3,2},{4,5},{5,4},{6,7},{7,6},{8,9},{9,8},{10,11... | collective-permute-start | bytes 589832 | tf_op jit(solution)/shard_map/ppermute | solution.py:17
  20.6 1.6 %collective-permute-start.3 = (bf16[896,128]{1,0:T(8,128)(2,1)S(1)}, bf16[896,128]{1,0:T(8,128)(2,1)S(1)}, u32[]{:S(2)}, u32[]{:S(2)}) collective-permute-start(bf16[896,128]{1,0:T(8,128)(2,1)S(1)} %constant_dynamic-update-slice_fusion), channel_id=1, source_target_pairs={{0,1},{1,0},{2,3},{3,2},{4,5},{5,4},{6,7},{7,6},{8,9},{9,8},{10,11... | collective-permute-start | bytes 688136 | tf_op jit(solution)/shard_map/ppermute | solution.py:17
  22.3 0.9 %copy-start = (bf16[192,384]{1,0:T(8,128)(2,1)S(1)}, bf16[192,384]{1,0:T(8,128)(2,1)}, u32[]{:S(2)}) copy-start(bf16[192,384]{1,0:T(8,128)(2,1)} %w_in_ref.1) | copy-start | bytes 442372
  22.3 0.8 %copy-start.1 = (bf16[16,4,192]{2,1,0:T(4,128)(2,1)S(1)}, bf16[16,4,192]{2,1,0:T(4,128)(2,1)}, u32[]{:S(2)}) copy-start(bf16[16,4,192]{2,1,0:T(4,128)(2,1)} %s_ref.3) | copy-start | bytes 73732

commit v2 on v0

--- a/solution.py
+++ b/solution.py
@@ -1,8 +1,11 @@
+import functools
 import math
 
 import jax
 import jax.numpy as jnp
 from jax import lax
+from jax.experimental import pallas as pl
+from jax.experimental.pallas import tpu as pltpu
 from jax.sharding import PartitionSpec as P
 
 gelu_coef = math.sqrt(2.0 / math.pi)
@@ -41,7 +44,7 @@
     )
 
 
-def on_device(features, spectrum, cotangent, w_first, w_second, w_in, w_out):
+def split_rows(features, spectrum, cotangent, w_first, w_second, w_in, w_out):
     frames, own_bins, channels = features.shape
     block = w_first.shape[1]
     quarter = frames // 4
@@ -123,6 +126,398 @@
     return (enhanced, grad_first, grad_second, grad_w_in, grad_w_out)
 
 
+f32, bf16 = jnp.float32, jnp.bfloat16
+NN = (((1,), (0,)), ((), ()))
+NT = (((1,), (1,)), ((), ()))
+TN = (((0,), (0,)), ((), ()))
+LANES = 128
+W_ROWS = 16
+CHUNK = 1024
+
+
+def mul(a, b, dims=NN):
+    return lax.dot_general(a, b, dims, preferred_element_type=f32)
+
+
+def mul_f32(a, b):
+    return lax.dot_general(a, b, NN, precision=lax.Precision.HIGHEST, preferred_element_type=f32)
+
+
+def iota(shape, dim):
+    return lax.broadcasted_iota(jnp.int32, shape, dim)
+
+
+def onehot(cond):
+    return cond.astype(f32).astype(bf16)
+
+
+def gelu_and_slope(v):
+    square = v * v
+    tanh_val = jnp.tanh(v * (gelu_coef + (gelu_coef * 0.044715) * square))
+    half = 0.5 + 0.5 * tanh_val
+    out = v * half
+    slope = half + out * (1.0 - half) * (
+        2.0 * gelu_coef + (6.0 * gelu_coef * 0.044715) * square
+    )
+    return out, slope
+
+
+class Rows:
+    def __init__(self, own, bins):
+        self.own, self.bins, self.per_block = own, bins, 2 * own
+        me = lax.axis_index("freq")
+        self.chip, self.side = me >> 1, (me & 1) * bins
+
+    def block(self, r):
+        return r // self.per_block
+
+    def place(self, r):
+        return ((r // self.own) & 1) * self.bins + (r & (self.bins - 1))
+
+    def frame(self, r):
+        return (r // self.bins) & (self.own // self.bins - 1)
+
+
+def pack_rows(rows):
+    half = rows.shape[0] // 2
+    low, high = rows[:half], rows[half:]
+    rest = jnp.concatenate([low[:, LANES:], high[:, LANES:]], 1)
+    return low[:, :LANES], high[:, :LANES], rest
+
+
+def unpacked(low, high, rest):
+    split = rest.shape[1] // 2
+    return (
+        jnp.concatenate([low, rest[:, :split]], 1),
+        jnp.concatenate([high, rest[:, split:]], 1),
+    )
+
+
+def cut(value):
+    return value[:, :LANES], value[:, LANES : 2 * LANES], value[:, 2 * LANES :]
+
+
+def piece(refs, per_device, j, start, size):
+    at = (j // 4) * per_device + start
+    return refs[j % 4][at : at + size, :]
+
+
+def tiles_of(refs, per_device, devices, own):
+    return [
+        jnp.concatenate([piece(refs, per_device, j, t * own, own) for j in range(devices)], 0)
+        for t in range(3)
+    ]
+
+
+def pack_kernel(x_ref, s_ref, c_ref, w1_ref, w2_ref, out_ref, spec_ref, *, scale):
+    frames, bins, channels = x_ref.shape
+    rows = frames * bins
+    half = rows // 2
+    half_c = channels // 2
+    block = w1_ref.shape[1]
+
+    for t, part in enumerate(pack_rows(x_ref[...].astype(f32).reshape(rows, channels))):
+        out_ref[t * half : (t + 1) * half, :] = part.astype(bf16)
+    weights = jnp.concatenate([w1_ref[...].astype(f32), w2_ref[...].astype(f32)], 1)
+    weights = jnp.concatenate([weights, jnp.zeros((bins, LANES - 2 * block), f32)], 1)
+    weights = jnp.concatenate([weights, jnp.zeros((W_ROWS - bins, LANES), f32)], 0)
+    start = 3 * half + W_ROWS
+    out_ref[3 * half : start, :] = weights.astype(bf16)
+
+    spec = s_ref[...].astype(f32).reshape(rows, channels)
+    grad = c_ref[...].astype(f32).reshape(rows, channels) * scale
+    spec_re, spec_im = spec[:, :half_c], spec[:, half_c:]
+    grad_re, grad_im = grad[:, :half_c], grad[:, half_c:]
+    dmask = jnp.concatenate(
+        [grad_re * spec_re + grad_im * spec_im, grad_im * spec_re - grad_re * spec_im], 1
+    )
+    for t, part in enumerate(pack_rows(dmask)):
+        out_ref[start + t * half : start + (t + 1) * half, :] = part.astype(bf16)
+    spec_ref[...] = s_ref[...]
+
+
+def prepare_kernel(
+    own_ref, w_in_hbm, w_out_hbm,
+    x_ref, d_ref, w_in_ref, w_out_ref, valid_ref, pick1_ref, spread1_ref, keep1_ref,
+    pick2_ref, spread2_ref, keep2_ref, chosen_ref, sems, *, bins,
+):
+    copies = [
+        pltpu.make_async_copy(w_in_hbm, w_in_ref, sems.at[0]),
+        pltpu.make_async_copy(w_out_hbm, w_out_ref, sems.at[1]),
+    ]
+    for copy in copies:
+        copy.start()
+
+    x_ref[...] = own_ref[: x_ref.shape[0], :]
+    d_ref[...] = own_ref[x_ref.shape[0] :, :]
+    own, rows = chosen_ref.shape
+    block = 2 * bins
+    at = Rows(own, bins)
+
+    def w_place(r):
+        return ((r // W_ROWS) & 1) * bins + (r & (W_ROWS - 1))
+
+    def w_block(r):
+        return r // (2 * W_ROWS)
+
+    r, w = iota(valid_ref.shape, 0), iota(valid_ref.shape, 1)
+    valid_ref[...] = onehot(((w & (W_ROWS - 1)) < bins) & (w_block(w) == at.block(r)))
+
+    r, lane = iota(pick1_ref.shape, 0), iota(pick1_ref.shape, 1)
+    pick1_ref[...] = onehot(lane == at.place(r))
+    pick2_ref[...] = onehot(lane == block + (at.place(r) ^ at.side))
+
+    w, r = iota(spread1_ref.shape, 0), iota(spread1_ref.shape, 1)
+    spread1_ref[...] = onehot((w_place(w) == at.place(r)) & (w_block(w) == at.block(r)))
+    spread2_ref[...] = onehot(w_place(w) == (at.block(r) ^ at.chip ^ at.side))
+
+    row, col = iota(keep1_ref.shape, 0), iota(keep1_ref.shape, 1)
+    same_frame = at.frame(row) == at.frame(col)
+    keep1_ref[...] = onehot(same_frame)
+    keep2_ref[...] = onehot(same_frame & (at.place(col) == (at.block(row) ^ at.chip)))
+
+    row, col = iota(chosen_ref.shape, 0), iota(chosen_ref.shape, 1)
+    chosen_ref[...] = onehot(
+        (at.block(col) == ((at.side + (row & (bins - 1))) ^ at.chip))
+        & (at.place(col) == at.chip)
+        & (at.frame(row) == at.frame(col))
+    )
+    for copy in copies:
+        copy.wait()
+
+
+def forward_kernel(
+    x0, x1, x2, x3, w_in_ref, valid_ref, pick1_ref, spread1_ref, keep1_ref,
+    pick2_ref, spread2_ref, keep2_ref, chosen_ref,
+    hid_ref, slope_ref, spt_ref, back_ref, first_ref, own_ref, sp_own_ref,
+    sp_ref,
+):
+    own = own_ref.shape[0] // 2
+    per_x = 3 * own + W_ROWS
+    devices = 4 * x0.shape[0] // per_x
+    rows = devices * own
+    refs = (x0, x1, x2, x3)
+
+    x_tiles = tiles_of(refs, per_x, devices, own)
+    weights = jnp.concatenate(
+        [piece(refs, per_x, j, 3 * own, W_ROWS) for j in range(devices)], 0
+    )
+
+    def mixing(pick, spread, keep):
+        of_row = mul(pick[...], weights, NT).astype(bf16) * valid_ref[...]
+        return mul(of_row, spread[...]).astype(bf16) * keep[...]
+
+    mix1 = mixing(pick1_ref, spread1_ref, keep1_ref)
+    mix2 = mixing(pick2_ref, spread2_ref, keep2_ref)
+    back_ref[...] = mix2[:, : 2 * own]
+
+    first = mul(mix1, jnp.concatenate(x_tiles, 1)).astype(bf16)
+    spectral = mul(mix2, first).astype(bf16)
+    sp_low, sp_high = unpacked(*cut(spectral))
+    sp_ref[:rows, :] = sp_low
+    sp_ref[rows:, :] = sp_high
+    sp_own_ref[:own, :], sp_own_ref[own:, :] = sp_low[:own], sp_high[:own]
+    own_ref[:own, :], own_ref[own:, :] = unpacked(*[tile[:own] for tile in x_tiles])
+
+    first_ref[:own, :], first_ref[own:, :] = unpacked(
+        *cut(mul(chosen_ref[...], first).astype(bf16))
+    )
+
+    @pl.loop(0, 2 * rows // CHUNK)
+    def _(i):
+        here = pl.ds(pl.multiple_of(i * CHUNK, CHUNK), CHUNK)
+        sp = sp_ref[here, :]
+        gelu_out, slope = gelu_and_slope(mul(sp, w_in_ref[...]))
+        hid_ref[here, :] = gelu_out.astype(bf16)
+        slope_ref[here, :] = slope
+        spt_ref[:, here] = sp.T
+
+
+def backward_kernel(
+    d0, d1, d2, d3, hid_ref, slope_ref, spt_ref, back_ref, first_ref, own_ref, sp_own_ref,
+    s_ref, w_in_ref, w_out_ref,
+    enh_ref, g1_ref, g2_ref, gwi_ref, gwo_ref,
+    dm_ref, dsp_ref,
+):
+    bins, block = g1_ref.shape
+    frames, _, channels = s_ref.shape
+    half_c = channels // 2
+    own = own_ref.shape[0] // 2
+    devices = 4 * d0.shape[0] // (3 * own)
+    rows = devices * own
+    at = Rows(own, bins)
+    dm_low, dm_high = unpacked(*tiles_of((d0, d1, d2, d3), 3 * own, devices, own))
+    dm_ref[:rows, :] = dm_low
+    dm_ref[rows:, :] = dm_high
+
+    sp_own = sp_own_ref[...]
+    hidden = jnp.concatenate([hid_ref[:own, :], hid_ref[rows : rows + own, :]], 0)
+    mask = (sp_own.astype(f32) + mul(hidden, w_out_ref[...], NT)).astype(bf16).astype(f32)
+    spec = s_ref[...].astype(f32).reshape(2 * own, channels)
+    spec_re, spec_im = spec[:, :half_c], spec[:, half_c:]
+    mask_re, mask_im = mask[:, :half_c], mask[:, half_c:]
+    enhanced = jnp.concatenate(
+        [spec_re * mask_re - spec_im * mask_im, spec_re * mask_im + spec_im * mask_re], 1
+    )
+    enh_ref[...] = enhanced.reshape(frames, bins, channels).astype(bf16)
+
+    gwi_ref[...] = jnp.zeros_like(gwi_ref)
+    gwo_ref[...] = jnp.zeros_like(gwo_ref)
+
+    @pl.loop(0, 2 * rows // CHUNK)
+    def _(i):
+        here = pl.ds(pl.multiple_of(i * CHUNK, CHUNK), CHUNK)
+        dm = dm_ref[here, :]
+        dpre = (mul(dm, w_out_ref[...]) * slope_ref[here, :]).astype(bf16)
+        gwo_ref[...] += mul(dm, hid_ref[here, :], TN)
+        gwi_ref[...] += mul(spt_ref[:, here], dpre)
+        dsp_ref[here, :] = (dm.astype(f32) + mul(dpre, w_in_ref[...], NT)).astype(bf16)
+
+    dsp_low, dsp_high = dsp_ref[:rows, :], dsp_ref[rows:, :]
+    dfirst_low = mul(back_ref[...], dsp_low, TN).astype(bf16)
+    dfirst_high = mul(back_ref[...], dsp_high, TN).astype(bf16)
+
+    per_block = at.per_block
+    frames_meet = at.frame(iota((own, per_block), 0)) == at.frame(iota((own, per_block), 1))
+
+    def bin_sums(gram):
+        parts = jnp.where(frames_meet, gram, 0.0)
+        total = sum(parts[n : n + 2 * bins] for n in range(0, own, 2 * bins))
+        return total[:bins] + total[bins:]
+
+    gram = mul(own_ref[:own, :], dfirst_low, NT) + mul(own_ref[own:, :], dfirst_high, NT)
+    sums = [bin_sums(gram)]
+    gram = mul(first_ref[:own, :], dsp_low[:per_block], NT)
+    gram += mul(first_ref[own:, :], dsp_high[:per_block], NT)
+    sums.append(bin_sums(gram))
+    row, col = iota((2 * per_block, 2 * block), 0), iota((2 * per_block, 2 * block), 1)
+    place = at.place(row & (per_block - 1))
+    take = ((row < per_block) & (place == col)) | (
+        (row >= per_block) & (block + (place ^ at.side) == col)
+    )
+    both = mul_f32(jnp.concatenate(sums, 1), take.astype(f32))
+    g1_ref[...] = both[:, :block]
+    g2_ref[...] = both[:, block:]
+
+
+def whole_rows(features, spectrum, cotangent, w_first, w_second, w_in, w_out):
+    frames, bins, channels = features.shape
+    block = w_first.shape[1]
+    hid = w_in.shape[1]
+    devices = lax.axis_size("freq")
+    own = frames // 2 * bins
+    rows = devices * own
+    in_vmem = lambda n: [pl.BlockSpec(memory_space=pltpu.VMEM)] * n
+    in_hbm = lambda n: [pl.BlockSpec(memory_space=pltpu.HBM)] * n
+    shaped = jax.ShapeDtypeStruct
+    params = pltpu.CompilerParams(vmem_limit_bytes=40 * 2**20)
+    scale = 1.0 / math.sqrt(frames * devices * bins)
+    own_rows, spec_in = pl.pallas_call(
+        functools.partial(pack_kernel, scale=scale),
+        out_shape=(
+            pltpu.VMEM((6 * own + W_ROWS, LANES), bf16),
+            pltpu.VMEM((frames, bins, channels), bf16),
+        ),
+        in_specs=in_vmem(5),
+        out_specs=tuple(in_vmem(2)),
+        name="pack",
+    )(features, spectrum, cotangent, w_first, w_second)
+    w_rows = devices * W_ROWS
+    x_own, d_own, w_in_in, w_out_in, *selections = pl.pallas_call(
+        functools.partial(prepare_kernel, bins=bins),
+        out_shape=tuple(
+            pltpu.VMEM(shape, bf16)
+            for shape in [
+                (3 * own + W_ROWS, LANES),
+                (3 * own, LANES),
+                (channels, hid),
+                (channels, hid),
+                (rows, w_rows),
+                (rows, LANES),
+                (w_rows, rows),
+                (rows, rows),
+                (rows, LANES),
+                (w_rows, rows),
+                (rows, rows),
+                (own, rows),
+            ]
+        ),
+        in_specs=in_vmem(1) + in_hbm(2),
+        out_specs=tuple(in_vmem(12)),
+        scratch_shapes=[pltpu.SemaphoreType.DMA((2,))],
+        compiler_params=params,
+        cost_estimate=pl.CostEstimate(flops=0, bytes_accessed=2**21, transcendentals=0),
+        name="prepare",
+    )(own_rows, w_in, w_out.T)
+
+    columns = [exchanged(own_rows, j) for j in range(devices - 4, 0, -4)][::-1]
+    x_rows = 3 * own + W_ROWS
+    x0 = jnp.concatenate([x_own] + [column[:x_rows] for column in columns], 0)
+    d0 = jnp.concatenate([d_own] + [column[x_rows:] for column in columns], 0)
+    x2, d2 = exchanged(x0, 2), exchanged(d0, 2)
+    x1, d1 = exchanged(x0, 1), exchanged(d0, 1)
+    x3, d3 = exchanged(x2, 1), exchanged(d2, 1)
+
+    kept = pl.pallas_call(
+        forward_kernel,
+        out_shape=(
+            shaped((2 * rows, hid), bf16),
+            shaped((2 * rows, hid), f32),
+            shaped((channels, 2 * rows), bf16),
+            shaped((rows, 2 * own), bf16),
+            shaped((2 * own, channels), bf16),
+            shaped((2 * own, channels), bf16),
+            shaped((2 * own, channels), bf16),
+        ),
+        in_specs=in_vmem(13),
+        out_specs=tuple(in_vmem(7)),
+        scratch_shapes=[pltpu.VMEM((2 * rows, channels), bf16)],
+        compiler_params=params,
+        name="forward",
+    )(x0, x1, x2, x3, w_in_in, *selections)
+
+    enhanced, grad_first, grad_second, grad_w_in, grad_w_out = pl.pallas_call(
+        backward_kernel,
+        out_shape=(
+            shaped((frames, bins, channels), bf16),
+            shaped((bins, block), f32),
+            shaped((bins, block), f32),
+            shaped((channels, hid), f32),
+            shaped((channels, hid), f32),
+        ),
+        in_specs=in_vmem(14),
+        out_specs=tuple(in_vmem(5)),
+        scratch_shapes=[pltpu.VMEM((2 * rows, channels), bf16)] * 2,
+        compiler_params=params,
+        name="backward",
+    )(d0, d1, d2, d3, *kept, spec_in, w_in_in, w_out_in)
+    return enhanced, grad_first, grad_second, grad_w_in, grad_w_out.T
+
+
+def exchanged(value, mask):
+    pairs = [(source, source ^ mask) for source in range(lax.axis_size("freq"))]
+    return lax.ppermute(value, "freq", pairs)
+
+
+def on_device(features, spectrum, cotangent, w_first, w_second, w_in, w_out):
+    frames, bins, channels = features.shape
+    block = w_first.shape[1]
+    devices = lax.axis_size("freq")
+    gathered_bytes = 2 * 2 * devices * frames * bins * channels
+    fits = gathered_bytes <= 4 * 2**20
+    shaped = (
+        block == 2 * bins
+        and devices == 2 * block
+        and bins <= W_ROWS
+        and 2 * block <= LANES
+        and LANES < channels
+        and 2 * (channels - LANES) == LANES
+        and devices % 4 == 0
+    )
+    plan = whole_rows if fits and shaped else split_rows
+    return plan(features, spectrum, cotangent, w_first, w_second, w_in, w_out)
+
+
 def solution(mesh):
     placed = (
         P("groups", "freq", None),

time: 145 us -> 24.7 us (0.17)
  waiting for transfers between devices: 103 us -> 6.73 us
  between operations: 14.3 us -> 0.71 us
  Pallas kernels: 0 us -> 6.81 us
  local copies, waits for them, and re-layouts: 7.63 us -> 1.84 us
  matrix products: 4.81 us -> 0 us
  starting transfers between devices: 12 us -> 8.33 us
  other arithmetic: 3.06 us -> 0.02 us
    psum x1 -> x0, waiting for transfers between devices: 89.3 us -> none  [on_device(): grad_w_in, grad_w_out = lax.psum((part_in, part_out), 'freq')]
    all_to_all x2 -> x0, waiting for transfers between devices: 12.3 us -> none  [the longest x1 6.93 us: on_device(): lax.all_to_all(partials, 'freq', split_axis=0, concat_axis=0, tiled=True)]
    all_to_all x2 -> x0, starting transfers between devices: 11 us -> none  [the longest x1 7.52 us: on_device(): lax.all_to_all(partials, 'freq', split_axis=0, concat_axis=0, tiled=True)]
    ppermute x4 -> x9, starting transfers between devices: 0.99 us -> 8.33 us  [exchanged(): return lax.ppermute(value, 'freq', pairs)]
    pallas_call x0 -> x4, Pallas kernels: none -> 6.81 us  [the longest x1 2.67 us: whole_rows(): pl.pallas_call(backward_kernel, out_shape=(shaped((frames, bins, channels...]
    ppermute x4 -> x9, waiting for transfers between devices: 0.79 us -> 6.73 us  [exchanged(): return lax.ppermute(value, 'freq', pairs)]
    dot_general x11 -> x0, matrix products: 4.81 us -> none  [the longest x1 0.96 us: on_device(): jnp.einsum('hgtbc,bp->pghtc', by_quarter, w_first, preferred_element_type...]
    unnamed x20 -> x4, local copies, waits for them, and re-layouts: 5.77 us -> 1.82 us
  transfers between devices with their start and end apart: 7 -> 9, of which waited for: 5 -> 4; matrix products, arithmetic and copies ran while one was open for 3% -> 0% of each run, Pallas kernels for 0% -> 13%
where the time goes in v2:
time: 24.7 us; the launch traced here: 24.4 us
  starting transfers between devices  8.33 us (34%)
  Pallas kernels  6.81 us (28%)
  waiting for transfers between devices  6.73 us (27%)
  local copies, waits for them, and re-layouts  1.84 us (7%)
  between operations  0.71 us (3%)
    ppermute x9, starting transfers between devices, exchanged(): return lax.ppermute(value, 'freq', pairs)  8.33 us
    ppermute x9, waiting for transfers between devices, exchanged(): return lax.ppermute(value, 'freq', pairs)  6.73 us
    pallas_call x1, Pallas kernels, whole_rows(): pl.pallas_call(backward_kernel, out_shape=(shaped((frames, bins, channels...  2.67 us
    pallas_call x1, Pallas kernels, whole_rows(): pl.pallas_call(forward_kernel, out_shape=(shaped((2 * rows, hid), bf16),...  2.15 us
    unnamed x4, local copies, waits for them, and re-layouts  1.82 us
    pallas_call x1, Pallas kernels, whole_rows(): pl.pallas_call(functools.partial(pack_kernel, scale=scale), out_shape=(pl...  1.03 us
    pallas_call x1, Pallas kernels, whole_rows(): pl.pallas_call(functools.partial(prepare_kernel, bins=bins), out_shape=tu...  0.96 us
  transfers between devices with their start and end apart: 9, of which 4 were waited for; matrix products, arithmetic and copies ran while one was open for 0% of the time, Pallas kernels for 13%

profile of v2, /device:TPU:0, one launch (start us, length us, event | category | flops | bytes accessed | tf_op | source)
XLA Modules:
  0.0 24.4 jit_solution(15396303182217109079)
XLA Ops:
  0.6 1.0 %pack.1 = (bf16[208,128]{1,0:T(8,128)(2,1)S(1)}, bf16[16,4,192]{2,1,0:T(4,128)(2,1)S(1)}) custom-call(bf16[16,4,192]{2,1,0:T(4,128)(2,1)} %x_ref.1, bf16[16,4,192]{2,1,0:T(4,128)(2,1)} %s_ref.1, bf16[16,4,192]{2,1,0:T(4,128)(2,1)} %c_ref.1, bf16[4,8]{1,0:T(4,128)(2,1)} %w1_ref.1, bf16[4,8]{1,0:T(4,128)(2,1)} %w2_ref.1), custom_call_target="tpu_custom_call" | custom-call | tf_op jit(solution)/shard_map/pack/pallas_call | solution.py:415
  1.7 3.1 %collective-permute-start = (bf16[208,128]{1,0:T(8,128)(2,1)S(1)}, bf16[208,128]{1,0:T(8,128)(2,1)S(1)}, u32[]{:S(2)}, u32[]{:S(2)}) collective-permute-start(bf16[208,128]{1,0:T(8,128)(2,1)S(1)} %get-tuple-element.31.own_ref), channel_id=1, source_target_pairs={{0,4},{1,5},{2,6},{3,7},{4,0},{5,1},{6,2},{7,3},{8,12},{9,13},{10,... | collective-permute-start | bytes 159752 | tf_op jit(solution)/shard_map/ppermute | solution.py:499
  4.7 2.6 %collective-permute-start.1 = (bf16[208,128]{1,0:T(8,128)(2,1)S(1)}, bf16[208,128]{1,0:T(8,128)(2,1)S(1)}, u32[]{:S(2)}, u32[]{:S(2)}) collective-permute-start(bf16[208,128]{1,0:T(8,128)(2,1)S(1)} %get-tuple-element.31.own_ref), channel_id=1, source_target_pairs={{0,8},{1,9},{2,10},{3,11},{4,12},{5,13},{6,14},{7,15},{8,0},{9,1},... | collective-permute-start | bytes 159752 | tf_op jit(solution)/shard_map/ppermute | solution.py:499
  7.3 0.0 collective-permute-start.2
  7.3 0.0 copy-start
  7.3 0.9 %copy-done = bf16[192,384]{1,0:T(8,128)(2,1)S(1)} copy-done((bf16[192,384]{1,0:T(8,128)(2,1)S(1)}, bf16[192,384]{1,0:T(8,128)(2,1)}, u32[]{:S(2)}) %copy-start) | copy-done | bytes 147480
  8.2 0.0 copy-start.1
  8.2 0.9 %copy-done.1 = bf16[384,192]{0,1:T(8,128)(2,1)S(1)} copy-done((bf16[384,192]{0,1:T(8,128)(2,1)S(1)}, bf16[384,192]{0,1:T(8,128)(2,1)}, u32[]{:S(2)}) %copy-start.1) | copy-done | bytes 147480
  9.1 1.0 %prepare.1 = (bf16[112,128]{1,0:T(8,128)(2,1)S(1)}, bf16[96,128]{1,0:T(8,128)(2,1)S(1)}, bf16[192,384]{1,0:T(8,128)(2,1)S(1)}, bf16[192,384]{1,0:T(8,128)(2,1)S(...) custom-call(bf16[208,128]{1,0:T(8,128)(2,1)S(1)} %get-tuple-element., ...), custom_call_target="tpu_custom_call" | custom-call | bytes 2097152 | tf_op jit(solution)/shard_map/prepare/pallas_call | solution.py:426
  10.1 0.0 collective-permute-done
  10.1 0.7 %collective-permute-done.1 = bf16[208,128]{1,0:T(8,128)(2,1)S(1)} collective-permute-done((bf16[208,128]{1,0:T(8,128)(2,1)S(1)}, bf16[208,128]{1,0:T(8,128)(2,1)S(1)}, u32[]{:S(2)}, u32[]{:S(2)}) %collective-permute-start.1) | collective-permute-done | bytes 53280 | tf_op jit(solution)/shard_map/ppermute | solution.py:499
  10.8 2.5 %collective-permute-done.2 = bf16[208,128]{1,0:T(8,128)(2,1)S(1)} collective-permute-done((bf16[208,128]{1,0:T(8,128)(2,1)S(1)}, bf16[208,128]{1,0:T(8,128)(2,1)S(1)}, u32[]{:S(2)}, u32[]{:S(2)}) %collective-permute-start.2) | collective-permute-done | bytes 53280 | tf_op jit(solution)/shard_map/ppermute | solution.py:499
  13.3 1.6 %collective-permute-start.7 = (bf16[448,128]{1,0:T(8,128)(2,1)S(1)}, bf16[448,128]{1,0:T(8,128)(2,1)S(1)}, u32[]{:S(2)}, u32[]{:S(2)}) collective-permute-start(bf16[448,128]{1,0:T(8,128)(2,1)S(1)} %pad_maximum_fusion.x0), channel_id=1, source_target_pairs={{0,2},{1,3},{2,0},{3,1},{4,6},{5,7},{6,4},{7,5},{8,10},{9,11},{10,... | collective-permute-start | bytes 344072 | tf_op jit(solution)/shard_map/ppermute | solution.py:499
  14.9 0.6 %collective-permute-start.4 = (bf16[384,128]{1,0:T(8,128)(2,1)S(1)}, bf16[384,128]{1,0:T(8,128)(2,1)S(1)}, u32[]{:S(2)}, u32[]{:S(2)}) collective-permute-start(bf16[384,128]{1,0:T(8,128)(2,1)S(1)} %pad_maximum_fusion.1.d0), channel_id=1, source_target_pairs={{0,2},{1,3},{2,0},{3,1},{4,6},{5,7},{6,4},{7,5},{8,10},{9,11},{10,... | collective-permute-start | bytes 294920 | tf_op jit(solution)/shard_map/ppermute | solution.py:499
  15.5 0.0 collective-permute-start.6
  15.5 2.7 %collective-permute-done.7.x2 = bf16[448,128]{1,0:T(8,128)(2,1)S(1)} collective-permute-done((bf16[448,128]{1,0:T(8,128)(2,1)S(1)}, bf16[448,128]{1,0:T(8,128)(2,1)S(1)}, u32[]{:S(2)}, u32[]{:S(2)}) %collective-permute-start.7) | collective-permute-done | bytes 114720 | tf_op jit(solution)/shard_map/ppermute | solution.py:499
  18.1 0.0 collective-permute-start.8
  18.1 0.5 %collective-permute-start.3 = (bf16[384,128]{1,0:T(8,128)(2,1)S(1)}, bf16[384,128]{1,0:T(8,128)(2,1)S(1)}, u32[]{:S(2)}, u32[]{:S(2)}) collective-permute-start(bf16[384,128]{1,0:T(8,128)(2,1)S(1)} %pad_maximum_fusion.1.d0), channel_id=1, source_target_pairs={{0,1},{1,0},{2,3},{3,2},{4,5},{5,4},{6,7},{7,6},{8,9},{9,8},{10,11... | collective-permute-start | bytes 294920 | tf_op jit(solution)/shard_map/ppermute | solution.py:499
  18.6 0.9 %collective-permute-done.4.d2 = bf16[384,128]{1,0:T(8,128)(2,1)S(1)} collective-permute-done((bf16[384,128]{1,0:T(8,128)(2,1)S(1)}, bf16[384,128]{1,0:T(8,128)(2,1)S(1)}, u32[]{:S(2)}, u32[]{:S(2)}) %collective-permute-start.4) | collective-permute-done | bytes 98336 | tf_op jit(solution)/shard_map/ppermute | solution.py:499
  19.6 0.0 collective-permute-start.5
  19.6 0.0 collective-permute-done.6.x1
  19.6 0.0 collective-permute-done.8.x3
  19.6 2.2 %forward.1 = (bf16[1024,384]{1,0:T(8,128)(2,1)S(1)}, f32[1024,384]{1,0:T(8,128)S(1)}, bf16[192,1024]{1,0:T(8,128)(2,1)S(1)}, bf16[512,64]{1,0:T(8,128)(2,1)S(1)}...) custom-call(bf16[448,128]{1,0:T(8,128)(2,1)S(1)} %pad_maximum_fusion.x0, ...), custom_call_target="tpu_custom_call" | custom-call | tf_op jit(solution)/shard_map/forward/pallas_call | solution.py:461
  21.7 0.0 collective-permute-done.3.d1
  21.7 0.0 collective-permute-done.5.d3
  21.8 2.7 %backward.1 = (bf16[16,4,192]{2,1,0:T(4,128)(2,1)}, f32[4,8]{1,0:T(4,128)}, f32[4,8]{1,0:T(4,128)}, f32[192,384]{1,0:T(8,128)}, f32[192,384]{1,0:T(8,128)}) custom-call(bf16[384,128]{1,0:T(8,128)(2,1)S(1)} %pad_maximum_fusion.1.d0, bf16[384,128]{1,0:T(8,128)(2,1)S(1)} %collective-permute-done.3.d1, bf16[384,128]{1,0:T(8,128)(2,1)S(1)} %collective-permute-done.4.d2, ...), custom_call_target="tpu_custom_call" | custom-call | tf_op jit(solution)/shard_map/backward/pallas_call | solution.py:479
  (8 shorter events, 0.0 us)
Async XLA Ops:
  1.7 8.4 %collective-permute-start = (bf16[208,128]{1,0:T(8,128)(2,1)S(1)}, bf16[208,128]{1,0:T(8,128)(2,1)S(1)}, u32[]{:S(2)}, u32[]{:S(2)}) collective-permute-start(bf16[208,128]{1,0:T(8,128)(2,1)S(1)} %get-tuple-element.31.own_ref), channel_id=1, source_target_pairs={{0,4},{1,5},{2,6},{3,7},{4,0},{5,1},{6,2},{7,3},{8,12},{9,13},{10,... | collective-permute-start | bytes 159752 | tf_op jit(solution)/shard_map/ppermute | solution.py:499
  4.7 6.1 %collective-permute-start.1 = (bf16[208,128]{1,0:T(8,128)(2,1)S(1)}, bf16[208,128]{1,0:T(8,128)(2,1)S(1)}, u32[]{:S(2)}, u32[]{:S(2)}) collective-permute-start(bf16[208,128]{1,0:T(8,128)(2,1)S(1)} %get-tuple-element.31.own_ref), channel_id=1, source_target_pairs={{0,8},{1,9},{2,10},{3,11},{4,12},{5,13},{6,14},{7,15},{8,0},{9,1},... | collective-permute-start | bytes 159752 | tf_op jit(solution)/shard_map/ppermute | solution.py:499
  7.3 5.9 %collective-permute-start.2 = (bf16[208,128]{1,0:T(8,128)(2,1)S(1)}, bf16[208,128]{1,0:T(8,128)(2,1)S(1)}, u32[]{:S(2)}, u32[]{:S(2)}) collective-permute-start(bf16[208,128]{1,0:T(8,128)(2,1)S(1)} %get-tuple-element.31.own_ref), channel_id=1, source_target_pairs={{0,12},{1,13},{2,14},{3,15},{4,8},{5,9},{6,10},{7,11},{8,4},{9,5},... | collective-permute-start | bytes 159752 | tf_op jit(solution)/shard_map/ppermute | solution.py:499
  7.3 0.9 %copy-start = (bf16[192,384]{1,0:T(8,128)(2,1)S(1)}, bf16[192,384]{1,0:T(8,128)(2,1)}, u32[]{:S(2)}) copy-start(bf16[192,384]{1,0:T(8,128)(2,1)} %w_in_hbm.1) | copy-start | bytes 442372
  8.2 0.9 %copy-start.1 = (bf16[384,192]{0,1:T(8,128)(2,1)S(1)}, bf16[384,192]{0,1:T(8,128)(2,1)}, u32[]{:S(2)}) copy-start(bf16[384,192]{0,1:T(8,128)(2,1)} %param.13) | copy-start | bytes 442372
  13.3 4.9 %collective-permute-start.7 = (bf16[448,128]{1,0:T(8,128)(2,1)S(1)}, bf16[448,128]{1,0:T(8,128)(2,1)S(1)}, u32[]{:S(2)}, u32[]{:S(2)}) collective-permute-start(bf16[448,128]{1,0:T(8,128)(2,1)S(1)} %pad_maximum_fusion.x0), channel_id=1, source_target_pairs={{0,2},{1,3},{2,0},{3,1},{4,6},{5,7},{6,4},{7,5},{8,10},{9,11},{10,... | collective-permute-start | bytes 344072 | tf_op jit(solution)/shard_map/ppermute | solution.py:499
  14.9 4.7 %collective-permute-start.4 = (bf16[384,128]{1,0:T(8,128)(2,1)S(1)}, bf16[384,128]{1,0:T(8,128)(2,1)S(1)}, u32[]{:S(2)}, u32[]{:S(2)}) collective-permute-start(bf16[384,128]{1,0:T(8,128)(2,1)S(1)} %pad_maximum_fusion.1.d0), channel_id=1, source_target_pairs={{0,2},{1,3},{2,0},{3,1},{4,6},{5,7},{6,4},{7,5},{8,10},{9,11},{10,... | collective-permute-start | bytes 294920 | tf_op jit(solution)/shard_map/ppermute | solution.py:499
  15.5 4.1 %collective-permute-start.6 = (bf16[448,128]{1,0:T(8,128)(2,1)S(1)}, bf16[448,128]{1,0:T(8,128)(2,1)S(1)}, u32[]{:S(2)}, u32[]{:S(2)}) collective-permute-start(bf16[448,128]{1,0:T(8,128)(2,1)S(1)} %pad_maximum_fusion.x0), channel_id=1, source_target_pairs={{0,1},{1,0},{2,3},{3,2},{4,5},{5,4},{6,7},{7,6},{8,9},{9,8},{10,11... | collective-permute-start | bytes 344072 | tf_op jit(solution)/shard_map/ppermute | solution.py:499
  18.1 1.4 %collective-permute-start.8 = (bf16[448,128]{1,0:T(8,128)(2,1)S(1)}, bf16[448,128]{1,0:T(8,128)(2,1)S(1)}, u32[]{:S(2)}, u32[]{:S(2)}) collective-permute-start(bf16[448,128]{1,0:T(8,128)(2,1)S(1)} %collective-permute-done.7.x2), channel_id=1, source_target_pairs={{0,1},{1,0},{2,3},{3,2},{4,5},{5,4},{6,7},{7,6},{8,9},{9,8},{10,11... | collective-permute-start | bytes 344072 | tf_op jit(solution)/shard_map/ppermute | solution.py:499
  18.1 3.6 %collective-permute-start.3 = (bf16[384,128]{1,0:T(8,128)(2,1)S(1)}, bf16[384,128]{1,0:T(8,128)(2,1)S(1)}, u32[]{:S(2)}, u32[]{:S(2)}) collective-permute-start(bf16[384,128]{1,0:T(8,128)(2,1)S(1)} %pad_maximum_fusion.1.d0), channel_id=1, source_target_pairs={{0,1},{1,0},{2,3},{3,2},{4,5},{5,4},{6,7},{7,6},{8,9},{9,8},{10,11... | collective-permute-start | bytes 294920 | tf_op jit(solution)/shard_map/ppermute | solution.py:499
  19.6 2.2 %collective-permute-start.5 = (bf16[384,128]{1,0:T(8,128)(2,1)S(1)}, bf16[384,128]{1,0:T(8,128)(2,1)S(1)}, u32[]{:S(2)}, u32[]{:S(2)}) collective-permute-start(bf16[384,128]{1,0:T(8,128)(2,1)S(1)} %collective-permute-done.4.d2), channel_id=1, source_target_pairs={{0,1},{1,0},{2,3},{3,2},{4,5},{5,4},{6,7},{7,6},{8,9},{9,8},{10,11... | collective-permute-start | bytes 294920 | tf_op jit(solution)/shard_map/ppermute | solution.py:499

commit v3 on v2

--- a/solution.py
+++ b/solution.py
@@ -132,7 +132,6 @@
 TN = (((0,), (0,)), ((), ()))
 LANES = 128
 W_ROWS = 16
-CHUNK = 1024
 
 
 def mul(a, b, dims=NN):
@@ -197,9 +196,17 @@
     return value[:, :LANES], value[:, LANES : 2 * LANES], value[:, 2 * LANES :]
 
 
+def received_from(devices):
+    column = [*range(devices - 4, 0, -4)]
+    near, far = [*column, 0], [j ^ 2 for j in [*column, 0]]
+    return [near, [j ^ 1 for j in near], far, [j ^ 1 for j in far]]
+
+
 def piece(refs, per_device, j, start, size):
-    at = (j // 4) * per_device + start
-    return refs[j % 4][at : at + size, :]
+    held = received_from(sum(ref.shape[0] for ref in refs) // per_device)
+    n = next(n for n, part in enumerate(held) if j in part)
+    at = held[n].index(j) * per_device + start
+    return refs[n][at : at + size, :]
 
 
 def tiles_of(refs, per_device, devices, own):
@@ -209,7 +216,29 @@
     ]
 
 
-def pack_kernel(x_ref, s_ref, c_ref, w1_ref, w2_ref, out_ref, spec_ref, *, scale):
+def pack_kernel(
+    x_hbm, s_hbm, c_hbm, w1_hbm, w2_hbm, w_in_hbm, w_out_hbm,
+    out_ref, s_ref, w_in_ref, w_out_ref,
+    x_ref, c_ref, w1_ref, w2_ref, sems, *, scale,
+):
+    copies = [
+        pltpu.make_async_copy(src, dst, sems.at[n])
+        for n, (src, dst) in enumerate(
+            [
+                (x_hbm, x_ref),
+                (w1_hbm, w1_ref),
+                (w2_hbm, w2_ref),
+                (s_hbm, s_ref),
+                (c_hbm, c_ref),
+                (w_in_hbm, w_in_ref),
+                (w_out_hbm, w_out_ref),
+            ]
+        )
+    ]
+    for copy in copies:
+        copy.start()
+    for copy in copies[:3]:
+        copy.wait()
     frames, bins, channels = x_ref.shape
     rows = frames * bins
     half = rows // 2
@@ -224,6 +253,8 @@
     start = 3 * half + W_ROWS
     out_ref[3 * half : start, :] = weights.astype(bf16)
 
+    for copy in copies[3:5]:
+        copy.wait()
     spec = s_ref[...].astype(f32).reshape(rows, channels)
     grad = c_ref[...].astype(f32).reshape(rows, channels) * scale
     spec_re, spec_im = spec[:, :half_c], spec[:, half_c:]
@@ -233,21 +264,15 @@
     )
     for t, part in enumerate(pack_rows(dmask)):
         out_ref[start + t * half : start + (t + 1) * half, :] = part.astype(bf16)
-    spec_ref[...] = s_ref[...]
+    for copy in copies[5:]:
+        copy.wait()
 
 
 def prepare_kernel(
-    own_ref, w_in_hbm, w_out_hbm,
-    x_ref, d_ref, w_in_ref, w_out_ref, valid_ref, pick1_ref, spread1_ref, keep1_ref,
-    pick2_ref, spread2_ref, keep2_ref, chosen_ref, sems, *, bins,
+    own_ref, w_in_ref, x_ref, d_ref, w_in_t_ref, valid_ref, pick1_ref, spread1_ref, keep1_ref,
+    pick2_ref, spread2_ref, keep2_ref, chosen_ref, *, bins,
 ):
-    copies = [
-        pltpu.make_async_copy(w_in_hbm, w_in_ref, sems.at[0]),
-        pltpu.make_async_copy(w_out_hbm, w_out_ref, sems.at[1]),
-    ]
-    for copy in copies:
-        copy.start()
-
+    w_in_t_ref[...] = w_in_ref[...].T
     x_ref[...] = own_ref[: x_ref.shape[0], :]
     d_ref[...] = own_ref[x_ref.shape[0] :, :]
     own, rows = chosen_ref.shape
@@ -269,12 +294,15 @@
 
     w, r = iota(spread1_ref.shape, 0), iota(spread1_ref.shape, 1)
     spread1_ref[...] = onehot((w_place(w) == at.place(r)) & (w_block(w) == at.block(r)))
+    w, r = iota(spread2_ref.shape, 0), iota(spread2_ref.shape, 1)
     spread2_ref[...] = onehot(w_place(w) == (at.block(r) ^ at.chip ^ at.side))
 
     row, col = iota(keep1_ref.shape, 0), iota(keep1_ref.shape, 1)
-    same_frame = at.frame(row) == at.frame(col)
-    keep1_ref[...] = onehot(same_frame)
-    keep2_ref[...] = onehot(same_frame & (at.place(col) == (at.block(row) ^ at.chip)))
+    keep1_ref[...] = onehot(at.frame(row) == at.frame(col))
+    row, col = iota(keep2_ref.shape, 0), iota(keep2_ref.shape, 1)
+    keep2_ref[...] = onehot(
+        (at.frame(row) == at.frame(col)) & (at.place(col) == (at.block(row) ^ at.chip))
+    )
 
     row, col = iota(chosen_ref.shape, 0), iota(chosen_ref.shape, 1)
     chosen_ref[...] = onehot(
@@ -282,40 +310,42 @@
         & (at.place(col) == at.chip)
         & (at.frame(row) == at.frame(col))
     )
-    for copy in copies:
-        copy.wait()
 
 
 def forward_kernel(
     x0, x1, x2, x3, w_in_ref, valid_ref, pick1_ref, spread1_ref, keep1_ref,
     pick2_ref, spread2_ref, keep2_ref, chosen_ref,
     hid_ref, slope_ref, spt_ref, back_ref, first_ref, own_ref, sp_own_ref,
-    sp_ref,
 ):
     own = own_ref.shape[0] // 2
     per_x = 3 * own + W_ROWS
-    devices = 4 * x0.shape[0] // per_x
+    refs = (x0, x1, x2, x3)
+    devices = sum(ref.shape[0] for ref in refs) // per_x
     rows = devices * own
-    refs = (x0, x1, x2, x3)
 
     x_tiles = tiles_of(refs, per_x, devices, own)
     weights = jnp.concatenate(
         [piece(refs, per_x, j, 3 * own, W_ROWS) for j in range(devices)], 0
     )
 
-    def mixing(pick, spread, keep):
-        of_row = mul(pick[...], weights, NT).astype(bf16) * valid_ref[...]
-        return mul(of_row, spread[...]).astype(bf16) * keep[...]
-
-    mix1 = mixing(pick1_ref, spread1_ref, keep1_ref)
-    mix2 = mixing(pick2_ref, spread2_ref, keep2_ref)
-    back_ref[...] = mix2[:, : 2 * own]
-
-    first = mul(mix1, jnp.concatenate(x_tiles, 1)).astype(bf16)
-    spectral = mul(mix2, first).astype(bf16)
+    packed_x = jnp.concatenate(x_tiles, 1)
+    half_rows, half_w = rows // 2, weights.shape[0] // 2
+    halves = [slice(0, half_rows), slice(half_rows, rows)]
+    factors = [weights[:half_w], weights[half_w:]]
+    picked = [
+        [mul(pick[...], f, NT).astype(bf16) * valid_ref[...] for f in factors]
+        for pick in (pick1_ref, pick2_ref)
+    ]
+    mix1 = [mul(p, spread1_ref[...]).astype(bf16) * keep1_ref[...] for p in picked[0]]
+    mix2 = [
+        mul(p, spread2_ref[...]).astype(bf16) * keep2_ref[here, :]
+        for p, here in zip(picked[1], halves)
+    ]
+    first = jnp.concatenate([mul(m, packed_x[here]).astype(bf16) for m, here in zip(mix1, halves)], 0)
+    spectral = jnp.concatenate([mul(m, first).astype(bf16) for m in mix2], 0)
+    for m, here in zip(mix2, halves):
+        back_ref[here, :] = m[:, : 2 * own]
     sp_low, sp_high = unpacked(*cut(spectral))
-    sp_ref[:rows, :] = sp_low
-    sp_ref[rows:, :] = sp_high
     sp_own_ref[:own, :], sp_own_ref[own:, :] = sp_low[:own], sp_high[:own]
     own_ref[:own, :], own_ref[own:, :] = unpacked(*[tile[:own] for tile in x_tiles])
 
@@ -323,32 +353,35 @@
         *cut(mul(chosen_ref[...], first).astype(bf16))
     )
 
-    @pl.loop(0, 2 * rows // CHUNK)
-    def _(i):
-        here = pl.ds(pl.multiple_of(i * CHUNK, CHUNK), CHUNK)
-        sp = sp_ref[here, :]
-        gelu_out, slope = gelu_and_slope(mul(sp, w_in_ref[...]))
-        hid_ref[here, :] = gelu_out.astype(bf16)
-        slope_ref[here, :] = slope
-        spt_ref[:, here] = sp.T
+    sp = jnp.concatenate([sp_low, sp_high], 0)
+    gelu_out, slope = gelu_and_slope(mul(sp, w_in_ref[...]))
+    hid_ref[...] = gelu_out.astype(bf16)
+    slope_ref[...] = slope
+    spt_ref[...] = sp.T
 
 
 def backward_kernel(
     d0, d1, d2, d3, hid_ref, slope_ref, spt_ref, back_ref, first_ref, own_ref, sp_own_ref,
-    s_ref, w_in_ref, w_out_ref,
+    s_ref, w_in_t_ref, w_out_ref,
     enh_ref, g1_ref, g2_ref, gwi_ref, gwo_ref,
-    dm_ref, dsp_ref,
 ):
     bins, block = g1_ref.shape
     frames, _, channels = s_ref.shape
     half_c = channels // 2
     own = own_ref.shape[0] // 2
-    devices = 4 * d0.shape[0] // (3 * own)
+    refs = (d0, d1, d2, d3)
+    devices = sum(ref.shape[0] for ref in refs) // (3 * own)
     rows = devices * own
     at = Rows(own, bins)
-    dm_low, dm_high = unpacked(*tiles_of((d0, d1, d2, d3), 3 * own, devices, own))
-    dm_ref[:rows, :] = dm_low
-    dm_ref[rows:, :] = dm_high
+    dm_low, dm_high = unpacked(*tiles_of(refs, 3 * own, devices, own))
+    dpre, dsp = [], []
+    for n, part in enumerate((dm_low, dm_high)):
+        to = slice(n * rows, (n + 1) * rows)
+        dpre.append((mul(part, w_out_ref[...]) * slope_ref[to, :]).astype(bf16))
+    for n, part in enumerate((dm_low, dm_high)):
+        dsp.append((part.astype(f32) + mul(dpre[n], w_in_t_ref[...])).astype(bf16))
+    gwi_ref[...] = mul(spt_ref[:, :rows], dpre[0]) + mul(spt_ref[:, rows:], dpre[1])
+    gwo_ref[...] = mul(dm_low, hid_ref[:rows, :], TN) + mul(dm_high, hid_ref[rows:, :], TN)
 
     sp_own = sp_own_ref[...]
     hidden = jnp.concatenate([hid_ref[:own, :], hid_ref[rows : rows + own, :]], 0)
@@ -361,19 +394,7 @@
     )
     enh_ref[...] = enhanced.reshape(frames, bins, channels).astype(bf16)
 
-    gwi_ref[...] = jnp.zeros_like(gwi_ref)
-    gwo_ref[...] = jnp.zeros_like(gwo_ref)
-
-    @pl.loop(0, 2 * rows // CHUNK)
-    def _(i):
-        here = pl.ds(pl.multiple_of(i * CHUNK, CHUNK), CHUNK)
-        dm = dm_ref[here, :]
-        dpre = (mul(dm, w_out_ref[...]) * slope_ref[here, :]).astype(bf16)
-        gwo_ref[...] += mul(dm, hid_ref[here, :], TN)
-        gwi_ref[...] += mul(spt_ref[:, here], dpre)
-        dsp_ref[here, :] = (dm.astype(f32) + mul(dpre, w_in_ref[...], NT)).astype(bf16)
-
-    dsp_low, dsp_high = dsp_ref[:rows, :], dsp_ref[rows:, :]
+    dsp_low, dsp_high = dsp
     dfirst_low = mul(back_ref[...], dsp_low, TN).astype(bf16)
     dfirst_high = mul(back_ref[...], dsp_high, TN).astype(bf16)
 
@@ -412,49 +433,58 @@
     shaped = jax.ShapeDtypeStruct
     params = pltpu.CompilerParams(vmem_limit_bytes=40 * 2**20)
     scale = 1.0 / math.sqrt(frames * devices * bins)
-    own_rows, spec_in = pl.pallas_call(
+    own_rows, spec_in, w_in_in, w_out_in = pl.pallas_call(
         functools.partial(pack_kernel, scale=scale),
         out_shape=(
             pltpu.VMEM((6 * own + W_ROWS, LANES), bf16),
             pltpu.VMEM((frames, bins, channels), bf16),
+            pltpu.VMEM((channels, hid), bf16),
+            pltpu.VMEM((channels, hid), bf16),
         ),
-        in_specs=in_vmem(5),
-        out_specs=tuple(in_vmem(2)),
+        in_specs=in_hbm(7),
+        out_specs=tuple(in_vmem(4)),
+        scratch_shapes=[
+            pltpu.VMEM((frames, bins, channels), bf16),
+            pltpu.VMEM((frames, bins, channels), bf16),
+            pltpu.VMEM((bins, block), bf16),
+            pltpu.VMEM((bins, block), bf16),
+            pltpu.SemaphoreType.DMA((7,)),
+        ],
         name="pack",
-    )(features, spectrum, cotangent, w_first, w_second)
+    )(features, spectrum, cotangent, w_first, w_second, w_in, w_out.T)
     w_rows = devices * W_ROWS
-    x_own, d_own, w_in_in, w_out_in, *selections = pl.pallas_call(
+    x_own, d_own, w_in_t, *selections = pl.pallas_call(
         functools.partial(prepare_kernel, bins=bins),
         out_shape=tuple(
             pltpu.VMEM(shape, bf16)
             for shape in [
                 (3 * own + W_ROWS, LANES),
                 (3 * own, LANES),
-                (channels, hid),
-                (channels, hid),
-                (rows, w_rows),
-                (rows, LANES),
-                (w_rows, rows),
-                (rows, rows),
-                (rows, LANES),
-                (w_rows, rows),
+                (hid, channels),
+                (rows // 2, w_rows // 2),
+                (rows // 2, LANES),
+                (w_rows // 2, rows // 2),
+                (rows // 2, rows // 2),
+                (rows // 2, LANES),
+                (w_rows // 2, rows),
                 (rows, rows),
                 (own, rows),
             ]
         ),
-        in_specs=in_vmem(1) + in_hbm(2),
-        out_specs=tuple(in_vmem(12)),
-        scratch_shapes=[pltpu.SemaphoreType.DMA((2,))],
+        in_specs=in_vmem(2),
+        out_specs=tuple(in_vmem(11)),
         compiler_params=params,
         cost_estimate=pl.CostEstimate(flops=0, bytes_accessed=2**21, transcendentals=0),
         name="prepare",
-    )(own_rows, w_in, w_out.T)
-
-    columns = [exchanged(own_rows, j) for j in range(devices - 4, 0, -4)][::-1]
+    )(own_rows, w_in_in)
+
+    column = [exchanged(own_rows, j) for j in range(devices - 4, 0, -4)]
     x_rows = 3 * own + W_ROWS
-    x0 = jnp.concatenate([x_own] + [column[:x_rows] for column in columns], 0)
-    d0 = jnp.concatenate([d_own] + [column[x_rows:] for column in columns], 0)
-    x2, d2 = exchanged(x0, 2), exchanged(d0, 2)
+    x_column = jnp.concatenate([*[got[:x_rows] for got in column], x_own], 0)
+    d_column = jnp.concatenate([*[got[x_rows:] for got in column], d_own], 0)
+    x2, d2 = exchanged(x_column, 2), exchanged(d_column, 2)
+    x0 = x_column
+    d0 = d_column
     x1, d1 = exchanged(x0, 1), exchanged(d0, 1)
     x3, d3 = exchanged(x2, 1), exchanged(d2, 1)
 
@@ -471,7 +501,6 @@
         ),
         in_specs=in_vmem(13),
         out_specs=tuple(in_vmem(7)),
-        scratch_shapes=[pltpu.VMEM((2 * rows, channels), bf16)],
         compiler_params=params,
         name="forward",
     )(x0, x1, x2, x3, w_in_in, *selections)
@@ -487,10 +516,9 @@
         ),
         in_specs=in_vmem(14),
         out_specs=tuple(in_vmem(5)),
-        scratch_shapes=[pltpu.VMEM((2 * rows, channels), bf16)] * 2,
         compiler_params=params,
         name="backward",
-    )(d0, d1, d2, d3, *kept, spec_in, w_in_in, w_out_in)
+    )(d0, d1, d2, d3, *kept, spec_in, w_in_t, w_out_in)
     return enhanced, grad_first, grad_second, grad_w_in, grad_w_out.T
 
 

time: 24.7 us -> 22.9 us (0.927)
  local copies, waits for them, and re-layouts: 1.84 us -> 0.02 us
  waiting for transfers between devices: 6.73 us -> 7.83 us
  Pallas kernels: 6.81 us -> 5.76 us
    unnamed x4 -> x0, local copies, waits for them, and re-layouts: 1.82 us -> none
    ppermute x9, waiting for transfers between devices: 6.73 us -> 7.83 us  [exchanged(): return lax.ppermute(value, 'freq', pairs)]
    pallas_call x1, Pallas kernels: 0.96 us -> 0.44 us  [whole_rows(): pl.pallas_call(functools.partial(prepare_kernel, bins=bins), out_shape=tu...]
    pallas_call x1, Pallas kernels: 2.15 us -> 1.81 us  [whole_rows(): pl.pallas_call(forward_kernel, out_shape=(shaped((2 * rows, hid), bf16),...]
    pallas_call x1, Pallas kernels: 2.67 us -> 2.38 us  [whole_rows(): pl.pallas_call(backward_kernel, out_shape=(shaped((frames, bins, channels...]
  transfers between devices with their start and end apart: 9 -> 9, of which waited for: 4 -> 5; matrix products, arithmetic and copies ran while one was open for 0% -> 0% of each run, Pallas kernels for 13% -> 10%
where the time goes in v3:
time: 22.9 us; the launch traced here: 22.8 us
  starting transfers between devices  8.43 us (37%)
  waiting for transfers between devices  7.83 us (34%)
  Pallas kernels  5.76 us (25%)
  between operations  0.7 us (3%)
    ppermute x9, starting transfers between devices, exchanged(): return lax.ppermute(value, 'freq', pairs)  8.43 us
    ppermute x9, waiting for transfers between devices, exchanged(): return lax.ppermute(value, 'freq', pairs)  7.83 us
    pallas_call x1, Pallas kernels, whole_rows(): pl.pallas_call(backward_kernel, out_shape=(shaped((frames, bins, channels...  2.38 us
    pallas_call x1, Pallas kernels, whole_rows(): pl.pallas_call(forward_kernel, out_shape=(shaped((2 * rows, hid), bf16),...  1.81 us
    pallas_call x1, Pallas kernels, whole_rows(): pl.pallas_call(functools.partial(pack_kernel, scale=scale), out_shape=(pl...  1.13 us
  transfers between devices with their start and end apart: 9, of which 5 were waited for; matrix products, arithmetic and copies ran while one was open for 0% of the time, Pallas kernels for 10%

profile of v3, /device:TPU:0, one launch (start us, length us, event | category | flops | bytes accessed | tf_op | source)
XLA Modules:
  0.0 22.8 jit_solution(9550347642904592711)
XLA Ops:
  0.6 1.1 %pack.1 = (bf16[208,128]{1,0:T(8,128)(2,1)S(1)}, bf16[16,4,192]{2,1,0:T(4,128)(2,1)S(1)}, bf16[192,384]{1,0:T(8,128)(2,1)S(1)}, bf16[192,384]{1,0:T(8,128)(2,1)S(1)}) custom-call(bf16[16,4,192]{2,1,0:T(4,128)(2,1)} %x_hbm.1, bf16[16,4,192]{2,1,0:T(4,128)(2,1)} %s_hbm.1, bf16[16,4,192]{2,1,0:T(4,128)(2,1)} %c_hbm.1, bf16[4,8]{1,0:T(4,128)(2,1)} %w1_hbm.1, ...), custom_call_target="tpu_custom_call" | custom-call | tf_op jit(solution)/shard_map/pack/pallas_call | solution.py:436
  1.8 5.1 %collective-permute-start = (bf16[208,128]{1,0:T(8,128)(2,1)S(1)}, bf16[208,128]{1,0:T(8,128)(2,1)S(1)}, u32[]{:S(2)}, u32[]{:S(2)}) collective-permute-start(bf16[208,128]{1,0:T(8,128)(2,1)S(1)} %get-tuple-element.32.own_ref), channel_id=1, source_target_pairs={{0,12},{1,13},{2,14},{3,15},{4,8},{5,9},{6,10},{7,11},{8,4},{9,5},... | collective-permute-start | bytes 159752 | tf_op jit(solution)/shard_map/ppermute | solution.py:527
  6.9 0.0 collective-permute-start.1
  6.9 0.6 %collective-permute-start.2 = (bf16[208,128]{1,0:T(8,128)(2,1)S(1)}, bf16[208,128]{1,0:T(8,128)(2,1)S(1)}, u32[]{:S(2)}, u32[]{:S(2)}) collective-permute-start(bf16[208,128]{1,0:T(8,128)(2,1)S(1)} %get-tuple-element.32.own_ref), channel_id=1, source_target_pairs={{0,4},{1,5},{2,6},{3,7},{4,0},{5,1},{6,2},{7,3},{8,12},{9,13},{10,... | collective-permute-start | bytes 159752 | tf_op jit(solution)/shard_map/ppermute | solution.py:527
  7.5 0.4 %prepare.1 = (bf16[112,128]{1,0:T(8,128)(2,1)S(1)}, bf16[96,128]{1,0:T(8,128)(2,1)S(1)}, bf16[384,192]{1,0:T(8,128)(2,1)S(1)}, bf16[256,128]{1,0:T(8,128)(2,1)S(...) custom-call(bf16[208,128]{1,0:T(8,128)(2,1)S(1)} %get-tuple-element., ...), custom_call_target="tpu_custom_call" | custom-call | bytes 2097152 | tf_op jit(solution)/shard_map/prepare/pallas_call | solution.py:456
  8.0 1.2 %collective-permute-done = bf16[208,128]{1,0:T(8,128)(2,1)S(1)} collective-permute-done((bf16[208,128]{1,0:T(8,128)(2,1)S(1)}, bf16[208,128]{1,0:T(8,128)(2,1)S(1)}, u32[]{:S(2)}, u32[]{:S(2)}) %collective-permute-start) | collective-permute-done | bytes 53280 | tf_op jit(solution)/shard_map/ppermute | solution.py:527
  9.2 2.7 %collective-permute-done.1 = bf16[208,128]{1,0:T(8,128)(2,1)S(1)} collective-permute-done((bf16[208,128]{1,0:T(8,128)(2,1)S(1)}, bf16[208,128]{1,0:T(8,128)(2,1)S(1)}, u32[]{:S(2)}, u32[]{:S(2)}) %collective-permute-start.1) | collective-permute-done | bytes 53280 | tf_op jit(solution)/shard_map/ppermute | solution.py:527
  11.9 0.0 collective-permute-done.2
  12.0 1.6 %collective-permute-start.7 = (bf16[448,128]{1,0:T(8,128)(2,1)S(1)}, bf16[448,128]{1,0:T(8,128)(2,1)S(1)}, u32[]{:S(2)}, u32[]{:S(2)}) collective-permute-start(bf16[448,128]{1,0:T(8,128)(2,1)S(1)} %pad_maximum_fusion.x0), channel_id=1, source_target_pairs={{0,2},{1,3},{2,0},{3,1},{4,6},{5,7},{6,4},{7,5},{8,10},{9,11},{10,... | collective-permute-start | bytes 344072 | tf_op jit(solution)/shard_map/ppermute | solution.py:527
  13.6 0.6 %collective-permute-start.4 = (bf16[384,128]{1,0:T(8,128)(2,1)S(1)}, bf16[384,128]{1,0:T(8,128)(2,1)S(1)}, u32[]{:S(2)}, u32[]{:S(2)}) collective-permute-start(bf16[384,128]{1,0:T(8,128)(2,1)S(1)} %pad_maximum_fusion.1.d0), channel_id=1, source_target_pairs={{0,2},{1,3},{2,0},{3,1},{4,6},{5,7},{6,4},{7,5},{8,10},{9,11},{10,... | collective-permute-start | bytes 294920 | tf_op jit(solution)/shard_map/ppermute | solution.py:527
  14.1 0.0 collective-permute-start.6
  14.1 3.1 %collective-permute-done.7.x2 = bf16[448,128]{1,0:T(8,128)(2,1)S(1)} collective-permute-done((bf16[448,128]{1,0:T(8,128)(2,1)S(1)}, bf16[448,128]{1,0:T(8,128)(2,1)S(1)}, u32[]{:S(2)}, u32[]{:S(2)}) %collective-permute-start.7) | collective-permute-done | bytes 114720 | tf_op jit(solution)/shard_map/ppermute | solution.py:527
  17.2 0.0 collective-permute-start.8
  17.2 0.5 %collective-permute-start.3 = (bf16[384,128]{1,0:T(8,128)(2,1)S(1)}, bf16[384,128]{1,0:T(8,128)(2,1)S(1)}, u32[]{:S(2)}, u32[]{:S(2)}) collective-permute-start(bf16[384,128]{1,0:T(8,128)(2,1)S(1)} %pad_maximum_fusion.1.d0), channel_id=1, source_target_pairs={{0,1},{1,0},{2,3},{3,2},{4,5},{5,4},{6,7},{7,6},{8,9},{9,8},{10,11... | collective-permute-start | bytes 294920 | tf_op jit(solution)/shard_map/ppermute | solution.py:527
  17.7 0.5 %collective-permute-done.4.d2 = bf16[384,128]{1,0:T(8,128)(2,1)S(1)} collective-permute-done((bf16[384,128]{1,0:T(8,128)(2,1)S(1)}, bf16[384,128]{1,0:T(8,128)(2,1)S(1)}, u32[]{:S(2)}, u32[]{:S(2)}) %collective-permute-start.4) | collective-permute-done | bytes 98336 | tf_op jit(solution)/shard_map/ppermute | solution.py:527
  18.3 0.0 collective-permute-start.5
  18.3 0.0 collective-permute-done.6.x1
  18.3 0.3 %collective-permute-done.8.x3 = bf16[448,128]{1,0:T(8,128)(2,1)S(1)} collective-permute-done((bf16[448,128]{1,0:T(8,128)(2,1)S(1)}, bf16[448,128]{1,0:T(8,128)(2,1)S(1)}, u32[]{:S(2)}, u32[]{:S(2)}) %collective-permute-start.8) | collective-permute-done | bytes 114720 | tf_op jit(solution)/shard_map/ppermute | solution.py:527
  18.5 1.8 %forward.1 = (bf16[1024,384]{1,0:T(8,128)(2,1)S(1)}, f32[1024,384]{1,0:T(8,128)S(1)}, bf16[192,1024]{1,0:T(8,128)(2,1)S(1)}, bf16[512,64]{1,0:T(8,128)(2,1)S(1)}...) custom-call(bf16[448,128]{1,0:T(8,128)(2,1)S(1)} %pad_maximum_fusion.x0, ...), custom_call_target="tpu_custom_call" | custom-call | tf_op jit(solution)/shard_map/forward/pallas_call | solution.py:491
  20.4 0.0 collective-permute-done.3.d1
  20.4 0.0 collective-permute-done.5.d3
  20.4 2.4 %backward.1 = (bf16[16,4,192]{2,1,0:T(4,128)(2,1)}, f32[4,8]{1,0:T(4,128)}, f32[4,8]{1,0:T(4,128)}, f32[192,384]{1,0:T(8,128)}, f32[192,384]{1,0:T(8,128)}) custom-call(bf16[384,128]{1,0:T(8,128)(2,1)S(1)} %pad_maximum_fusion.1.d0, bf16[384,128]{1,0:T(8,128)(2,1)S(1)} %collective-permute-done.3.d1, bf16[384,128]{1,0:T(8,128)(2,1)S(1)} %collective-permute-done.4.d2, ...), custom_call_target="tpu_custom_call" | custom-call | tf_op jit(solution)/shard_map/backward/pallas_call | solution.py:508
  (8 shorter events, 0.0 us)
Async XLA Ops:
  1.8 7.4 %collective-permute-start = (bf16[208,128]{1,0:T(8,128)(2,1)S(1)}, bf16[208,128]{1,0:T(8,128)(2,1)S(1)}, u32[]{:S(2)}, u32[]{:S(2)}) collective-permute-start(bf16[208,128]{1,0:T(8,128)(2,1)S(1)} %get-tuple-element.32.own_ref), channel_id=1, source_target_pairs={{0,12},{1,13},{2,14},{3,15},{4,8},{5,9},{6,10},{7,11},{8,4},{9,5},... | collective-permute-start | bytes 159752 | tf_op jit(solution)/shard_map/ppermute | solution.py:527
  6.9 5.0 %collective-permute-start.1 = (bf16[208,128]{1,0:T(8,128)(2,1)S(1)}, bf16[208,128]{1,0:T(8,128)(2,1)S(1)}, u32[]{:S(2)}, u32[]{:S(2)}) collective-permute-start(bf16[208,128]{1,0:T(8,128)(2,1)S(1)} %get-tuple-element.32.own_ref), channel_id=1, source_target_pairs={{0,8},{1,9},{2,10},{3,11},{4,12},{5,13},{6,14},{7,15},{8,0},{9,1},... | collective-permute-start | bytes 159752 | tf_op jit(solution)/shard_map/ppermute | solution.py:527
  6.9 5.0 %collective-permute-start.2 = (bf16[208,128]{1,0:T(8,128)(2,1)S(1)}, bf16[208,128]{1,0:T(8,128)(2,1)S(1)}, u32[]{:S(2)}, u32[]{:S(2)}) collective-permute-start(bf16[208,128]{1,0:T(8,128)(2,1)S(1)} %get-tuple-element.32.own_ref), channel_id=1, source_target_pairs={{0,4},{1,5},{2,6},{3,7},{4,0},{5,1},{6,2},{7,3},{8,12},{9,13},{10,... | collective-permute-start | bytes 159752 | tf_op jit(solution)/shard_map/ppermute | solution.py:527
  12.0 5.3 %collective-permute-start.7 = (bf16[448,128]{1,0:T(8,128)(2,1)S(1)}, bf16[448,128]{1,0:T(8,128)(2,1)S(1)}, u32[]{:S(2)}, u32[]{:S(2)}) collective-permute-start(bf16[448,128]{1,0:T(8,128)(2,1)S(1)} %pad_maximum_fusion.x0), channel_id=1, source_target_pairs={{0,2},{1,3},{2,0},{3,1},{4,6},{5,7},{6,4},{7,5},{8,10},{9,11},{10,... | collective-permute-start | bytes 344072 | tf_op jit(solution)/shard_map/ppermute | solution.py:527
  13.6 4.7 %collective-permute-start.4 = (bf16[384,128]{1,0:T(8,128)(2,1)S(1)}, bf16[384,128]{1,0:T(8,128)(2,1)S(1)}, u32[]{:S(2)}, u32[]{:S(2)}) collective-permute-start(bf16[384,128]{1,0:T(8,128)(2,1)S(1)} %pad_maximum_fusion.1.d0), channel_id=1, source_target_pairs={{0,2},{1,3},{2,0},{3,1},{4,6},{5,7},{6,4},{7,5},{8,10},{9,11},{10,... | collective-permute-start | bytes 294920 | tf_op jit(solution)/shard_map/ppermute | solution.py:527
  14.1 4.1 %collective-permute-start.6 = (bf16[448,128]{1,0:T(8,128)(2,1)S(1)}, bf16[448,128]{1,0:T(8,128)(2,1)S(1)}, u32[]{:S(2)}, u32[]{:S(2)}) collective-permute-start(bf16[448,128]{1,0:T(8,128)(2,1)S(1)} %pad_maximum_fusion.x0), channel_id=1, source_target_pairs={{0,1},{1,0},{2,3},{3,2},{4,5},{5,4},{6,7},{7,6},{8,9},{9,8},{10,11... | collective-permute-start | bytes 344072 | tf_op jit(solution)/shard_map/ppermute | solution.py:527
  17.2 1.3 %collective-permute-start.8 = (bf16[448,128]{1,0:T(8,128)(2,1)S(1)}, bf16[448,128]{1,0:T(8,128)(2,1)S(1)}, u32[]{:S(2)}, u32[]{:S(2)}) collective-permute-start(bf16[448,128]{1,0:T(8,128)(2,1)S(1)} %collective-permute-done.7.x2), channel_id=1, source_target_pairs={{0,1},{1,0},{2,3},{3,2},{4,5},{5,4},{6,7},{7,6},{8,9},{9,8},{10,11... | collective-permute-start | bytes 344072 | tf_op jit(solution)/shard_map/ppermute | solution.py:527
  17.2 3.1 %collective-permute-start.3 = (bf16[384,128]{1,0:T(8,128)(2,1)S(1)}, bf16[384,128]{1,0:T(8,128)(2,1)S(1)}, u32[]{:S(2)}, u32[]{:S(2)}) collective-permute-start(bf16[384,128]{1,0:T(8,128)(2,1)S(1)} %pad_maximum_fusion.1.d0), channel_id=1, source_target_pairs={{0,1},{1,0},{2,3},{3,2},{4,5},{5,4},{6,7},{7,6},{8,9},{9,8},{10,11... | collective-permute-start | bytes 294920 | tf_op jit(solution)/shard_map/ppermute | solution.py:527
  18.3 2.1 %collective-permute-start.5 = (bf16[384,128]{1,0:T(8,128)(2,1)S(1)}, bf16[384,128]{1,0:T(8,128)(2,1)S(1)}, u32[]{:S(2)}, u32[]{:S(2)}) collective-permute-start(bf16[384,128]{1,0:T(8,128)(2,1)S(1)} %collective-permute-done.4.d2), channel_id=1, source_target_pairs={{0,1},{1,0},{2,3},{3,2},{4,5},{5,4},{6,7},{7,6},{8,9},{9,8},{10,11... | collective-permute-start | bytes 294920 | tf_op jit(solution)/shard_map/ppermute | solution.py:527

commit v4 on v3

--- a/solution.py
+++ b/solution.py
@@ -162,13 +162,18 @@
 
 
 class Rows:
-    def __init__(self, own, bins):
+    def __init__(self, own, bins, rows):
         self.own, self.bins, self.per_block = own, bins, 2 * own
+        self.half = rows // (2 * self.per_block)
         me = lax.axis_index("freq")
         self.chip, self.side = me >> 1, (me & 1) * bins
 
+    def local(self, r):
+        return r // self.per_block
+
     def block(self, r):
-        return r // self.per_block
+        k = self.local(r)
+        return ((k & (self.half - 1)) << 1) | (k // self.half)
 
     def place(self, r):
         return ((r // self.own) & 1) * self.bins + (r & (self.bins - 1))
@@ -198,20 +203,24 @@
 
 def received_from(devices):
     column = [*range(devices - 4, 0, -4)]
-    near, far = [*column, 0], [j ^ 2 for j in [*column, 0]]
+    near, far = [*column, 0, 2], [j ^ 2 for j in column]
     return [near, [j ^ 1 for j in near], far, [j ^ 1 for j in far]]
 
 
-def piece(refs, per_device, j, start, size):
-    held = received_from(sum(ref.shape[0] for ref in refs) // per_device)
+def piece(refs, per_device, devices, j, start, size):
+    held = received_from(devices)
     n = next(n for n, part in enumerate(held) if j in part)
     at = held[n].index(j) * per_device + start
     return refs[n][at : at + size, :]
 
 
-def tiles_of(refs, per_device, devices, own):
+def halves_of(devices):
+    return [[j for j in range(devices) if j & 2 == bit] for bit in (0, 2)]
+
+
+def tiles_of(refs, per_device, devices, own, order):
     return [
-        jnp.concatenate([piece(refs, per_device, j, t * own, own) for j in range(devices)], 0)
+        jnp.concatenate([piece(refs, per_device, devices, j, t * own, own) for j in order], 0)
         for t in range(3)
     ]
 
@@ -277,7 +286,7 @@
     d_ref[...] = own_ref[x_ref.shape[0] :, :]
     own, rows = chosen_ref.shape
     block = 2 * bins
-    at = Rows(own, bins)
+    at = Rows(own, bins, rows)
 
     def w_place(r):
         return ((r // W_ROWS) & 1) * bins + (r & (W_ROWS - 1))
@@ -286,14 +295,14 @@
         return r // (2 * W_ROWS)
 
     r, w = iota(valid_ref.shape, 0), iota(valid_ref.shape, 1)
-    valid_ref[...] = onehot(((w & (W_ROWS - 1)) < bins) & (w_block(w) == at.block(r)))
+    valid_ref[...] = onehot(((w & (W_ROWS - 1)) < bins) & (w_block(w) == at.local(r)))
 
     r, lane = iota(pick1_ref.shape, 0), iota(pick1_ref.shape, 1)
     pick1_ref[...] = onehot(lane == at.place(r))
     pick2_ref[...] = onehot(lane == block + (at.place(r) ^ at.side))
 
     w, r = iota(spread1_ref.shape, 0), iota(spread1_ref.shape, 1)
-    spread1_ref[...] = onehot((w_place(w) == at.place(r)) & (w_block(w) == at.block(r)))
+    spread1_ref[...] = onehot((w_place(w) == at.place(r)) & (w_block(w) == at.local(r)))
     w, r = iota(spread2_ref.shape, 0), iota(spread2_ref.shape, 1)
     spread2_ref[...] = onehot(w_place(w) == (at.block(r) ^ at.chip ^ at.side))
 
@@ -312,48 +321,75 @@
     )
 
 
-def forward_kernel(
-    x0, x1, x2, x3, w_in_ref, valid_ref, pick1_ref, spread1_ref, keep1_ref,
-    pick2_ref, spread2_ref, keep2_ref, chosen_ref,
-    hid_ref, slope_ref, spt_ref, back_ref, first_ref, own_ref, sp_own_ref,
+def mixing(refs, devices, own, order, selections, keep2):
+    valid_ref, pick1_ref, spread1_ref, keep1_ref, pick2_ref, spread2_ref = selections
+    per_x = 3 * own + W_ROWS
+    factors = jnp.concatenate(
+        [piece(refs, per_x, devices, j, 3 * own, W_ROWS) for j in order], 0
+    )
+    tiles = tiles_of(refs, per_x, devices, own, order)
+    picked = [
+        mul(pick[...], factors, NT).astype(bf16) * valid_ref[...] for pick in (pick1_ref, pick2_ref)
+    ]
+    mix1 = mul(picked[0], spread1_ref[...]).astype(bf16) * keep1_ref[...]
+    mix2 = mul(picked[1], spread2_ref[...]).astype(bf16) * keep2
+    return tiles, mul(mix1, jnp.concatenate(tiles, 1)).astype(bf16), mix2
+
+
+def near_kernel(
+    x0, x1, valid_ref, pick1_ref, spread1_ref, keep1_ref, pick2_ref, spread2_ref, keep2_ref,
+    first_ref, mix2_ref, part_ref, own_ref, mark_ref,
 ):
     own = own_ref.shape[0] // 2
-    per_x = 3 * own + W_ROWS
-    refs = (x0, x1, x2, x3)
-    devices = sum(ref.shape[0] for ref in refs) // per_x
-    rows = devices * own
-
-    x_tiles = tiles_of(refs, per_x, devices, own)
-    weights = jnp.concatenate(
-        [piece(refs, per_x, j, 3 * own, W_ROWS) for j in range(devices)], 0
-    )
-
-    packed_x = jnp.concatenate(x_tiles, 1)
-    half_rows, half_w = rows // 2, weights.shape[0] // 2
-    halves = [slice(0, half_rows), slice(half_rows, rows)]
-    factors = [weights[:half_w], weights[half_w:]]
-    picked = [
-        [mul(pick[...], f, NT).astype(bf16) * valid_ref[...] for f in factors]
-        for pick in (pick1_ref, pick2_ref)
-    ]
-    mix1 = [mul(p, spread1_ref[...]).astype(bf16) * keep1_ref[...] for p in picked[0]]
-    mix2 = [
-        mul(p, spread2_ref[...]).astype(bf16) * keep2_ref[here, :]
-        for p, here in zip(picked[1], halves)
-    ]
-    first = jnp.concatenate([mul(m, packed_x[here]).astype(bf16) for m, here in zip(mix1, halves)], 0)
-    spectral = jnp.concatenate([mul(m, first).astype(bf16) for m in mix2], 0)
-    for m, here in zip(mix2, halves):
-        back_ref[here, :] = m[:, : 2 * own]
+    half, rows = mix2_ref.shape
+    devices = rows // own
+    selections = (valid_ref, pick1_ref, spread1_ref, keep1_ref, pick2_ref, spread2_ref)
+    tiles, first, mix2 = mixing(
+        (x0, x1), devices, own, halves_of(devices)[0], selections, keep2_ref[:half, :]
+    )
+    first_ref[...] = first
+    mix2_ref[...] = mix2
+    part_ref[...] = mul(mix2[:, :half], first)
+    own_ref[:own, :], own_ref[own:, :] = unpacked(*[tile[:own] for tile in tiles])
+    mark_ref[...] = jnp.zeros_like(mark_ref)
+
+
+def mix_kernel(
+    x2, x3, x0, x1, first_near_ref, mix2_near_ref, part_ref,
+    valid_ref, pick1_ref, spread1_ref, keep1_ref,
+    pick2_ref, spread2_ref, keep2_ref, chosen_ref,
+    sp_ref, back_ref, first_ref, sp_own_ref, mark_ref,
+):
+    own = sp_own_ref.shape[0] // 2
+    half, rows = mix2_near_ref.shape
+    devices = rows // own
+    selections = (valid_ref, pick1_ref, spread1_ref, keep1_ref, pick2_ref, spread2_ref)
+    _, first_far, mix2_far = mixing(
+        (x0, x1, x2, x3), devices, own, halves_of(devices)[1], selections, keep2_ref[half:, :]
+    )
+    first = jnp.concatenate([first_near_ref[...], first_far], 0)
+    spectral = jnp.concatenate(
+        [
+            (part_ref[...] + mul(mix2_near_ref[:, half:], first_far)).astype(bf16),
+            mul(mix2_far, first).astype(bf16),
+        ],
+        0,
+    )
+    back_ref[:half, :] = mix2_near_ref[:, : 2 * own]
+    back_ref[half:, :] = mix2_far[:, : 2 * own]
     sp_low, sp_high = unpacked(*cut(spectral))
     sp_own_ref[:own, :], sp_own_ref[own:, :] = sp_low[:own], sp_high[:own]
-    own_ref[:own, :], own_ref[own:, :] = unpacked(*[tile[:own] for tile in x_tiles])
-
     first_ref[:own, :], first_ref[own:, :] = unpacked(
         *cut(mul(chosen_ref[...], first).astype(bf16))
     )
 
-    sp = jnp.concatenate([sp_low, sp_high], 0)
+    sp_ref[:rows, :] = sp_low
+    sp_ref[rows:, :] = sp_high
+    mark_ref[...] = jnp.zeros_like(mark_ref)
+
+
+def hidden_kernel(sp_ref, w_in_ref, hid_ref, slope_ref, spt_ref):
+    sp = sp_ref[...]
     gelu_out, slope = gelu_and_slope(mul(sp, w_in_ref[...]))
     hid_ref[...] = gelu_out.astype(bf16)
     slope_ref[...] = slope
@@ -361,7 +397,7 @@
 
 
 def backward_kernel(
-    d0, d1, d2, d3, hid_ref, slope_ref, spt_ref, back_ref, first_ref, own_ref, sp_own_ref,
+    hid_ref, slope_ref, spt_ref, back_ref, first_ref, sp_own_ref, own_ref, d2, d0, d1, d3,
     s_ref, w_in_t_ref, w_out_ref,
     enh_ref, g1_ref, g2_ref, gwi_ref, gwo_ref,
 ):
@@ -370,10 +406,11 @@
     half_c = channels // 2
     own = own_ref.shape[0] // 2
     refs = (d0, d1, d2, d3)
-    devices = sum(ref.shape[0] for ref in refs) // (3 * own)
-    rows = devices * own
-    at = Rows(own, bins)
-    dm_low, dm_high = unpacked(*tiles_of(refs, 3 * own, devices, own))
+    rows = hid_ref.shape[0] // 2
+    devices = rows // own
+    at = Rows(own, bins, rows)
+    order = sum(halves_of(devices), [])
+    dm_low, dm_high = unpacked(*tiles_of(refs, 3 * own, devices, own, order))
     dpre, dsp = [], []
     for n, part in enumerate((dm_low, dm_high)):
         to = slice(n * rows, (n + 1) * rows)
@@ -480,30 +517,58 @@
 
     column = [exchanged(own_rows, j) for j in range(devices - 4, 0, -4)]
     x_rows = 3 * own + W_ROWS
-    x_column = jnp.concatenate([*[got[:x_rows] for got in column], x_own], 0)
-    d_column = jnp.concatenate([*[got[x_rows:] for got in column], d_own], 0)
+    across = exchanged(own_rows, 2)
+    x_column = jnp.concatenate([got[:x_rows] for got in column], 0)
+    d_column = jnp.concatenate([got[x_rows:] for got in column], 0)
     x2, d2 = exchanged(x_column, 2), exchanged(d_column, 2)
-    x0 = x_column
-    d0 = d_column
+    x0 = jnp.concatenate([x_column, x_own, across[:x_rows]], 0)
+    d0 = jnp.concatenate([d_column, d_own, across[x_rows:]], 0)
     x1, d1 = exchanged(x0, 1), exchanged(d0, 1)
-    x3, d3 = exchanged(x2, 1), exchanged(d2, 1)
-
-    kept = pl.pallas_call(
-        forward_kernel,
+    first_near, mix2_near, part, x_rows_own, mark = pl.pallas_call(
+        near_kernel,
         out_shape=(
-            shaped((2 * rows, hid), bf16),
-            shaped((2 * rows, hid), f32),
-            shaped((channels, 2 * rows), bf16),
-            shaped((rows, 2 * own), bf16),
-            shaped((2 * own, channels), bf16),
-            shaped((2 * own, channels), bf16),
-            shaped((2 * own, channels), bf16),
+            pltpu.VMEM((rows // 2, 2 * channels), bf16),
+            pltpu.VMEM((rows // 2, rows), bf16),
+            pltpu.VMEM((rows // 2, 2 * channels), f32),
+            pltpu.VMEM((2 * own, channels), bf16),
+            pltpu.VMEM((W_ROWS, LANES), bf16),
         ),
-        in_specs=in_vmem(13),
-        out_specs=tuple(in_vmem(7)),
+        in_specs=in_vmem(9),
+        out_specs=tuple(in_vmem(5)),
         compiler_params=params,
-        name="forward",
-    )(x0, x1, x2, x3, w_in_in, *selections)
+        name="near",
+    )(x0, x1, *selections[:-1])
+    x3 = exchanged(jnp.concatenate([x2, mark], 0), 1)
+    spectral, *kept, mark = pl.pallas_call(
+        mix_kernel,
+        out_shape=tuple(
+            pltpu.VMEM(shape, bf16)
+            for shape in [
+                (2 * rows, channels),
+                (rows, 2 * own),
+                (2 * own, channels),
+                (2 * own, channels),
+                (W_ROWS, LANES),
+            ]
+        ),
+        in_specs=in_vmem(15),
+        out_specs=tuple(in_vmem(5)),
+        compiler_params=params,
+        name="mix",
+    )(x2, x3, x0, x1, first_near, mix2_near, part, *selections)
+    d3 = exchanged(jnp.concatenate([d2, mark], 0), 1)
+    hidden = pl.pallas_call(
+        hidden_kernel,
+        out_shape=(
+            pltpu.VMEM((2 * rows, hid), bf16),
+            pltpu.VMEM((2 * rows, hid), f32),
+            pltpu.VMEM((channels, 2 * rows), bf16),
+        ),
+        in_specs=in_vmem(2),
+        out_specs=tuple(in_vmem(3)),
+        compiler_params=params,
+        name="hidden",
+    )(spectral, w_in_in)
 
     enhanced, grad_first, grad_second, grad_w_in, grad_w_out = pl.pallas_call(
         backward_kernel,
@@ -518,7 +583,7 @@
         out_specs=tuple(in_vmem(5)),
         compiler_params=params,
         name="backward",
-    )(d0, d1, d2, d3, *kept, spec_in, w_in_t, w_out_in)
+    )(*hidden, *kept, x_rows_own, d2, d0, d1, d3, spec_in, w_in_t, w_out_in)
     return enhanced, grad_first, grad_second, grad_w_in, grad_w_out.T
 
 

time: 22.9 us -> 22.8 us (level)
  waiting for transfers between devices: 7.83 us -> 4.69 us
  starting transfers between devices: 8.43 us -> 10.4 us
  Pallas kernels: 5.76 us -> 6.58 us
    ppermute x9 -> x10, waiting for transfers between devices: 7.83 us -> 4.69 us  [exchanged(): return lax.ppermute(value, 'freq', pairs)]
    ppermute x9 -> x10, starting transfers between devices: 8.43 us -> 10.4 us  [exchanged(): return lax.ppermute(value, 'freq', pairs)]
    pallas_call x1 -> x3, Pallas kernels: 1.81 us -> 2.57 us  [the longest x1 0.96 us: whole_rows(): pl.pallas_call(mix_kernel, out_shape=tuple((pltpu.VMEM(shape, bf16) for s...]
  transfers between devices with their start and end apart: 9 -> 10, of which waited for: 5 -> 5; matrix products, arithmetic and copies ran while one was open for 0% -> 1% of each run, Pallas kernels for 10% -> 14%
where the time goes in v4:
time: 22.8 us; the launch traced here: 22.6 us
  starting transfers between devices  10.4 us (46%)
  Pallas kernels  6.58 us (29%)
  waiting for transfers between devices  4.69 us (21%)
  between operations  0.78 us (3%)
    ppermute x10, starting transfers between devices, exchanged(): return lax.ppermute(value, 'freq', pairs)  10.4 us
    ppermute x10, waiting for transfers between devices, exchanged(): return lax.ppermute(value, 'freq', pairs)  4.69 us
    pallas_call x1, Pallas kernels, whole_rows(): pl.pallas_call(backward_kernel, out_shape=(shaped((frames, bins, channels...  2.39 us
    pallas_call x1, Pallas kernels, whole_rows(): pl.pallas_call(functools.partial(pack_kernel, scale=scale), out_shape=(pl...  1.13 us
    pallas_call x1, Pallas kernels, whole_rows(): pl.pallas_call(mix_kernel, out_shape=tuple((pltpu.VMEM(shape, bf16) for s...  0.96 us
    pallas_call x1, Pallas kernels, whole_rows(): pl.pallas_call(hidden_kernel, out_shape=(pltpu.VMEM((2 * rows, hid), bf16...  0.93 us
    pallas_call x1, Pallas kernels, whole_rows(): pl.pallas_call(near_kernel, out_shape=(pltpu.VMEM((rows // 2, 2 * channel...  0.68 us
    pallas_call x1, Pallas kernels, whole_rows(): pl.pallas_call(functools.partial(prepare_kernel, bins=bins), out_shape=tu...  0.49 us
  transfers between devices with their start and end apart: 10, of which 5 were waited for; matrix products, arithmetic and copies ran while one was open for 1% of the time, Pallas kernels for 14%

profile of v4, /device:TPU:0, one launch (start us, length us, event | category | flops | bytes accessed | tf_op | source)
XLA Modules:
  0.0 22.6 jit_solution(4045079341120272501)
XLA Ops:
  0.6 1.1 %pack.1 = (bf16[208,128]{1,0:T(8,128)(2,1)S(1)}, bf16[16,4,192]{2,1,0:T(4,128)(2,1)S(1)}, bf16[192,384]{1,0:T(8,128)(2,1)S(1)}, bf16[192,384]{1,0:T(8,128)(2,1)S(1)}) custom-call(bf16[16,4,192]{2,1,0:T(4,128)(2,1)} %x_hbm.1, bf16[16,4,192]{2,1,0:T(4,128)(2,1)} %s_hbm.1, bf16[16,4,192]{2,1,0:T(4,128)(2,1)} %c_hbm.1, bf16[4,8]{1,0:T(4,128)(2,1)} %w1_hbm.1, ...), custom_call_target="tpu_custom_call" | custom-call | tf_op jit(solution)/shard_map/pack/pallas_call | solution.py:473
  1.8 5.1 %collective-permute-start = (bf16[208,128]{1,0:T(8,128)(2,1)S(1)}, bf16[208,128]{1,0:T(8,128)(2,1)S(1)}, u32[]{:S(2)}, u32[]{:S(2)}) collective-permute-start(bf16[208,128]{1,0:T(8,128)(2,1)S(1)} %get-tuple-element.38.own_ref), channel_id=1, source_target_pairs={{0,12},{1,13},{2,14},{3,15},{4,8},{5,9},{6,10},{7,11},{8,4},{9,5},... | collective-permute-start | bytes 159752 | tf_op jit(solution)/shard_map/ppermute | solution.py:592
  6.9 0.0 collective-permute-start.1
  6.9 0.6 %collective-permute-start.2 = (bf16[208,128]{1,0:T(8,128)(2,1)S(1)}, bf16[208,128]{1,0:T(8,128)(2,1)S(1)}, u32[]{:S(2)}, u32[]{:S(2)}) collective-permute-start(bf16[208,128]{1,0:T(8,128)(2,1)S(1)} %get-tuple-element.38.own_ref), channel_id=1, source_target_pairs={{0,4},{1,5},{2,6},{3,7},{4,0},{5,1},{6,2},{7,3},{8,12},{9,13},{10,... | collective-permute-start | bytes 159752 | tf_op jit(solution)/shard_map/ppermute | solution.py:592
  7.5 1.7 %collective-permute-start.4 = (bf16[208,128]{1,0:T(8,128)(2,1)S(1)}, bf16[208,128]{1,0:T(8,128)(2,1)S(1)}, u32[]{:S(2)}, u32[]{:S(2)}) collective-permute-start(bf16[208,128]{1,0:T(8,128)(2,1)S(1)} %get-tuple-element.38.own_ref), channel_id=1, source_target_pairs={{0,2},{1,3},{2,0},{3,1},{4,6},{5,7},{6,4},{7,5},{8,10},{9,11},{10,... | collective-permute-start | bytes 159752 | tf_op jit(solution)/shard_map/ppermute | solution.py:592
  9.2 0.5 %prepare.1 = (bf16[112,128]{1,0:T(8,128)(2,1)S(1)}, bf16[96,128]{1,0:T(8,128)(2,1)S(1)}, bf16[384,192]{1,0:T(8,128)(2,1)S(1)}, bf16[256,128]{1,0:T(8,128)(2,1)S(...) custom-call(bf16[208,128]{1,0:T(8,128)(2,1)S(1)} %get-tuple-element., ...), custom_call_target="tpu_custom_call" | custom-call | bytes 2097152 | tf_op jit(solution)/shard_map/prepare/pallas_call | solution.py:493
  9.7 0.0 collective-permute-done
  9.7 2.2 %collective-permute-done.1 = bf16[208,128]{1,0:T(8,128)(2,1)S(1)} collective-permute-done((bf16[208,128]{1,0:T(8,128)(2,1)S(1)}, bf16[208,128]{1,0:T(8,128)(2,1)S(1)}, u32[]{:S(2)}, u32[]{:S(2)}) %collective-permute-start.1) | collective-permute-done | bytes 53280 | tf_op jit(solution)/shard_map/ppermute | solution.py:592
  11.9 0.0 collective-permute-done.2
  12.0 1.6 %collective-permute-start.3 = (bf16[336,128]{1,0:T(8,128)(2,1)S(1)}, bf16[336,128]{1,0:T(8,128)(2,1)S(1)}, u32[]{:S(2)}, u32[]{:S(2)}) collective-permute-start(bf16[336,128]{1,0:T(8,128)(2,1)S(1)} %pad_maximum_fusion.1), channel_id=1, source_target_pairs={{0,2},{1,3},{2,0},{3,1},{4,6},{5,7},{6,4},{7,5},{8,10},{9,11},{10,... | collective-permute-start | bytes 258056 | tf_op jit(solution)/shard_map/ppermute | solution.py:592
  13.6 0.0 collective-permute-done.4
  13.6 0.1 collective-permute-start.5
  13.7 0.6 %collective-permute-start.7 = (bf16[288,128]{1,0:T(8,128)(2,1)S(1)}, bf16[288,128]{1,0:T(8,128)(2,1)S(1)}, u32[]{:S(2)}, u32[]{:S(2)}) collective-permute-start(bf16[288,128]{1,0:T(8,128)(2,1)S(1)} %pad_maximum_fusion.3), channel_id=1, source_target_pairs={{0,2},{1,3},{2,0},{3,1},{4,6},{5,7},{6,4},{7,5},{8,10},{9,11},{10,... | collective-permute-start | bytes 221192 | tf_op jit(solution)/shard_map/ppermute | solution.py:592
  14.3 0.7 %collective-permute-done.5.x1 = bf16[560,128]{1,0:T(8,128)(2,1)S(1)} collective-permute-done((bf16[560,128]{1,0:T(8,128)(2,1)S(1)}, bf16[560,128]{1,0:T(8,128)(2,1)S(1)}, u32[]{:S(2)}, u32[]{:S(2)}) %collective-permute-start.5) | collective-permute-done | bytes 143392 | tf_op jit(solution)/shard_map/ppermute | solution.py:592
  15.0 0.7 %near.1 = (bf16[256,384]{1,0:T(8,128)(2,1)S(1)}, bf16[256,512]{1,0:T(8,128)(2,1)S(1)}, f32[256,384]{1,0:T(8,128)S(1)}, bf16[64,192]{1,0:T(8,128)(2,1)S(1)}, bf16[16,128]{1,0:T(8,128)(2,1)S(1)}) custom-call(bf16[560,128]{1,0:T(8,128)(2,1)S(1)} %slice_dynamic-update-slice_fusion.x0, bf16[560,128]{1,0:T(8,128)(2,1)S(1)} %collective-permute-done.5.x1, ...), custom_call_target="tpu_custom_call" | custom-call | tf_op jit(solution)/shard_map/near/pallas_call | solution.py:527
  15.7 0.8 %collective-permute-done.3.x2 = bf16[336,128]{1,0:T(8,128)(2,1)S(1)} collective-permute-done((bf16[336,128]{1,0:T(8,128)(2,1)S(1)}, bf16[336,128]{1,0:T(8,128)(2,1)S(1)}, u32[]{:S(2)}, u32[]{:S(2)}) %collective-permute-start.3) | collective-permute-done | bytes 86048 | tf_op jit(solution)/shard_map/ppermute | solution.py:592
  16.5 0.1 collective-permute-start.6
  16.6 0.5 %collective-permute-start.8 = (bf16[480,128]{1,0:T(8,128)(2,1)S(1)}, bf16[480,128]{1,0:T(8,128)(2,1)S(1)}, u32[]{:S(2)}, u32[]{:S(2)}) collective-permute-start(bf16[480,128]{1,0:T(8,128)(2,1)S(1)} %slice_dynamic-update-slice_fusion.1.d0), channel_id=1, source_target_pairs={{0,1},{1,0},{2,3},{3,2},{4,5},{5,4},{6,7},{7,6},{8,9},{9,8},{10,11... | collective-permute-start | bytes 368648 | tf_op jit(solution)/shard_map/ppermute | solution.py:592
  17.1 0.8 %collective-permute-done.6.x3 = bf16[352,128]{1,0:T(8,128)(2,1)S(1)} collective-permute-done((bf16[352,128]{1,0:T(8,128)(2,1)S(1)}, bf16[352,128]{1,0:T(8,128)(2,1)S(1)}, u32[]{:S(2)}, u32[]{:S(2)}) %collective-permute-start.6) | collective-permute-done | bytes 90144 | tf_op jit(solution)/shard_map/ppermute | solution.py:592
  17.9 1.0 %mix.1 = (bf16[1024,192]{1,0:T(8,128)(2,1)S(1)}, bf16[512,64]{1,0:T(8,128)(2,1)S(1)}, bf16[64,192]{1,0:T(8,128)(2,1)S(1)}, bf16[64,192]{1,0:T(8,128)(2,1)S(1)}, bf16[16,128]{1,0:T(8,128)(2,1)S(1)}) custom-call(bf16[336,128]{1,0:T(8,128)(2,1)S(1)} %collective-permute-done.3.x2, bf16[352,128]{1,0:T(8,128)(2,1)S(1)} %collective-permute-done.6.x3, ...), custom_call_target="tpu_custom_call" | custom-call | tf_op jit(solution)/shard_map/mix/pallas_call | solution.py:542
  18.9 0.0 collective-permute-done.7.d2
  18.9 0.2 collective-permute-start.9
  19.1 0.9 %hidden.1 = (bf16[1024,384]{1,0:T(8,128)(2,1)S(1)}, f32[1024,384]{1,0:T(8,128)S(1)}, bf16[192,1024]{1,0:T(8,128)(2,1)S(1)}) custom-call(bf16[1024,192]{1,0:T(8,128)(2,1)S(1)} %get-tuple-element.53.sp_ref, bf16[192,384]{1,0:T(8,128)(2,1)S(1)} %get-tuple-element.39.w_in_ref), custom_call_target="tpu_custom_call" | custom-call | tf_op jit(solution)/shard_map/hidden/pallas_call | solution.py:560
  20.0 0.0 collective-permute-done.8.d1
  20.0 0.2 collective-permute-done.9.d3
  20.2 2.4 %backward.1 = (bf16[16,4,192]{2,1,0:T(4,128)(2,1)}, f32[4,8]{1,0:T(4,128)}, f32[4,8]{1,0:T(4,128)}, f32[192,384]{1,0:T(8,128)}, f32[192,384]{1,0:T(8,128)}) custom-call(bf16[1024,384]{1,0:T(8,128)(2,1)S(1)} %get-tuple-element.54.hid_ref, f32[1024,384]{1,0:T(8,128)S(1)} %get-tuple-element.55.slope_ref, bf16[192,1024]{1,0:T(8,128)(2,1)S(1)} %get-tuple-element.56.spt_ref, ...), custom_call_target="tpu_custom_call" | custom-call | tf_op jit(solution)/shard_map/backward/pallas_call | solution.py:573
  (14 shorter events, 0.1 us)
Async XLA Ops:
  1.8 7.9 %collective-permute-start = (bf16[208,128]{1,0:T(8,128)(2,1)S(1)}, bf16[208,128]{1,0:T(8,128)(2,1)S(1)}, u32[]{:S(2)}, u32[]{:S(2)}) collective-permute-start(bf16[208,128]{1,0:T(8,128)(2,1)S(1)} %get-tuple-element.38.own_ref), channel_id=1, source_target_pairs={{0,12},{1,13},{2,14},{3,15},{4,8},{5,9},{6,10},{7,11},{8,4},{9,5},... | collective-permute-start | bytes 159752 | tf_op jit(solution)/shard_map/ppermute | solution.py:592
  6.9 5.0 %collective-permute-start.1 = (bf16[208,128]{1,0:T(8,128)(2,1)S(1)}, bf16[208,128]{1,0:T(8,128)(2,1)S(1)}, u32[]{:S(2)}, u32[]{:S(2)}) collective-permute-start(bf16[208,128]{1,0:T(8,128)(2,1)S(1)} %get-tuple-element.38.own_ref), channel_id=1, source_target_pairs={{0,8},{1,9},{2,10},{3,11},{4,12},{5,13},{6,14},{7,15},{8,0},{9,1},... | collective-permute-start | bytes 159752 | tf_op jit(solution)/shard_map/ppermute | solution.py:592
  6.9 5.0 %collective-permute-start.2 = (bf16[208,128]{1,0:T(8,128)(2,1)S(1)}, bf16[208,128]{1,0:T(8,128)(2,1)S(1)}, u32[]{:S(2)}, u32[]{:S(2)}) collective-permute-start(bf16[208,128]{1,0:T(8,128)(2,1)S(1)} %get-tuple-element.38.own_ref), channel_id=1, source_target_pairs={{0,4},{1,5},{2,6},{3,7},{4,0},{5,1},{6,2},{7,3},{8,12},{9,13},{10,... | collective-permute-start | bytes 159752 | tf_op jit(solution)/shard_map/ppermute | solution.py:592
  7.5 6.0 %collective-permute-start.4 = (bf16[208,128]{1,0:T(8,128)(2,1)S(1)}, bf16[208,128]{1,0:T(8,128)(2,1)S(1)}, u32[]{:S(2)}, u32[]{:S(2)}) collective-permute-start(bf16[208,128]{1,0:T(8,128)(2,1)S(1)} %get-tuple-element.38.own_ref), channel_id=1, source_target_pairs={{0,2},{1,3},{2,0},{3,1},{4,6},{5,7},{6,4},{7,5},{8,10},{9,11},{10,... | collective-permute-start | bytes 159752 | tf_op jit(solution)/shard_map/ppermute | solution.py:592
  12.0 4.6 %collective-permute-start.3 = (bf16[336,128]{1,0:T(8,128)(2,1)S(1)}, bf16[336,128]{1,0:T(8,128)(2,1)S(1)}, u32[]{:S(2)}, u32[]{:S(2)}) collective-permute-start(bf16[336,128]{1,0:T(8,128)(2,1)S(1)} %pad_maximum_fusion.1), channel_id=1, source_target_pairs={{0,2},{1,3},{2,0},{3,1},{4,6},{5,7},{6,4},{7,5},{8,10},{9,11},{10,... | collective-permute-start | bytes 258056 | tf_op jit(solution)/shard_map/ppermute | solution.py:592
  13.6 1.4 %collective-permute-start.5 = (bf16[560,128]{1,0:T(8,128)(2,1)S(1)}, bf16[560,128]{1,0:T(8,128)(2,1)S(1)}, u32[]{:S(2)}, u32[]{:S(2)}) collective-permute-start(bf16[560,128]{1,0:T(8,128)(2,1)S(1)} %slice_dynamic-update-slice_fusion.x0), channel_id=1, source_target_pairs={{0,1},{1,0},{2,3},{3,2},{4,5},{5,4},{6,7},{7,6},{8,9},{9,8},{10,11... | collective-permute-start | bytes 430088 | tf_op jit(solution)/shard_map/ppermute | solution.py:592
  13.7 5.1 %collective-permute-start.7 = (bf16[288,128]{1,0:T(8,128)(2,1)S(1)}, bf16[288,128]{1,0:T(8,128)(2,1)S(1)}, u32[]{:S(2)}, u32[]{:S(2)}) collective-permute-start(bf16[288,128]{1,0:T(8,128)(2,1)S(1)} %pad_maximum_fusion.3), channel_id=1, source_target_pairs={{0,2},{1,3},{2,0},{3,1},{4,6},{5,7},{6,4},{7,5},{8,10},{9,11},{10,... | collective-permute-start | bytes 221192 | tf_op jit(solution)/shard_map/ppermute | solution.py:592
  16.5 1.4 %collective-permute-start.6 = (bf16[352,128]{1,0:T(8,128)(2,1)S(1)}, bf16[352,128]{1,0:T(8,128)(2,1)S(1)}, u32[]{:S(2)}, u32[]{:S(2)}) collective-permute-start(bf16[352,128]{1,0:T(8,128)(2,1)S(1)} %pad_maximum_fusion), channel_id=1, source_target_pairs={{0,1},{1,0},{2,3},{3,2},{4,5},{5,4},{6,7},{7,6},{8,9},{9,8},{10,11... | collective-permute-start | bytes 270344 | tf_op jit(solution)/shard_map/ppermute | solution.py:592
  16.6 3.4 %collective-permute-start.8 = (bf16[480,128]{1,0:T(8,128)(2,1)S(1)}, bf16[480,128]{1,0:T(8,128)(2,1)S(1)}, u32[]{:S(2)}, u32[]{:S(2)}) collective-permute-start(bf16[480,128]{1,0:T(8,128)(2,1)S(1)} %slice_dynamic-update-slice_fusion.1.d0), channel_id=1, source_target_pairs={{0,1},{1,0},{2,3},{3,2},{4,5},{5,4},{6,7},{7,6},{8,9},{9,8},{10,11... | collective-permute-start | bytes 368648 | tf_op jit(solution)/shard_map/ppermute | solution.py:592
  18.9 1.3 %collective-permute-start.9 = (bf16[304,128]{1,0:T(8,128)(2,1)S(1)}, bf16[304,128]{1,0:T(8,128)(2,1)S(1)}, u32[]{:S(2)}, u32[]{:S(2)}) collective-permute-start(bf16[304,128]{1,0:T(8,128)(2,1)S(1)} %pad_maximum_fusion.2), channel_id=1, source_target_pairs={{0,1},{1,0},{2,3},{3,2},{4,5},{5,4},{6,7},{7,6},{8,9},{9,8},{10,11... | collective-permute-start | bytes 233480 | tf_op jit(solution)/shard_map/ppermute | solution.py:592

commit v5 on v4

--- a/solution.py
+++ b/solution.py
@@ -357,8 +357,8 @@
 def mix_kernel(
     x2, x3, x0, x1, first_near_ref, mix2_near_ref, part_ref,
     valid_ref, pick1_ref, spread1_ref, keep1_ref,
-    pick2_ref, spread2_ref, keep2_ref, chosen_ref,
-    sp_ref, back_ref, first_ref, sp_own_ref, mark_ref,
+    pick2_ref, spread2_ref, keep2_ref,
+    sp_ref, back_ref, sp_own_ref, first_far_ref, mark_ref,
 ):
     own = sp_own_ref.shape[0] // 2
     half, rows = mix2_near_ref.shape
@@ -379,16 +379,20 @@
     back_ref[half:, :] = mix2_far[:, : 2 * own]
     sp_low, sp_high = unpacked(*cut(spectral))
     sp_own_ref[:own, :], sp_own_ref[own:, :] = sp_low[:own], sp_high[:own]
-    first_ref[:own, :], first_ref[own:, :] = unpacked(
-        *cut(mul(chosen_ref[...], first).astype(bf16))
-    )
-
+    first_far_ref[...] = first_far
     sp_ref[:rows, :] = sp_low
     sp_ref[rows:, :] = sp_high
     mark_ref[...] = jnp.zeros_like(mark_ref)
 
 
-def hidden_kernel(sp_ref, w_in_ref, hid_ref, slope_ref, spt_ref):
+def hidden_kernel(
+    sp_ref, w_in_ref, first_near_ref, first_far_ref, chosen_ref,
+    hid_ref, slope_ref, spt_ref, first_ref,
+):
+    own, half = chosen_ref.shape[0], first_near_ref.shape[0]
+    first = mul(chosen_ref[:, :half], first_near_ref[...])
+    first += mul(chosen_ref[:, half:], first_far_ref[...])
+    first_ref[:own, :], first_ref[own:, :] = unpacked(*cut(first.astype(bf16)))
     sp = sp_ref[...]
     gelu_out, slope = gelu_and_slope(mul(sp, w_in_ref[...]))
     hid_ref[...] = gelu_out.astype(bf16)
@@ -397,7 +401,7 @@
 
 
 def backward_kernel(
-    hid_ref, slope_ref, spt_ref, back_ref, first_ref, sp_own_ref, own_ref, d2, d0, d1, d3,
+    hid_ref, slope_ref, spt_ref, first_ref, back_ref, sp_own_ref, own_ref, d2, d0, d1, d3,
     s_ref, w_in_t_ref, w_out_ref,
     enh_ref, g1_ref, g2_ref, gwi_ref, gwo_ref,
 ):
@@ -411,14 +415,17 @@
     at = Rows(own, bins, rows)
     order = sum(halves_of(devices), [])
     dm_low, dm_high = unpacked(*tiles_of(refs, 3 * own, devices, own, order))
+    parts = 2 * rows // 4
+    dm = [half[k : k + parts] for half in (dm_low, dm_high) for k in range(0, rows, parts)]
     dpre, dsp = [], []
-    for n, part in enumerate((dm_low, dm_high)):
-        to = slice(n * rows, (n + 1) * rows)
+    for n, part in enumerate(dm):
+        to = slice(n * parts, (n + 1) * parts)
         dpre.append((mul(part, w_out_ref[...]) * slope_ref[to, :]).astype(bf16))
-    for n, part in enumerate((dm_low, dm_high)):
         dsp.append((part.astype(f32) + mul(dpre[n], w_in_t_ref[...])).astype(bf16))
-    gwi_ref[...] = mul(spt_ref[:, :rows], dpre[0]) + mul(spt_ref[:, rows:], dpre[1])
-    gwo_ref[...] = mul(dm_low, hid_ref[:rows, :], TN) + mul(dm_high, hid_ref[rows:, :], TN)
+    dpre, dsp = jnp.concatenate(dpre, 0), jnp.concatenate(dsp, 0)
+    dsp = dsp[:rows], dsp[rows:]
+    gwi_ref[...] = mul(spt_ref[...], dpre)
+    gwo_ref[...] = mul(jnp.concatenate([dm_low, dm_high], 0), hid_ref[...], TN)
 
     sp_own = sp_own_ref[...]
     hidden = jnp.concatenate([hid_ref[:own, :], hid_ref[rows : rows + own, :]], 0)
@@ -453,7 +460,11 @@
     take = ((row < per_block) & (place == col)) | (
         (row >= per_block) & (block + (place ^ at.side) == col)
     )
-    both = mul_f32(jnp.concatenate(sums, 1), take.astype(f32))
+    left, both, chosen = jnp.concatenate(sums, 1), 0.0, onehot(take)
+    for _ in range(3):
+        part = left.astype(bf16)
+        both += mul(part, chosen)
+        left -= part.astype(f32)
     g1_ref[...] = both[:, :block]
     g2_ref[...] = both[:, block:]
 
@@ -539,7 +550,7 @@
         name="near",
     )(x0, x1, *selections[:-1])
     x3 = exchanged(jnp.concatenate([x2, mark], 0), 1)
-    spectral, *kept, mark = pl.pallas_call(
+    spectral, *kept, first_far, mark = pl.pallas_call(
         mix_kernel,
         out_shape=tuple(
             pltpu.VMEM(shape, bf16)
@@ -547,15 +558,15 @@
                 (2 * rows, channels),
                 (rows, 2 * own),
                 (2 * own, channels),
-                (2 * own, channels),
+                (rows // 2, 2 * channels),
                 (W_ROWS, LANES),
             ]
         ),
-        in_specs=in_vmem(15),
+        in_specs=in_vmem(14),
         out_specs=tuple(in_vmem(5)),
         compiler_params=params,
         name="mix",
-    )(x2, x3, x0, x1, first_near, mix2_near, part, *selections)
+    )(x2, x3, x0, x1, first_near, mix2_near, part, *selections[:-1])
     d3 = exchanged(jnp.concatenate([d2, mark], 0), 1)
     hidden = pl.pallas_call(
         hidden_kernel,
@@ -563,12 +574,13 @@
             pltpu.VMEM((2 * rows, hid), bf16),
             pltpu.VMEM((2 * rows, hid), f32),
             pltpu.VMEM((channels, 2 * rows), bf16),
+            pltpu.VMEM((2 * own, channels), bf16),
         ),
-        in_specs=in_vmem(2),
-        out_specs=tuple(in_vmem(3)),
+        in_specs=in_vmem(5),
+        out_specs=tuple(in_vmem(4)),
         compiler_params=params,
         name="hidden",
-    )(spectral, w_in_in)
+    )(spectral, w_in_in, first_near, first_far, selections[-1])
 
     enhanced, grad_first, grad_second, grad_w_in, grad_w_out = pl.pallas_call(
         backward_kernel,

time: 22.8 us -> 22.6 us (level)
  transfers between devices with their start and end apart: 10 -> 10, of which waited for: 5 -> 5; matrix products, arithmetic and copies ran while one was open for 1% -> 1% of each run, Pallas kernels for 14% -> 13%
where the time goes in v5:
time: 22.6 us; the launch traced here: 22.5 us
  starting transfers between devices  10.4 us (46%)
  Pallas kernels  6.49 us (29%)
  waiting for transfers between devices  4.64 us (21%)
  between operations  0.78 us (3%)
    ppermute x10, starting transfers between devices, exchanged(): return lax.ppermute(value, 'freq', pairs)  10.4 us
    ppermute x10, waiting for transfers between devices, exchanged(): return lax.ppermute(value, 'freq', pairs)  4.64 us
    pallas_call x1, Pallas kernels, whole_rows(): pl.pallas_call(backward_kernel, out_shape=(shaped((frames, bins, channels...  2.32 us
    pallas_call x1, Pallas kernels, whole_rows(): pl.pallas_call(functools.partial(pack_kernel, scale=scale), out_shape=(pl...  1.13 us
    pallas_call x1, Pallas kernels, whole_rows(): pl.pallas_call(hidden_kernel, out_shape=(pltpu.VMEM((2 * rows, hid), bf16...  0.97 us
    pallas_call x1, Pallas kernels, whole_rows(): pl.pallas_call(mix_kernel, out_shape=tuple((pltpu.VMEM(shape, bf16) for s...  0.9 us
    pallas_call x1, Pallas kernels, whole_rows(): pl.pallas_call(near_kernel, out_shape=(pltpu.VMEM((rows // 2, 2 * channel...  0.68 us
    pallas_call x1, Pallas kernels, whole_rows(): pl.pallas_call(functools.partial(prepare_kernel, bins=bins), out_shape=tu...  0.49 us
  transfers between devices with their start and end apart: 10, of which 5 were waited for; matrix products, arithmetic and copies ran while one was open for 1% of the time, Pallas kernels for 13%

profile of v5, /device:TPU:0, one launch (start us, length us, event | category | flops | bytes accessed | tf_op | source)
XLA Modules:
  0.0 22.5 jit_solution(1411289105446927778)
XLA Ops:
  0.6 1.1 %pack.1 = (bf16[208,128]{1,0:T(8,128)(2,1)S(1)}, bf16[16,4,192]{2,1,0:T(4,128)(2,1)S(1)}, bf16[192,384]{1,0:T(8,128)(2,1)S(1)}, bf16[192,384]{1,0:T(8,128)(2,1)S(1)}) custom-call(bf16[16,4,192]{2,1,0:T(4,128)(2,1)} %x_hbm.1, bf16[16,4,192]{2,1,0:T(4,128)(2,1)} %s_hbm.1, bf16[16,4,192]{2,1,0:T(4,128)(2,1)} %c_hbm.1, bf16[4,8]{1,0:T(4,128)(2,1)} %w1_hbm.1, ...), custom_call_target="tpu_custom_call" | custom-call | tf_op jit(solution)/shard_map/pack/pallas_call | solution.py:484
  1.8 5.1 %collective-permute-start = (bf16[208,128]{1,0:T(8,128)(2,1)S(1)}, bf16[208,128]{1,0:T(8,128)(2,1)S(1)}, u32[]{:S(2)}, u32[]{:S(2)}) collective-permute-start(bf16[208,128]{1,0:T(8,128)(2,1)S(1)} %get-tuple-element.39.own_ref), channel_id=1, source_target_pairs={{0,12},{1,13},{2,14},{3,15},{4,8},{5,9},{6,10},{7,11},{8,4},{9,5},... | collective-permute-start | bytes 159752 | tf_op jit(solution)/shard_map/ppermute | solution.py:604
  6.9 0.0 collective-permute-start.1
  6.9 0.6 %collective-permute-start.2 = (bf16[208,128]{1,0:T(8,128)(2,1)S(1)}, bf16[208,128]{1,0:T(8,128)(2,1)S(1)}, u32[]{:S(2)}, u32[]{:S(2)}) collective-permute-start(bf16[208,128]{1,0:T(8,128)(2,1)S(1)} %get-tuple-element.39.own_ref), channel_id=1, source_target_pairs={{0,4},{1,5},{2,6},{3,7},{4,0},{5,1},{6,2},{7,3},{8,12},{9,13},{10,... | collective-permute-start | bytes 159752 | tf_op jit(solution)/shard_map/ppermute | solution.py:604
  7.5 1.7 %collective-permute-start.4 = (bf16[208,128]{1,0:T(8,128)(2,1)S(1)}, bf16[208,128]{1,0:T(8,128)(2,1)S(1)}, u32[]{:S(2)}, u32[]{:S(2)}) collective-permute-start(bf16[208,128]{1,0:T(8,128)(2,1)S(1)} %get-tuple-element.39.own_ref), channel_id=1, source_target_pairs={{0,2},{1,3},{2,0},{3,1},{4,6},{5,7},{6,4},{7,5},{8,10},{9,11},{10,... | collective-permute-start | bytes 159752 | tf_op jit(solution)/shard_map/ppermute | solution.py:604
  9.2 0.5 %prepare.1 = (bf16[112,128]{1,0:T(8,128)(2,1)S(1)}, bf16[96,128]{1,0:T(8,128)(2,1)S(1)}, bf16[384,192]{1,0:T(8,128)(2,1)S(1)}, bf16[256,128]{1,0:T(8,128)(2,1)S(...) custom-call(bf16[208,128]{1,0:T(8,128)(2,1)S(1)} %get-tuple-element., ...), custom_call_target="tpu_custom_call" | custom-call | bytes 2097152 | tf_op jit(solution)/shard_map/prepare/pallas_call | solution.py:504
  9.7 0.0 collective-permute-done
  9.7 2.2 %collective-permute-done.1 = bf16[208,128]{1,0:T(8,128)(2,1)S(1)} collective-permute-done((bf16[208,128]{1,0:T(8,128)(2,1)S(1)}, bf16[208,128]{1,0:T(8,128)(2,1)S(1)}, u32[]{:S(2)}, u32[]{:S(2)}) %collective-permute-start.1) | collective-permute-done | bytes 53280 | tf_op jit(solution)/shard_map/ppermute | solution.py:604
  11.9 0.0 collective-permute-done.2
  12.0 1.6 %collective-permute-start.3 = (bf16[336,128]{1,0:T(8,128)(2,1)S(1)}, bf16[336,128]{1,0:T(8,128)(2,1)S(1)}, u32[]{:S(2)}, u32[]{:S(2)}) collective-permute-start(bf16[336,128]{1,0:T(8,128)(2,1)S(1)} %pad_maximum_fusion.1), channel_id=1, source_target_pairs={{0,2},{1,3},{2,0},{3,1},{4,6},{5,7},{6,4},{7,5},{8,10},{9,11},{10,... | collective-permute-start | bytes 258056 | tf_op jit(solution)/shard_map/ppermute | solution.py:604
  13.6 0.0 collective-permute-done.4
  13.6 0.1 collective-permute-start.5
  13.7 0.6 %collective-permute-start.7 = (bf16[288,128]{1,0:T(8,128)(2,1)S(1)}, bf16[288,128]{1,0:T(8,128)(2,1)S(1)}, u32[]{:S(2)}, u32[]{:S(2)}) collective-permute-start(bf16[288,128]{1,0:T(8,128)(2,1)S(1)} %pad_maximum_fusion.3), channel_id=1, source_target_pairs={{0,2},{1,3},{2,0},{3,1},{4,6},{5,7},{6,4},{7,5},{8,10},{9,11},{10,... | collective-permute-start | bytes 221192 | tf_op jit(solution)/shard_map/ppermute | solution.py:604
  14.3 0.7 %collective-permute-done.5.x1 = bf16[560,128]{1,0:T(8,128)(2,1)S(1)} collective-permute-done((bf16[560,128]{1,0:T(8,128)(2,1)S(1)}, bf16[560,128]{1,0:T(8,128)(2,1)S(1)}, u32[]{:S(2)}, u32[]{:S(2)}) %collective-permute-start.5) | collective-permute-done | bytes 143392 | tf_op jit(solution)/shard_map/ppermute | solution.py:604
  15.0 0.7 %near.1 = (bf16[256,384]{1,0:T(8,128)(2,1)S(1)}, bf16[256,512]{1,0:T(8,128)(2,1)S(1)}, f32[256,384]{1,0:T(8,128)S(1)}, bf16[64,192]{1,0:T(8,128)(2,1)S(1)}, bf16[16,128]{1,0:T(8,128)(2,1)S(1)}) custom-call(bf16[560,128]{1,0:T(8,128)(2,1)S(1)} %slice_dynamic-update-slice_fusion.x0, bf16[560,128]{1,0:T(8,128)(2,1)S(1)} %collective-permute-done.5.x1, ...), custom_call_target="tpu_custom_call" | custom-call | tf_op jit(solution)/shard_map/near/pallas_call | solution.py:538
  15.7 0.8 %collective-permute-done.3.x2 = bf16[336,128]{1,0:T(8,128)(2,1)S(1)} collective-permute-done((bf16[336,128]{1,0:T(8,128)(2,1)S(1)}, bf16[336,128]{1,0:T(8,128)(2,1)S(1)}, u32[]{:S(2)}, u32[]{:S(2)}) %collective-permute-start.3) | collective-permute-done | bytes 86048 | tf_op jit(solution)/shard_map/ppermute | solution.py:604
  16.5 0.1 collective-permute-start.6
  16.6 0.5 %collective-permute-start.8 = (bf16[480,128]{1,0:T(8,128)(2,1)S(1)}, bf16[480,128]{1,0:T(8,128)(2,1)S(1)}, u32[]{:S(2)}, u32[]{:S(2)}) collective-permute-start(bf16[480,128]{1,0:T(8,128)(2,1)S(1)} %slice_dynamic-update-slice_fusion.1.d0), channel_id=1, source_target_pairs={{0,1},{1,0},{2,3},{3,2},{4,5},{5,4},{6,7},{7,6},{8,9},{9,8},{10,11... | collective-permute-start | bytes 368648 | tf_op jit(solution)/shard_map/ppermute | solution.py:604
  17.1 0.8 %collective-permute-done.6.x3 = bf16[352,128]{1,0:T(8,128)(2,1)S(1)} collective-permute-done((bf16[352,128]{1,0:T(8,128)(2,1)S(1)}, bf16[352,128]{1,0:T(8,128)(2,1)S(1)}, u32[]{:S(2)}, u32[]{:S(2)}) %collective-permute-start.6) | collective-permute-done | bytes 90144 | tf_op jit(solution)/shard_map/ppermute | solution.py:604
  17.9 0.9 %mix.1 = (bf16[1024,192]{1,0:T(8,128)(2,1)S(1)}, bf16[512,64]{1,0:T(8,128)(2,1)S(1)}, bf16[64,192]{1,0:T(8,128)(2,1)S(1)}, bf16[256,384]{1,0:T(8,128)(2,1)S(1)}, bf16[16,128]{1,0:T(8,128)(2,1)S(1)}) custom-call(bf16[336,128]{1,0:T(8,128)(2,1)S(1)} %collective-permute-done.3.x2, bf16[352,128]{1,0:T(8,128)(2,1)S(1)} %collective-permute-done.6.x3, ...), custom_call_target="tpu_custom_call" | custom-call | tf_op jit(solution)/shard_map/mix/pallas_call | solution.py:553
  18.8 0.0 collective-permute-done.7.d2
  18.8 0.2 collective-permute-start.9
  19.0 1.0 %hidden.1 = (bf16[1024,384]{1,0:T(8,128)(2,1)S(1)}, f32[1024,384]{1,0:T(8,128)S(1)}, bf16[192,1024]{1,0:T(8,128)(2,1)S(1)}, bf16[64,192]{1,0:T(8,128)(2,1)S(1)}) custom-call(bf16[1024,192]{1,0:T(8,128)(2,1)S(1)} %get-tuple-element.53.sp_ref, bf16[192,384]{1,0:T(8,128)(2,1)S(1)} %get-tuple-element.40.w_in_ref, ...), custom_call_target="tpu_custom_call" | custom-call | tf_op jit(solution)/shard_map/hidden/pallas_call | solution.py:571
  20.0 0.0 collective-permute-done.8.d1
  20.0 0.1 collective-permute-done.9.d3
  20.1 2.3 %backward.1 = (bf16[16,4,192]{2,1,0:T(4,128)(2,1)}, f32[4,8]{1,0:T(4,128)}, f32[4,8]{1,0:T(4,128)}, f32[192,384]{1,0:T(8,128)}, f32[192,384]{1,0:T(8,128)}) custom-call(bf16[1024,384]{1,0:T(8,128)(2,1)S(1)} %get-tuple-element.56.hid_ref, f32[1024,384]{1,0:T(8,128)S(1)} %get-tuple-element.57.slope_ref, bf16[192,1024]{1,0:T(8,128)(2,1)S(1)} %get-tuple-element.58.spt_ref, ...), custom_call_target="tpu_custom_call" | custom-call | tf_op jit(solution)/shard_map/backward/pallas_call | solution.py:585
  (14 shorter events, 0.1 us)
Async XLA Ops:
  1.8 7.9 %collective-permute-start = (bf16[208,128]{1,0:T(8,128)(2,1)S(1)}, bf16[208,128]{1,0:T(8,128)(2,1)S(1)}, u32[]{:S(2)}, u32[]{:S(2)}) collective-permute-start(bf16[208,128]{1,0:T(8,128)(2,1)S(1)} %get-tuple-element.39.own_ref), channel_id=1, source_target_pairs={{0,12},{1,13},{2,14},{3,15},{4,8},{5,9},{6,10},{7,11},{8,4},{9,5},... | collective-permute-start | bytes 159752 | tf_op jit(solution)/shard_map/ppermute | solution.py:604
  6.9 5.0 %collective-permute-start.1 = (bf16[208,128]{1,0:T(8,128)(2,1)S(1)}, bf16[208,128]{1,0:T(8,128)(2,1)S(1)}, u32[]{:S(2)}, u32[]{:S(2)}) collective-permute-start(bf16[208,128]{1,0:T(8,128)(2,1)S(1)} %get-tuple-element.39.own_ref), channel_id=1, source_target_pairs={{0,8},{1,9},{2,10},{3,11},{4,12},{5,13},{6,14},{7,15},{8,0},{9,1},... | collective-permute-start | bytes 159752 | tf_op jit(solution)/shard_map/ppermute | solution.py:604
  6.9 5.0 %collective-permute-start.2 = (bf16[208,128]{1,0:T(8,128)(2,1)S(1)}, bf16[208,128]{1,0:T(8,128)(2,1)S(1)}, u32[]{:S(2)}, u32[]{:S(2)}) collective-permute-start(bf16[208,128]{1,0:T(8,128)(2,1)S(1)} %get-tuple-element.39.own_ref), channel_id=1, source_target_pairs={{0,4},{1,5},{2,6},{3,7},{4,0},{5,1},{6,2},{7,3},{8,12},{9,13},{10,... | collective-permute-start | bytes 159752 | tf_op jit(solution)/shard_map/ppermute | solution.py:604
  7.5 6.0 %collective-permute-start.4 = (bf16[208,128]{1,0:T(8,128)(2,1)S(1)}, bf16[208,128]{1,0:T(8,128)(2,1)S(1)}, u32[]{:S(2)}, u32[]{:S(2)}) collective-permute-start(bf16[208,128]{1,0:T(8,128)(2,1)S(1)} %get-tuple-element.39.own_ref), channel_id=1, source_target_pairs={{0,2},{1,3},{2,0},{3,1},{4,6},{5,7},{6,4},{7,5},{8,10},{9,11},{10,... | collective-permute-start | bytes 159752 | tf_op jit(solution)/shard_map/ppermute | solution.py:604
  12.0 4.6 %collective-permute-start.3 = (bf16[336,128]{1,0:T(8,128)(2,1)S(1)}, bf16[336,128]{1,0:T(8,128)(2,1)S(1)}, u32[]{:S(2)}, u32[]{:S(2)}) collective-permute-start(bf16[336,128]{1,0:T(8,128)(2,1)S(1)} %pad_maximum_fusion.1), channel_id=1, source_target_pairs={{0,2},{1,3},{2,0},{3,1},{4,6},{5,7},{6,4},{7,5},{8,10},{9,11},{10,... | collective-permute-start | bytes 258056 | tf_op jit(solution)/shard_map/ppermute | solution.py:604
  13.6 1.4 %collective-permute-start.5 = (bf16[560,128]{1,0:T(8,128)(2,1)S(1)}, bf16[560,128]{1,0:T(8,128)(2,1)S(1)}, u32[]{:S(2)}, u32[]{:S(2)}) collective-permute-start(bf16[560,128]{1,0:T(8,128)(2,1)S(1)} %slice_dynamic-update-slice_fusion.x0), channel_id=1, source_target_pairs={{0,1},{1,0},{2,3},{3,2},{4,5},{5,4},{6,7},{7,6},{8,9},{9,8},{10,11... | collective-permute-start | bytes 430088 | tf_op jit(solution)/shard_map/ppermute | solution.py:604
  13.7 5.1 %collective-permute-start.7 = (bf16[288,128]{1,0:T(8,128)(2,1)S(1)}, bf16[288,128]{1,0:T(8,128)(2,1)S(1)}, u32[]{:S(2)}, u32[]{:S(2)}) collective-permute-start(bf16[288,128]{1,0:T(8,128)(2,1)S(1)} %pad_maximum_fusion.3), channel_id=1, source_target_pairs={{0,2},{1,3},{2,0},{3,1},{4,6},{5,7},{6,4},{7,5},{8,10},{9,11},{10,... | collective-permute-start | bytes 221192 | tf_op jit(solution)/shard_map/ppermute | solution.py:604
  16.5 1.4 %collective-permute-start.6 = (bf16[352,128]{1,0:T(8,128)(2,1)S(1)}, bf16[352,128]{1,0:T(8,128)(2,1)S(1)}, u32[]{:S(2)}, u32[]{:S(2)}) collective-permute-start(bf16[352,128]{1,0:T(8,128)(2,1)S(1)} %pad_maximum_fusion), channel_id=1, source_target_pairs={{0,1},{1,0},{2,3},{3,2},{4,5},{5,4},{6,7},{7,6},{8,9},{9,8},{10,11... | collective-permute-start | bytes 270344 | tf_op jit(solution)/shard_map/ppermute | solution.py:604
  16.6 3.4 %collective-permute-start.8 = (bf16[480,128]{1,0:T(8,128)(2,1)S(1)}, bf16[480,128]{1,0:T(8,128)(2,1)S(1)}, u32[]{:S(2)}, u32[]{:S(2)}) collective-permute-start(bf16[480,128]{1,0:T(8,128)(2,1)S(1)} %slice_dynamic-update-slice_fusion.1.d0), channel_id=1, source_target_pairs={{0,1},{1,0},{2,3},{3,2},{4,5},{5,4},{6,7},{7,6},{8,9},{9,8},{10,11... | collective-permute-start | bytes 368648 | tf_op jit(solution)/shard_map/ppermute | solution.py:604
  18.8 1.3 %collective-permute-start.9 = (bf16[304,128]{1,0:T(8,128)(2,1)S(1)}, bf16[304,128]{1,0:T(8,128)(2,1)S(1)}, u32[]{:S(2)}, u32[]{:S(2)}) collective-permute-start(bf16[304,128]{1,0:T(8,128)(2,1)S(1)} %pad_maximum_fusion.2), channel_id=1, source_target_pairs={{0,1},{1,0},{2,3},{3,2},{4,5},{5,4},{6,7},{7,6},{8,9},{9,8},{10,11... | collective-permute-start | bytes 233480 | tf_op jit(solution)/shard_map/ppermute | solution.py:604

commit v6 on v5

--- a/solution.py
+++ b/solution.py
@@ -210,7 +210,7 @@
 def piece(refs, per_device, devices, j, start, size):
     held = received_from(devices)
     n = next(n for n, part in enumerate(held) if j in part)
-    at = held[n].index(j) * per_device + start
+    at = held[n].index(j) * per_device[n] + start
     return refs[n][at : at + size, :]
 
 
@@ -279,7 +279,8 @@
 
 def prepare_kernel(
     own_ref, w_in_ref, x_ref, d_ref, w_in_t_ref, valid_ref, pick1_ref, spread1_ref, keep1_ref,
-    pick2_ref, spread2_ref, keep2_ref, chosen_ref, *, bins,
+    pick2_ref, spread2_ref, keep2_ref, valid_far_ref, spread1_far_ref, spread2_far_ref, chosen_ref,
+    *, bins,
 ):
     w_in_t_ref[...] = w_in_ref[...].T
     x_ref[...] = own_ref[: x_ref.shape[0], :]
@@ -313,6 +314,19 @@
         (at.frame(row) == at.frame(col)) & (at.place(col) == (at.block(row) ^ at.chip))
     )
 
+    def far_place(r):
+        return (r // W_ROWS) * bins + (r & (bins - 1))
+
+    def far_local(r):
+        return W_ROWS // bins - 1 - (r & (W_ROWS - 1)) // bins
+
+    r, w = iota(valid_far_ref.shape, 0), iota(valid_far_ref.shape, 1)
+    valid_far_ref[...] = onehot(far_local(w) == at.local(r))
+    w, r = iota(spread1_far_ref.shape, 0), iota(spread1_far_ref.shape, 1)
+    spread1_far_ref[...] = onehot((far_place(w) == at.place(r)) & (far_local(w) == at.local(r)))
+    w, r = iota(spread2_far_ref.shape, 0), iota(spread2_far_ref.shape, 1)
+    spread2_far_ref[...] = onehot(far_place(w) == (at.block(r) ^ at.chip ^ at.side))
+
     row, col = iota(chosen_ref.shape, 0), iota(chosen_ref.shape, 1)
     chosen_ref[...] = onehot(
         (at.block(col) == ((at.side + (row & (bins - 1))) ^ at.chip))
@@ -321,13 +335,13 @@
     )
 
 
-def mixing(refs, devices, own, order, selections, keep2):
+def x_rows_of(own):
+    return (3 * own + W_ROWS,) * 2 + (3 * own,) * 2
+
+
+def mixing(refs, devices, own, order, factors, selections, keep2):
     valid_ref, pick1_ref, spread1_ref, keep1_ref, pick2_ref, spread2_ref = selections
-    per_x = 3 * own + W_ROWS
-    factors = jnp.concatenate(
-        [piece(refs, per_x, devices, j, 3 * own, W_ROWS) for j in order], 0
-    )
-    tiles = tiles_of(refs, per_x, devices, own, order)
+    tiles = tiles_of(refs, x_rows_of(own), devices, own, order)
     picked = [
         mul(pick[...], factors, NT).astype(bf16) * valid_ref[...] for pick in (pick1_ref, pick2_ref)
     ]
@@ -344,8 +358,10 @@
     half, rows = mix2_ref.shape
     devices = rows // own
     selections = (valid_ref, pick1_ref, spread1_ref, keep1_ref, pick2_ref, spread2_ref)
+    order = halves_of(devices)[0]
+    factors = [piece((x0, x1), x_rows_of(own), devices, j, 3 * own, W_ROWS) for j in order]
     tiles, first, mix2 = mixing(
-        (x0, x1), devices, own, halves_of(devices)[0], selections, keep2_ref[:half, :]
+        (x0, x1), devices, own, order, jnp.concatenate(factors, 0), selections, keep2_ref[:half, :]
     )
     first_ref[...] = first
     mix2_ref[...] = mix2
@@ -364,8 +380,10 @@
     half, rows = mix2_near_ref.shape
     devices = rows // own
     selections = (valid_ref, pick1_ref, spread1_ref, keep1_ref, pick2_ref, spread2_ref)
+    at_end = (devices // 4 - 1) * 3 * own
+    factors = jnp.concatenate([ref[at_end : at_end + W_ROWS, :] for ref in (x2, x3)], 0)
     _, first_far, mix2_far = mixing(
-        (x0, x1, x2, x3), devices, own, halves_of(devices)[1], selections, keep2_ref[half:, :]
+        (x0, x1, x2, x3), devices, own, halves_of(devices)[1], factors, selections, keep2_ref[half:, :]
     )
     first = jnp.concatenate([first_near_ref[...], first_far], 0)
     spectral = jnp.concatenate(
@@ -414,7 +432,7 @@
     devices = rows // own
     at = Rows(own, bins, rows)
     order = sum(halves_of(devices), [])
-    dm_low, dm_high = unpacked(*tiles_of(refs, 3 * own, devices, own, order))
+    dm_low, dm_high = unpacked(*tiles_of(refs, (3 * own,) * 4, devices, own, order))
     parts = 2 * rows // 4
     dm = [half[k : k + parts] for half in (dm_low, dm_high) for k in range(0, rows, parts)]
     dpre, dsp = [], []
@@ -516,11 +534,14 @@
                 (rows // 2, LANES),
                 (w_rows // 2, rows),
                 (rows, rows),
+                (rows // 2, 2 * W_ROWS),
+                (2 * W_ROWS, rows // 2),
+                (2 * W_ROWS, rows),
                 (own, rows),
             ]
         ),
         in_specs=in_vmem(2),
-        out_specs=tuple(in_vmem(11)),
+        out_specs=tuple(in_vmem(14)),
         compiler_params=params,
         cost_estimate=pl.CostEstimate(flops=0, bytes_accessed=2**21, transcendentals=0),
         name="prepare",
@@ -529,10 +550,15 @@
     column = [exchanged(own_rows, j) for j in range(devices - 4, 0, -4)]
     x_rows = 3 * own + W_ROWS
     across = exchanged(own_rows, 2)
-    x_column = jnp.concatenate([got[:x_rows] for got in column], 0)
+    sent = [*column, own_rows]
+    x_column = jnp.concatenate(
+        [got[: 3 * own] for got in column]
+        + [got[3 * own : 3 * own + bins] for got in sent],
+        0,
+    )
     d_column = jnp.concatenate([got[x_rows:] for got in column], 0)
     x2, d2 = exchanged(x_column, 2), exchanged(d_column, 2)
-    x0 = jnp.concatenate([x_column, x_own, across[:x_rows]], 0)
+    x0 = jnp.concatenate([*[got[:x_rows] for got in column], x_own, across[:x_rows]], 0)
     d0 = jnp.concatenate([d_column, d_own, across[x_rows:]], 0)
     x1, d1 = exchanged(x0, 1), exchanged(d0, 1)
     first_near, mix2_near, part, x_rows_own, mark = pl.pallas_call(
@@ -548,8 +574,10 @@
         out_specs=tuple(in_vmem(5)),
         compiler_params=params,
         name="near",
-    )(x0, x1, *selections[:-1])
+    )(x0, x1, *selections[:7])
     x3 = exchanged(jnp.concatenate([x2, mark], 0), 1)
+    pick1, keep1, pick2, keep2 = (selections[n] for n in (1, 3, 4, 6))
+    valid_far, spread1_far, spread2_far = selections[7:10]
     spectral, *kept, first_far, mark = pl.pallas_call(
         mix_kernel,
         out_shape=tuple(
@@ -566,7 +594,10 @@
         out_specs=tuple(in_vmem(5)),
         compiler_params=params,
         name="mix",
-    )(x2, x3, x0, x1, first_near, mix2_near, part, *selections[:-1])
+    )(
+        x2, x3, x0, x1, first_near, mix2_near, part,
+        valid_far, pick1, spread1_far, keep1, pick2, spread2_far, keep2,
+    )
     d3 = exchanged(jnp.concatenate([d2, mark], 0), 1)
     hidden = pl.pallas_call(
         hidden_kernel,
@@ -618,6 +649,7 @@
         and LANES < channels
         and 2 * (channels - LANES) == LANES
         and devices % 4 == 0
+        and devices // 4 * bins == W_ROWS
     )
     plan = whole_rows if fits and shaped else split_rows
     return plan(features, spectrum, cotangent, w_first, w_second, w_in, w_out)

time: 22.6 us -> 22.5 us (level)
  transfers between devices with their start and end apart: 10 -> 10, of which waited for: 5 -> 5; matrix products, arithmetic and copies ran while one was open for 1% -> 1% of each run, Pallas kernels for 13% -> 14%
where the time goes in v6:
time: 22.5 us; the launch traced here: 22.4 us
  starting transfers between devices  10.3 us (46%)
  Pallas kernels  6.49 us (29%)
  waiting for transfers between devices  4.5 us (20%)
  between operations  0.79 us (4%)
    ppermute x10, starting transfers between devices, exchanged(): return lax.ppermute(value, 'freq', pairs)  10.3 us
    ppermute x10, waiting for transfers between devices, exchanged(): return lax.ppermute(value, 'freq', pairs)  4.5 us
    pallas_call x1, Pallas kernels, whole_rows(): pl.pallas_call(backward_kernel, out_shape=(shaped((frames, bins, channels...  2.3 us
    pallas_call x1, Pallas kernels, whole_rows(): pl.pallas_call(functools.partial(pack_kernel, scale=scale), out_shape=(pl...  1.13 us
    pallas_call x1, Pallas kernels, whole_rows(): pl.pallas_call(hidden_kernel, out_shape=(pltpu.VMEM((2 * rows, hid), bf16...  0.99 us
    pallas_call x1, Pallas kernels, whole_rows(): pl.pallas_call(mix_kernel, out_shape=tuple((pltpu.VMEM(shape, bf16) for s...  0.87 us
    pallas_call x1, Pallas kernels, whole_rows(): pl.pallas_call(near_kernel, out_shape=(pltpu.VMEM((rows // 2, 2 * channel...  0.68 us
    pallas_call x1, Pallas kernels, whole_rows(): pl.pallas_call(functools.partial(prepare_kernel, bins=bins), out_shape=tu...  0.52 us
  transfers between devices with their start and end apart: 10, of which 5 were waited for; matrix products, arithmetic and copies ran while one was open for 1% of the time, Pallas kernels for 14%

profile of v6, /device:TPU:0, one launch (start us, length us, event | category | flops | bytes accessed | tf_op | source)
XLA Modules:
  0.0 22.4 jit_solution(6662439825221231162)
XLA Ops:
  0.6 1.1 %pack.1 = (bf16[208,128]{1,0:T(8,128)(2,1)S(1)}, bf16[16,4,192]{2,1,0:T(4,128)(2,1)S(1)}, bf16[192,384]{1,0:T(8,128)(2,1)S(1)}, bf16[192,384]{1,0:T(8,128)(2,1)S(1)}) custom-call(bf16[16,4,192]{2,1,0:T(4,128)(2,1)} %x_hbm.1, bf16[16,4,192]{2,1,0:T(4,128)(2,1)} %s_hbm.1, bf16[16,4,192]{2,1,0:T(4,128)(2,1)} %c_hbm.1, bf16[4,8]{1,0:T(4,128)(2,1)} %w1_hbm.1, ...), custom_call_target="tpu_custom_call" | custom-call | tf_op jit(solution)/shard_map/pack/pallas_call | solution.py:502
  1.8 5.1 %collective-permute-start = (bf16[208,128]{1,0:T(8,128)(2,1)S(1)}, bf16[208,128]{1,0:T(8,128)(2,1)S(1)}, u32[]{:S(2)}, u32[]{:S(2)}) collective-permute-start(bf16[208,128]{1,0:T(8,128)(2,1)S(1)} %get-tuple-element.42.own_ref), channel_id=1, source_target_pairs={{0,12},{1,13},{2,14},{3,15},{4,8},{5,9},{6,10},{7,11},{8,4},{9,5},... | collective-permute-start | bytes 159752 | tf_op jit(solution)/shard_map/ppermute | solution.py:635
  6.9 0.0 collective-permute-start.1
  6.9 0.6 %collective-permute-start.2 = (bf16[208,128]{1,0:T(8,128)(2,1)S(1)}, bf16[208,128]{1,0:T(8,128)(2,1)S(1)}, u32[]{:S(2)}, u32[]{:S(2)}) collective-permute-start(bf16[208,128]{1,0:T(8,128)(2,1)S(1)} %get-tuple-element.42.own_ref), channel_id=1, source_target_pairs={{0,4},{1,5},{2,6},{3,7},{4,0},{5,1},{6,2},{7,3},{8,12},{9,13},{10,... | collective-permute-start | bytes 159752 | tf_op jit(solution)/shard_map/ppermute | solution.py:635
  7.5 1.7 %collective-permute-start.4 = (bf16[208,128]{1,0:T(8,128)(2,1)S(1)}, bf16[208,128]{1,0:T(8,128)(2,1)S(1)}, u32[]{:S(2)}, u32[]{:S(2)}) collective-permute-start(bf16[208,128]{1,0:T(8,128)(2,1)S(1)} %get-tuple-element.42.own_ref), channel_id=1, source_target_pairs={{0,2},{1,3},{2,0},{3,1},{4,6},{5,7},{6,4},{7,5},{8,10},{9,11},{10,... | collective-permute-start | bytes 159752 | tf_op jit(solution)/shard_map/ppermute | solution.py:635
  9.2 0.5 %prepare.1 = (bf16[112,128]{1,0:T(8,128)(2,1)S(1)}, bf16[96,128]{1,0:T(8,128)(2,1)S(1)}, bf16[384,192]{1,0:T(8,128)(2,1)S(1)}, bf16[256,128]{1,0:T(8,128)(2,1)S(...) custom-call(bf16[208,128]{1,0:T(8,128)(2,1)S(1)} %get-tuple-element., ...), custom_call_target="tpu_custom_call" | custom-call | bytes 2097152 | tf_op jit(solution)/shard_map/prepare/pallas_call | solution.py:522
  9.7 0.0 collective-permute-done
  9.8 2.2 %collective-permute-done.1 = bf16[208,128]{1,0:T(8,128)(2,1)S(1)} collective-permute-done((bf16[208,128]{1,0:T(8,128)(2,1)S(1)}, bf16[208,128]{1,0:T(8,128)(2,1)S(1)}, u32[]{:S(2)}, u32[]{:S(2)}) %collective-permute-start.1) | collective-permute-done | bytes 53280 | tf_op jit(solution)/shard_map/ppermute | solution.py:635
  12.0 0.0 collective-permute-done.2
  12.0 0.1 concatenate.19
  12.1 1.6 %collective-permute-start.3 = (bf16[304,128]{1,0:T(8,128)(2,1)S(1)}, bf16[304,128]{1,0:T(8,128)(2,1)S(1)}, u32[]{:S(2)}, u32[]{:S(2)}) collective-permute-start(bf16[304,128]{1,0:T(8,128)(2,1)S(1)} %concatenate.19), channel_id=1, source_target_pairs={{0,2},{1,3},{2,0},{3,1},{4,6},{5,7},{6,4},{7,5},{8,10},{9,11},{10,... | collective-permute-start | bytes 233480 | tf_op jit(solution)/shard_map/ppermute | solution.py:635
  13.7 0.0 collective-permute-done.4
  13.7 0.1 collective-permute-start.5
  13.8 0.6 %collective-permute-start.7 = (bf16[288,128]{1,0:T(8,128)(2,1)S(1)}, bf16[288,128]{1,0:T(8,128)(2,1)S(1)}, u32[]{:S(2)}, u32[]{:S(2)}) collective-permute-start(bf16[288,128]{1,0:T(8,128)(2,1)S(1)} %pad_maximum_fusion.2), channel_id=1, source_target_pairs={{0,2},{1,3},{2,0},{3,1},{4,6},{5,7},{6,4},{7,5},{8,10},{9,11},{10,... | collective-permute-start | bytes 221192 | tf_op jit(solution)/shard_map/ppermute | solution.py:635
  14.4 0.8 %collective-permute-done.5.x1 = bf16[560,128]{1,0:T(8,128)(2,1)S(1)} collective-permute-done((bf16[560,128]{1,0:T(8,128)(2,1)S(1)}, bf16[560,128]{1,0:T(8,128)(2,1)S(1)}, u32[]{:S(2)}, u32[]{:S(2)}) %collective-permute-start.5) | collective-permute-done | bytes 143392 | tf_op jit(solution)/shard_map/ppermute | solution.py:635
  15.2 0.7 %near.1 = (bf16[256,384]{1,0:T(8,128)(2,1)S(1)}, bf16[256,512]{1,0:T(8,128)(2,1)S(1)}, f32[256,384]{1,0:T(8,128)S(1)}, bf16[64,192]{1,0:T(8,128)(2,1)S(1)}, bf16[16,128]{1,0:T(8,128)(2,1)S(1)}) custom-call(bf16[560,128]{1,0:T(8,128)(2,1)S(1)} %slice_dynamic-update-slice_fusion.x0, bf16[560,128]{1,0:T(8,128)(2,1)S(1)} %collective-permute-done.5.x1, ...), custom_call_target="tpu_custom_call" | custom-call | tf_op jit(solution)/shard_map/near/pallas_call | solution.py:564
  15.9 0.7 %collective-permute-done.3.x2 = bf16[304,128]{1,0:T(8,128)(2,1)S(1)} collective-permute-done((bf16[304,128]{1,0:T(8,128)(2,1)S(1)}, bf16[304,128]{1,0:T(8,128)(2,1)S(1)}, u32[]{:S(2)}, u32[]{:S(2)}) %collective-permute-start.3) | collective-permute-done | bytes 77856 | tf_op jit(solution)/shard_map/ppermute | solution.py:635
  16.6 0.0 collective-permute-start.6
  16.6 0.5 %collective-permute-start.8 = (bf16[480,128]{1,0:T(8,128)(2,1)S(1)}, bf16[480,128]{1,0:T(8,128)(2,1)S(1)}, u32[]{:S(2)}, u32[]{:S(2)}) collective-permute-start(bf16[480,128]{1,0:T(8,128)(2,1)S(1)} %slice_dynamic-update-slice_fusion.4.d0), channel_id=1, source_target_pairs={{0,1},{1,0},{2,3},{3,2},{4,5},{5,4},{6,7},{7,6},{8,9},{9,8},{10,11... | collective-permute-start | bytes 368648 | tf_op jit(solution)/shard_map/ppermute | solution.py:635
  17.1 0.8 %collective-permute-done.6.x3 = bf16[320,128]{1,0:T(8,128)(2,1)S(1)} collective-permute-done((bf16[320,128]{1,0:T(8,128)(2,1)S(1)}, bf16[320,128]{1,0:T(8,128)(2,1)S(1)}, u32[]{:S(2)}, u32[]{:S(2)}) %collective-permute-start.6) | collective-permute-done | bytes 81952 | tf_op jit(solution)/shard_map/ppermute | solution.py:635
  17.8 0.9 %mix.1 = (bf16[1024,192]{1,0:T(8,128)(2,1)S(1)}, bf16[512,64]{1,0:T(8,128)(2,1)S(1)}, bf16[64,192]{1,0:T(8,128)(2,1)S(1)}, bf16[256,384]{1,0:T(8,128)(2,1)S(1)}, bf16[16,128]{1,0:T(8,128)(2,1)S(1)}) custom-call(bf16[304,128]{1,0:T(8,128)(2,1)S(1)} %collective-permute-done.3.x2, bf16[320,128]{1,0:T(8,128)(2,1)S(1)} %collective-permute-done.6.x3, ...), custom_call_target="tpu_custom_call" | custom-call | tf_op jit(solution)/shard_map/mix/pallas_call | solution.py:581
  18.7 0.0 collective-permute-done.7.d2
  18.7 0.2 collective-permute-start.9
  18.9 1.0 %hidden.1 = (bf16[1024,384]{1,0:T(8,128)(2,1)S(1)}, f32[1024,384]{1,0:T(8,128)S(1)}, bf16[192,1024]{1,0:T(8,128)(2,1)S(1)}, bf16[64,192]{1,0:T(8,128)(2,1)S(1)}) custom-call(bf16[1024,192]{1,0:T(8,128)(2,1)S(1)} %get-tuple-element.59.sp_ref, bf16[192,384]{1,0:T(8,128)(2,1)S(1)} %get-tuple-element.43.w_in_ref, ...), custom_call_target="tpu_custom_call" | custom-call | tf_op jit(solution)/shard_map/hidden/pallas_call | solution.py:602
  19.9 0.0 collective-permute-done.8.d1
  20.0 0.1 collective-permute-done.9.d3
  20.1 2.3 %backward.1 = (bf16[16,4,192]{2,1,0:T(4,128)(2,1)}, f32[4,8]{1,0:T(4,128)}, f32[4,8]{1,0:T(4,128)}, f32[192,384]{1,0:T(8,128)}, f32[192,384]{1,0:T(8,128)}) custom-call(bf16[1024,384]{1,0:T(8,128)(2,1)S(1)} %get-tuple-element.62.hid_ref, f32[1024,384]{1,0:T(8,128)S(1)} %get-tuple-element.63.slope_ref, bf16[192,1024]{1,0:T(8,128)(2,1)S(1)} %get-tuple-element.64.spt_ref, ...), custom_call_target="tpu_custom_call" | custom-call | tf_op jit(solution)/shard_map/backward/pallas_call | solution.py:616
  (17 shorter events, 0.1 us)
Async XLA Ops:
  1.8 8.0 %collective-permute-start = (bf16[208,128]{1,0:T(8,128)(2,1)S(1)}, bf16[208,128]{1,0:T(8,128)(2,1)S(1)}, u32[]{:S(2)}, u32[]{:S(2)}) collective-permute-start(bf16[208,128]{1,0:T(8,128)(2,1)S(1)} %get-tuple-element.42.own_ref), channel_id=1, source_target_pairs={{0,12},{1,13},{2,14},{3,15},{4,8},{5,9},{6,10},{7,11},{8,4},{9,5},... | collective-permute-start | bytes 159752 | tf_op jit(solution)/shard_map/ppermute | solution.py:635
  6.9 5.0 %collective-permute-start.1 = (bf16[208,128]{1,0:T(8,128)(2,1)S(1)}, bf16[208,128]{1,0:T(8,128)(2,1)S(1)}, u32[]{:S(2)}, u32[]{:S(2)}) collective-permute-start(bf16[208,128]{1,0:T(8,128)(2,1)S(1)} %get-tuple-element.42.own_ref), channel_id=1, source_target_pairs={{0,8},{1,9},{2,10},{3,11},{4,12},{5,13},{6,14},{7,15},{8,0},{9,1},... | collective-permute-start | bytes 159752 | tf_op jit(solution)/shard_map/ppermute | solution.py:635
  6.9 5.1 %collective-permute-start.2 = (bf16[208,128]{1,0:T(8,128)(2,1)S(1)}, bf16[208,128]{1,0:T(8,128)(2,1)S(1)}, u32[]{:S(2)}, u32[]{:S(2)}) collective-permute-start(bf16[208,128]{1,0:T(8,128)(2,1)S(1)} %get-tuple-element.42.own_ref), channel_id=1, source_target_pairs={{0,4},{1,5},{2,6},{3,7},{4,0},{5,1},{6,2},{7,3},{8,12},{9,13},{10,... | collective-permute-start | bytes 159752 | tf_op jit(solution)/shard_map/ppermute | solution.py:635
  7.5 6.2 %collective-permute-start.4 = (bf16[208,128]{1,0:T(8,128)(2,1)S(1)}, bf16[208,128]{1,0:T(8,128)(2,1)S(1)}, u32[]{:S(2)}, u32[]{:S(2)}) collective-permute-start(bf16[208,128]{1,0:T(8,128)(2,1)S(1)} %get-tuple-element.42.own_ref), channel_id=1, source_target_pairs={{0,2},{1,3},{2,0},{3,1},{4,6},{5,7},{6,4},{7,5},{8,10},{9,11},{10,... | collective-permute-start | bytes 159752 | tf_op jit(solution)/shard_map/ppermute | solution.py:635
  12.1 4.4 %collective-permute-start.3 = (bf16[304,128]{1,0:T(8,128)(2,1)S(1)}, bf16[304,128]{1,0:T(8,128)(2,1)S(1)}, u32[]{:S(2)}, u32[]{:S(2)}) collective-permute-start(bf16[304,128]{1,0:T(8,128)(2,1)S(1)} %concatenate.19), channel_id=1, source_target_pairs={{0,2},{1,3},{2,0},{3,1},{4,6},{5,7},{6,4},{7,5},{8,10},{9,11},{10,... | collective-permute-start | bytes 233480 | tf_op jit(solution)/shard_map/ppermute | solution.py:635
  13.7 1.4 %collective-permute-start.5 = (bf16[560,128]{1,0:T(8,128)(2,1)S(1)}, bf16[560,128]{1,0:T(8,128)(2,1)S(1)}, u32[]{:S(2)}, u32[]{:S(2)}) collective-permute-start(bf16[560,128]{1,0:T(8,128)(2,1)S(1)} %slice_dynamic-update-slice_fusion.x0), channel_id=1, source_target_pairs={{0,1},{1,0},{2,3},{3,2},{4,5},{5,4},{6,7},{7,6},{8,9},{9,8},{10,11... | collective-permute-start | bytes 430088 | tf_op jit(solution)/shard_map/ppermute | solution.py:635
  13.8 4.9 %collective-permute-start.7 = (bf16[288,128]{1,0:T(8,128)(2,1)S(1)}, bf16[288,128]{1,0:T(8,128)(2,1)S(1)}, u32[]{:S(2)}, u32[]{:S(2)}) collective-permute-start(bf16[288,128]{1,0:T(8,128)(2,1)S(1)} %pad_maximum_fusion.2), channel_id=1, source_target_pairs={{0,2},{1,3},{2,0},{3,1},{4,6},{5,7},{6,4},{7,5},{8,10},{9,11},{10,... | collective-permute-start | bytes 221192 | tf_op jit(solution)/shard_map/ppermute | solution.py:635
  16.6 1.3 %collective-permute-start.6 = (bf16[320,128]{1,0:T(8,128)(2,1)S(1)}, bf16[320,128]{1,0:T(8,128)(2,1)S(1)}, u32[]{:S(2)}, u32[]{:S(2)}) collective-permute-start(bf16[320,128]{1,0:T(8,128)(2,1)S(1)} %pad_maximum_fusion), channel_id=1, source_target_pairs={{0,1},{1,0},{2,3},{3,2},{4,5},{5,4},{6,7},{7,6},{8,9},{9,8},{10,11... | collective-permute-start | bytes 245768 | tf_op jit(solution)/shard_map/ppermute | solution.py:635
  16.6 3.4 %collective-permute-start.8 = (bf16[480,128]{1,0:T(8,128)(2,1)S(1)}, bf16[480,128]{1,0:T(8,128)(2,1)S(1)}, u32[]{:S(2)}, u32[]{:S(2)}) collective-permute-start(bf16[480,128]{1,0:T(8,128)(2,1)S(1)} %slice_dynamic-update-slice_fusion.4.d0), channel_id=1, source_target_pairs={{0,1},{1,0},{2,3},{3,2},{4,5},{5,4},{6,7},{7,6},{8,9},{9,8},{10,11... | collective-permute-start | bytes 368648 | tf_op jit(solution)/shard_map/ppermute | solution.py:635
  18.7 1.3 %collective-permute-start.9 = (bf16[304,128]{1,0:T(8,128)(2,1)S(1)}, bf16[304,128]{1,0:T(8,128)(2,1)S(1)}, u32[]{:S(2)}, u32[]{:S(2)}) collective-permute-start(bf16[304,128]{1,0:T(8,128)(2,1)S(1)} %pad_maximum_fusion.1), channel_id=1, source_target_pairs={{0,1},{1,0},{2,3},{3,2},{4,5},{5,4},{6,7},{7,6},{8,9},{9,8},{10,11... | collective-permute-start | bytes 233480 | tf_op jit(solution)/shard_map/ppermute | solution.py:635

commit v7 on v6

--- a/solution.py
+++ b/solution.py
@@ -433,6 +433,17 @@
     at = Rows(own, bins, rows)
     order = sum(halves_of(devices), [])
     dm_low, dm_high = unpacked(*tiles_of(refs, (3 * own,) * 4, devices, own, order))
+    sp_own = sp_own_ref[...]
+    hidden = jnp.concatenate([hid_ref[:own, :], hid_ref[rows : rows + own, :]], 0)
+    mask = (sp_own.astype(f32) + mul(hidden, w_out_ref[...], NT)).astype(bf16).astype(f32)
+    spec = s_ref[...].astype(f32).reshape(2 * own, channels)
+    spec_re, spec_im = spec[:, :half_c], spec[:, half_c:]
+    mask_re, mask_im = mask[:, :half_c], mask[:, half_c:]
+    enhanced = jnp.concatenate(
+        [spec_re * mask_re - spec_im * mask_im, spec_re * mask_im + spec_im * mask_re], 1
+    )
+    enh_ref[...] = enhanced.reshape(frames, bins, channels).astype(bf16)
+
     parts = 2 * rows // 4
     dm = [half[k : k + parts] for half in (dm_low, dm_high) for k in range(0, rows, parts)]
     dpre, dsp = [], []
@@ -444,17 +455,6 @@
     dsp = dsp[:rows], dsp[rows:]
     gwi_ref[...] = mul(spt_ref[...], dpre)
     gwo_ref[...] = mul(jnp.concatenate([dm_low, dm_high], 0), hid_ref[...], TN)
-
-    sp_own = sp_own_ref[...]
-    hidden = jnp.concatenate([hid_ref[:own, :], hid_ref[rows : rows + own, :]], 0)
-    mask = (sp_own.astype(f32) + mul(hidden, w_out_ref[...], NT)).astype(bf16).astype(f32)
-    spec = s_ref[...].astype(f32).reshape(2 * own, channels)
-    spec_re, spec_im = spec[:, :half_c], spec[:, half_c:]
-    mask_re, mask_im = mask[:, :half_c], mask[:, half_c:]
-    enhanced = jnp.concatenate(
-        [spec_re * mask_re - spec_im * mask_im, spec_re * mask_im + spec_im * mask_re], 1
-    )
-    enh_ref[...] = enhanced.reshape(frames, bins, channels).astype(bf16)
 
     dsp_low, dsp_high = dsp
     dfirst_low = mul(back_ref[...], dsp_low, TN).astype(bf16)

time: 22.5 us -> 22.4 us (level)
  no operation moved by 1% of the time
where the time goes in v7:
time: 22.4 us; the launch traced here: 22.3 us
  starting transfers between devices  10.3 us (46%)
  Pallas kernels  6.4 us (29%)
  waiting for transfers between devices  4.5 us (20%)
  between operations  0.79 us (4%)
    ppermute x10, starting transfers between devices, exchanged(): return lax.ppermute(value, 'freq', pairs)  10.3 us
    ppermute x10, waiting for transfers between devices, exchanged(): return lax.ppermute(value, 'freq', pairs)  4.5 us
    pallas_call x1, Pallas kernels, whole_rows(): pl.pallas_call(backward_kernel, out_shape=(shaped((frames, bins, channels...  2.21 us
    pallas_call x1, Pallas kernels, whole_rows(): pl.pallas_call(functools.partial(pack_kernel, scale=scale), out_shape=(pl...  1.13 us
    pallas_call x1, Pallas kernels, whole_rows(): pl.pallas_call(hidden_kernel, out_shape=(pltpu.VMEM((2 * rows, hid), bf16...  0.99 us
    pallas_call x1, Pallas kernels, whole_rows(): pl.pallas_call(mix_kernel, out_shape=tuple((pltpu.VMEM(shape, bf16) for s...  0.87 us
    pallas_call x1, Pallas kernels, whole_rows(): pl.pallas_call(near_kernel, out_shape=(pltpu.VMEM((rows // 2, 2 * channel...  0.68 us
    pallas_call x1, Pallas kernels, whole_rows(): pl.pallas_call(functools.partial(prepare_kernel, bins=bins), out_shape=tu...  0.52 us
  transfers between devices with their start and end apart: 10, of which 5 were waited for; matrix products, arithmetic and copies ran while one was open for 1% of the time, Pallas kernels for 14%

profile of v7, /device:TPU:0, one launch (start us, length us, event | category | flops | bytes accessed | tf_op | source)
XLA Modules:
  0.0 22.3 jit_solution(6415346995934365503)
XLA Ops:
  0.6 1.1 %pack.1 = (bf16[208,128]{1,0:T(8,128)(2,1)S(1)}, bf16[16,4,192]{2,1,0:T(4,128)(2,1)S(1)}, bf16[192,384]{1,0:T(8,128)(2,1)S(1)}, bf16[192,384]{1,0:T(8,128)(2,1)S(1)}) custom-call(bf16[16,4,192]{2,1,0:T(4,128)(2,1)} %x_hbm.1, bf16[16,4,192]{2,1,0:T(4,128)(2,1)} %s_hbm.1, bf16[16,4,192]{2,1,0:T(4,128)(2,1)} %c_hbm.1, bf16[4,8]{1,0:T(4,128)(2,1)} %w1_hbm.1, ...), custom_call_target="tpu_custom_call" | custom-call | tf_op jit(solution)/shard_map/pack/pallas_call | solution.py:502
  1.8 5.1 %collective-permute-start = (bf16[208,128]{1,0:T(8,128)(2,1)S(1)}, bf16[208,128]{1,0:T(8,128)(2,1)S(1)}, u32[]{:S(2)}, u32[]{:S(2)}) collective-permute-start(bf16[208,128]{1,0:T(8,128)(2,1)S(1)} %get-tuple-element.42.own_ref), channel_id=1, source_target_pairs={{0,12},{1,13},{2,14},{3,15},{4,8},{5,9},{6,10},{7,11},{8,4},{9,5},... | collective-permute-start | bytes 159752 | tf_op jit(solution)/shard_map/ppermute | solution.py:635
  6.9 0.0 collective-permute-start.1
  6.9 0.6 %collective-permute-start.2 = (bf16[208,128]{1,0:T(8,128)(2,1)S(1)}, bf16[208,128]{1,0:T(8,128)(2,1)S(1)}, u32[]{:S(2)}, u32[]{:S(2)}) collective-permute-start(bf16[208,128]{1,0:T(8,128)(2,1)S(1)} %get-tuple-element.42.own_ref), channel_id=1, source_target_pairs={{0,4},{1,5},{2,6},{3,7},{4,0},{5,1},{6,2},{7,3},{8,12},{9,13},{10,... | collective-permute-start | bytes 159752 | tf_op jit(solution)/shard_map/ppermute | solution.py:635
  7.5 1.7 %collective-permute-start.4 = (bf16[208,128]{1,0:T(8,128)(2,1)S(1)}, bf16[208,128]{1,0:T(8,128)(2,1)S(1)}, u32[]{:S(2)}, u32[]{:S(2)}) collective-permute-start(bf16[208,128]{1,0:T(8,128)(2,1)S(1)} %get-tuple-element.42.own_ref), channel_id=1, source_target_pairs={{0,2},{1,3},{2,0},{3,1},{4,6},{5,7},{6,4},{7,5},{8,10},{9,11},{10,... | collective-permute-start | bytes 159752 | tf_op jit(solution)/shard_map/ppermute | solution.py:635
  9.2 0.5 %prepare.1 = (bf16[112,128]{1,0:T(8,128)(2,1)S(1)}, bf16[96,128]{1,0:T(8,128)(2,1)S(1)}, bf16[384,192]{1,0:T(8,128)(2,1)S(1)}, bf16[256,128]{1,0:T(8,128)(2,1)S(...) custom-call(bf16[208,128]{1,0:T(8,128)(2,1)S(1)} %get-tuple-element., ...), custom_call_target="tpu_custom_call" | custom-call | bytes 2097152 | tf_op jit(solution)/shard_map/prepare/pallas_call | solution.py:522
  9.7 0.0 collective-permute-done
  9.8 2.2 %collective-permute-done.1 = bf16[208,128]{1,0:T(8,128)(2,1)S(1)} collective-permute-done((bf16[208,128]{1,0:T(8,128)(2,1)S(1)}, bf16[208,128]{1,0:T(8,128)(2,1)S(1)}, u32[]{:S(2)}, u32[]{:S(2)}) %collective-permute-start.1) | collective-permute-done | bytes 53280 | tf_op jit(solution)/shard_map/ppermute | solution.py:635
  12.0 0.0 collective-permute-done.2
  12.0 0.1 concatenate.19
  12.1 1.6 %collective-permute-start.3 = (bf16[304,128]{1,0:T(8,128)(2,1)S(1)}, bf16[304,128]{1,0:T(8,128)(2,1)S(1)}, u32[]{:S(2)}, u32[]{:S(2)}) collective-permute-start(bf16[304,128]{1,0:T(8,128)(2,1)S(1)} %concatenate.19), channel_id=1, source_target_pairs={{0,2},{1,3},{2,0},{3,1},{4,6},{5,7},{6,4},{7,5},{8,10},{9,11},{10,... | collective-permute-start | bytes 233480 | tf_op jit(solution)/shard_map/ppermute | solution.py:635
  13.7 0.0 collective-permute-done.4
  13.7 0.1 collective-permute-start.5
  13.8 0.6 %collective-permute-start.7 = (bf16[288,128]{1,0:T(8,128)(2,1)S(1)}, bf16[288,128]{1,0:T(8,128)(2,1)S(1)}, u32[]{:S(2)}, u32[]{:S(2)}) collective-permute-start(bf16[288,128]{1,0:T(8,128)(2,1)S(1)} %pad_maximum_fusion.2), channel_id=1, source_target_pairs={{0,2},{1,3},{2,0},{3,1},{4,6},{5,7},{6,4},{7,5},{8,10},{9,11},{10,... | collective-permute-start | bytes 221192 | tf_op jit(solution)/shard_map/ppermute | solution.py:635
  14.4 0.8 %collective-permute-done.5.x1 = bf16[560,128]{1,0:T(8,128)(2,1)S(1)} collective-permute-done((bf16[560,128]{1,0:T(8,128)(2,1)S(1)}, bf16[560,128]{1,0:T(8,128)(2,1)S(1)}, u32[]{:S(2)}, u32[]{:S(2)}) %collective-permute-start.5) | collective-permute-done | bytes 143392 | tf_op jit(solution)/shard_map/ppermute | solution.py:635
  15.2 0.7 %near.1 = (bf16[256,384]{1,0:T(8,128)(2,1)S(1)}, bf16[256,512]{1,0:T(8,128)(2,1)S(1)}, f32[256,384]{1,0:T(8,128)S(1)}, bf16[64,192]{1,0:T(8,128)(2,1)S(1)}, bf16[16,128]{1,0:T(8,128)(2,1)S(1)}) custom-call(bf16[560,128]{1,0:T(8,128)(2,1)S(1)} %slice_dynamic-update-slice_fusion.x0, bf16[560,128]{1,0:T(8,128)(2,1)S(1)} %collective-permute-done.5.x1, ...), custom_call_target="tpu_custom_call" | custom-call | tf_op jit(solution)/shard_map/near/pallas_call | solution.py:564
  15.9 0.7 %collective-permute-done.3.x2 = bf16[304,128]{1,0:T(8,128)(2,1)S(1)} collective-permute-done((bf16[304,128]{1,0:T(8,128)(2,1)S(1)}, bf16[304,128]{1,0:T(8,128)(2,1)S(1)}, u32[]{:S(2)}, u32[]{:S(2)}) %collective-permute-start.3) | collective-permute-done | bytes 77856 | tf_op jit(solution)/shard_map/ppermute | solution.py:635
  16.6 0.0 collective-permute-start.6
  16.6 0.5 %collective-permute-start.8 = (bf16[480,128]{1,0:T(8,128)(2,1)S(1)}, bf16[480,128]{1,0:T(8,128)(2,1)S(1)}, u32[]{:S(2)}, u32[]{:S(2)}) collective-permute-start(bf16[480,128]{1,0:T(8,128)(2,1)S(1)} %slice_dynamic-update-slice_fusion.4.d0), channel_id=1, source_target_pairs={{0,1},{1,0},{2,3},{3,2},{4,5},{5,4},{6,7},{7,6},{8,9},{9,8},{10,11... | collective-permute-start | bytes 368648 | tf_op jit(solution)/shard_map/ppermute | solution.py:635
  17.1 0.8 %collective-permute-done.6.x3 = bf16[320,128]{1,0:T(8,128)(2,1)S(1)} collective-permute-done((bf16[320,128]{1,0:T(8,128)(2,1)S(1)}, bf16[320,128]{1,0:T(8,128)(2,1)S(1)}, u32[]{:S(2)}, u32[]{:S(2)}) %collective-permute-start.6) | collective-permute-done | bytes 81952 | tf_op jit(solution)/shard_map/ppermute | solution.py:635
  17.8 0.9 %mix.1 = (bf16[1024,192]{1,0:T(8,128)(2,1)S(1)}, bf16[512,64]{1,0:T(8,128)(2,1)S(1)}, bf16[64,192]{1,0:T(8,128)(2,1)S(1)}, bf16[256,384]{1,0:T(8,128)(2,1)S(1)}, bf16[16,128]{1,0:T(8,128)(2,1)S(1)}) custom-call(bf16[304,128]{1,0:T(8,128)(2,1)S(1)} %collective-permute-done.3.x2, bf16[320,128]{1,0:T(8,128)(2,1)S(1)} %collective-permute-done.6.x3, ...), custom_call_target="tpu_custom_call" | custom-call | tf_op jit(solution)/shard_map/mix/pallas_call | solution.py:581
  18.7 0.0 collective-permute-done.7.d2
  18.7 0.2 collective-permute-start.9
  18.9 1.0 %hidden.1 = (bf16[1024,384]{1,0:T(8,128)(2,1)S(1)}, f32[1024,384]{1,0:T(8,128)S(1)}, bf16[192,1024]{1,0:T(8,128)(2,1)S(1)}, bf16[64,192]{1,0:T(8,128)(2,1)S(1)}) custom-call(bf16[1024,192]{1,0:T(8,128)(2,1)S(1)} %get-tuple-element.59.sp_ref, bf16[192,384]{1,0:T(8,128)(2,1)S(1)} %get-tuple-element.43.w_in_ref, ...), custom_call_target="tpu_custom_call" | custom-call | tf_op jit(solution)/shard_map/hidden/pallas_call | solution.py:602
  19.9 0.0 collective-permute-done.8.d1
  20.0 0.1 collective-permute-done.9.d3
  20.1 2.2 %backward.1 = (bf16[16,4,192]{2,1,0:T(4,128)(2,1)}, f32[4,8]{1,0:T(4,128)}, f32[4,8]{1,0:T(4,128)}, f32[192,384]{1,0:T(8,128)}, f32[192,384]{1,0:T(8,128)}) custom-call(bf16[1024,384]{1,0:T(8,128)(2,1)S(1)} %get-tuple-element.62.hid_ref, f32[1024,384]{1,0:T(8,128)S(1)} %get-tuple-element.63.slope_ref, bf16[192,1024]{1,0:T(8,128)(2,1)S(1)} %get-tuple-element.64.spt_ref, ...), custom_call_target="tpu_custom_call" | custom-call | tf_op jit(solution)/shard_map/backward/pallas_call | solution.py:616
  (17 shorter events, 0.1 us)
Async XLA Ops:
  1.8 8.0 %collective-permute-start = (bf16[208,128]{1,0:T(8,128)(2,1)S(1)}, bf16[208,128]{1,0:T(8,128)(2,1)S(1)}, u32[]{:S(2)}, u32[]{:S(2)}) collective-permute-start(bf16[208,128]{1,0:T(8,128)(2,1)S(1)} %get-tuple-element.42.own_ref), channel_id=1, source_target_pairs={{0,12},{1,13},{2,14},{3,15},{4,8},{5,9},{6,10},{7,11},{8,4},{9,5},... | collective-permute-start | bytes 159752 | tf_op jit(solution)/shard_map/ppermute | solution.py:635
  6.9 5.0 %collective-permute-start.1 = (bf16[208,128]{1,0:T(8,128)(2,1)S(1)}, bf16[208,128]{1,0:T(8,128)(2,1)S(1)}, u32[]{:S(2)}, u32[]{:S(2)}) collective-permute-start(bf16[208,128]{1,0:T(8,128)(2,1)S(1)} %get-tuple-element.42.own_ref), channel_id=1, source_target_pairs={{0,8},{1,9},{2,10},{3,11},{4,12},{5,13},{6,14},{7,15},{8,0},{9,1},... | collective-permute-start | bytes 159752 | tf_op jit(solution)/shard_map/ppermute | solution.py:635
  6.9 5.1 %collective-permute-start.2 = (bf16[208,128]{1,0:T(8,128)(2,1)S(1)}, bf16[208,128]{1,0:T(8,128)(2,1)S(1)}, u32[]{:S(2)}, u32[]{:S(2)}) collective-permute-start(bf16[208,128]{1,0:T(8,128)(2,1)S(1)} %get-tuple-element.42.own_ref), channel_id=1, source_target_pairs={{0,4},{1,5},{2,6},{3,7},{4,0},{5,1},{6,2},{7,3},{8,12},{9,13},{10,... | collective-permute-start | bytes 159752 | tf_op jit(solution)/shard_map/ppermute | solution.py:635
  7.5 6.2 %collective-permute-start.4 = (bf16[208,128]{1,0:T(8,128)(2,1)S(1)}, bf16[208,128]{1,0:T(8,128)(2,1)S(1)}, u32[]{:S(2)}, u32[]{:S(2)}) collective-permute-start(bf16[208,128]{1,0:T(8,128)(2,1)S(1)} %get-tuple-element.42.own_ref), channel_id=1, source_target_pairs={{0,2},{1,3},{2,0},{3,1},{4,6},{5,7},{6,4},{7,5},{8,10},{9,11},{10,... | collective-permute-start | bytes 159752 | tf_op jit(solution)/shard_map/ppermute | solution.py:635
  12.1 4.4 %collective-permute-start.3 = (bf16[304,128]{1,0:T(8,128)(2,1)S(1)}, bf16[304,128]{1,0:T(8,128)(2,1)S(1)}, u32[]{:S(2)}, u32[]{:S(2)}) collective-permute-start(bf16[304,128]{1,0:T(8,128)(2,1)S(1)} %concatenate.19), channel_id=1, source_target_pairs={{0,2},{1,3},{2,0},{3,1},{4,6},{5,7},{6,4},{7,5},{8,10},{9,11},{10,... | collective-permute-start | bytes 233480 | tf_op jit(solution)/shard_map/ppermute | solution.py:635
  13.7 1.4 %collective-permute-start.5 = (bf16[560,128]{1,0:T(8,128)(2,1)S(1)}, bf16[560,128]{1,0:T(8,128)(2,1)S(1)}, u32[]{:S(2)}, u32[]{:S(2)}) collective-permute-start(bf16[560,128]{1,0:T(8,128)(2,1)S(1)} %slice_dynamic-update-slice_fusion.x0), channel_id=1, source_target_pairs={{0,1},{1,0},{2,3},{3,2},{4,5},{5,4},{6,7},{7,6},{8,9},{9,8},{10,11... | collective-permute-start | bytes 430088 | tf_op jit(solution)/shard_map/ppermute | solution.py:635
  13.8 4.9 %collective-permute-start.7 = (bf16[288,128]{1,0:T(8,128)(2,1)S(1)}, bf16[288,128]{1,0:T(8,128)(2,1)S(1)}, u32[]{:S(2)}, u32[]{:S(2)}) collective-permute-start(bf16[288,128]{1,0:T(8,128)(2,1)S(1)} %pad_maximum_fusion.2), channel_id=1, source_target_pairs={{0,2},{1,3},{2,0},{3,1},{4,6},{5,7},{6,4},{7,5},{8,10},{9,11},{10,... | collective-permute-start | bytes 221192 | tf_op jit(solution)/shard_map/ppermute | solution.py:635
  16.6 1.3 %collective-permute-start.6 = (bf16[320,128]{1,0:T(8,128)(2,1)S(1)}, bf16[320,128]{1,0:T(8,128)(2,1)S(1)}, u32[]{:S(2)}, u32[]{:S(2)}) collective-permute-start(bf16[320,128]{1,0:T(8,128)(2,1)S(1)} %pad_maximum_fusion), channel_id=1, source_target_pairs={{0,1},{1,0},{2,3},{3,2},{4,5},{5,4},{6,7},{7,6},{8,9},{9,8},{10,11... | collective-permute-start | bytes 245768 | tf_op jit(solution)/shard_map/ppermute | solution.py:635
  16.6 3.4 %collective-permute-start.8 = (bf16[480,128]{1,0:T(8,128)(2,1)S(1)}, bf16[480,128]{1,0:T(8,128)(2,1)S(1)}, u32[]{:S(2)}, u32[]{:S(2)}) collective-permute-start(bf16[480,128]{1,0:T(8,128)(2,1)S(1)} %slice_dynamic-update-slice_fusion.4.d0), channel_id=1, source_target_pairs={{0,1},{1,0},{2,3},{3,2},{4,5},{5,4},{6,7},{7,6},{8,9},{9,8},{10,11... | collective-permute-start | bytes 368648 | tf_op jit(solution)/shard_map/ppermute | solution.py:635
  18.7 1.3 %collective-permute-start.9 = (bf16[304,128]{1,0:T(8,128)(2,1)S(1)}, bf16[304,128]{1,0:T(8,128)(2,1)S(1)}, u32[]{:S(2)}, u32[]{:S(2)}) collective-permute-start(bf16[304,128]{1,0:T(8,128)(2,1)S(1)} %pad_maximum_fusion.1), channel_id=1, source_target_pairs={{0,1},{1,0},{2,3},{3,2},{4,5},{5,4},{6,7},{7,6},{8,9},{9,8},{10,11... | collective-permute-start | bytes 233480 | tf_op jit(solution)/shard_map/ppermute | solution.py:635
